TPU v7x, 32 devices: a whole 2x2x4 slice. The times are simulated.
32 devices in a mesh: dp: 2 (over x), expert: 16 (over z, y, core).
Axes of the slice: x: 2, y: 2, z: 4, core: 2. Of those that a mesh axis runs over, the one named last changes fastest.
Arguments:
- tokens: bfloat16 [512, 2048], P(('dp', 'expert')), may hold values from -6 to 6
- routes: int32 [512, 8], P(('dp', 'expert')), may hold values from 0 to 15, all different within a row; in each aligned block of 16 rows (0 to 15, 16 to 31, ...) at most 16 rows name the same one
- gates: float32 [512, 8], P(('dp', 'expert')), may hold values from 0.02 to 0.5
- cotangent: bfloat16 [512, 2048], P(('dp', 'expert')), may hold values from -6 to 6
- w_gate: bfloat16 [16, 2048, 768], P('expert', 'dp'), may hold values from -0.125 to 0.125
- w_up: bfloat16 [16, 2048, 768], P('expert', 'dp'), may hold values from -0.125 to 0.125
- w_down: bfloat16 [16, 768, 2048], P('expert', None, 'dp'), may hold values from -0.21875 to 0.21875
Outputs:
- layer_out: bfloat16 [512, 2048], P(('dp', 'expert'))
- d_tokens: bfloat16 [512, 2048], P(('dp', 'expert'))
- grad_gate: bfloat16 [16, 2048, 768], P('expert', 'dp')
- grad_up: bfloat16 [16, 2048, 768], P('expert', 'dp')
- grad_down: bfloat16 [16, 768, 2048], P('expert', None, 'dp')
Inputs may be any that keep to these rules, and one draw needn't show every extreme that they name: `routes`: each token names 8 different experts. Among the 16 tokens of one device (aligned blocks of token rows) no expert is named by more than 16 tokens, a bound that some block reaches.
All inputs are finite; a program needn't handle non-finite values.
Results may differ from a plain program's by a relative error of at most 0.019.
Values may be sent and summed in bfloat16 or wider, within the bound.
No kernel may reach another device: no remote copies, remote signals or barrier semaphores. Data moves between devices by JAX's collectives and lax.ppermute only.
A program may use at most 64 MiB of HBM per device.

v0:
```python
import jax
import jax.numpy as jnp
from jax import lax
from jax.sharding import PartitionSpec as P


def local(tokens, routes, gates, cotangent, w_gate, w_up, w_down):
    tok_rows, features = tokens.shape
    fanout = routes.shape[1]
    experts = lax.axis_size("expert")
    groups = lax.axis_size("dp")
    capacity = min(tok_rows, max(2, 2 * tok_rows * fanout // experts))
    assigned = tok_rows * fanout
    expert_ids = routes.reshape(assigned)
    onehot = (expert_ids[:, None] == jnp.arange(experts, dtype=jnp.int32)[None, :]).astype(
        jnp.float32
    )
    assign_iota = jnp.arange(assigned, dtype=jnp.int32)
    earlier = (assign_iota[:, None] > assign_iota[None, :]).astype(jnp.float32)
    prior_count = jnp.dot(earlier, onehot, precision=lax.Precision.HIGHEST)
    slot_index = jnp.sum(prior_count * onehot, axis=1).astype(jnp.int32)
    position = expert_ids * capacity + slot_index
    slot_map = (
        jnp.arange(experts * capacity, dtype=jnp.int32)[:, None] == position[None, :]
    ).astype(jnp.float32)
    token_owner = (
        assign_iota[:, None] // fanout == jnp.arange(tok_rows, dtype=jnp.int32)[None, :]
    ).astype(jnp.float32)
    dispatch = jnp.dot(slot_map, token_owner, precision=lax.Precision.HIGHEST)
    weighted = jnp.dot(
        slot_map, token_owner * gates.reshape(assigned)[:, None], precision=lax.Precision.HIGHEST
    )
    send_input = jnp.dot(
        dispatch.astype(jnp.bfloat16), tokens, preferred_element_type=jnp.float32
    ).astype(jnp.bfloat16)
    send_dout = jnp.dot(
        weighted, cotangent.astype(jnp.float32), precision=lax.Precision.HIGHEST
    ).astype(jnp.bfloat16)
    send_input = send_input.reshape(1, experts, capacity, features)
    send_dout = send_dout.reshape(1, experts, capacity, features)
    moved = (
        lax.all_to_all(send_input, "dp", split_axis=3, concat_axis=0, tiled=True),
        lax.all_to_all(send_dout, "dp", split_axis=3, concat_axis=0, tiled=True),
    )
    moved = (
        lax.all_to_all(moved[0], "expert", split_axis=1, concat_axis=1, tiled=True),
        lax.all_to_all(moved[1], "expert", split_axis=1, concat_axis=1, tiled=True),
    )
    part_width = moved[0].shape[3]
    total_rows = groups * experts * capacity
    input_rows = moved[0].reshape(total_rows, part_width)
    dout_rows = moved[1].reshape(total_rows, part_width)
    gate_local = w_gate[0]
    up_local = w_up[0]
    down_local = w_down[0]
    own_rows = total_rows // groups
    own_start = lax.axis_index("dp") * own_rows
    gate_part = jnp.dot(input_rows, gate_local, preferred_element_type=jnp.float32)
    up_part = jnp.dot(input_rows, up_local, preferred_element_type=jnp.float32)
    gate_all, up_all = (
        lax.psum(gate_part.astype(jnp.bfloat16), "dp").astype(jnp.float32),
        lax.psum(up_part.astype(jnp.bfloat16), "dp").astype(jnp.float32),
    )
    hidden = (jax.nn.silu(gate_all) * up_all).astype(jnp.bfloat16)
    gate_own = lax.dynamic_slice_in_dim(gate_all, own_start, own_rows, 0)
    up_own = lax.dynamic_slice_in_dim(up_all, own_start, own_rows, 0)
    out_slots = jnp.dot(hidden, down_local, preferred_element_type=jnp.float32).astype(jnp.bfloat16)
    grad_down = jnp.einsum(
        "rf,rd->fd", hidden, dout_rows, preferred_element_type=jnp.float32
    ).astype(jnp.bfloat16)
    dhidden_part = jnp.einsum(
        "rd,fd->rf", dout_rows, down_local, preferred_element_type=jnp.float32
    )
    dhidden_own = lax.psum_scatter(
        dhidden_part.astype(jnp.bfloat16), "dp", scatter_dimension=0, tiled=True
    ).astype(jnp.float32)
    sigmoid_gate = jax.nn.sigmoid(gate_own)
    silu_gate = gate_own * sigmoid_gate
    dgate_own = (
        dhidden_own * up_own * sigmoid_gate * (1.0 + gate_own * (1.0 - sigmoid_gate))
    ).astype(jnp.bfloat16)
    dup_own = (dhidden_own * silu_gate).astype(jnp.bfloat16)
    dgate_all, dup_all = (
        lax.all_gather(dgate_own, "dp", axis=0, tiled=True),
        lax.all_gather(dup_own, "dp", axis=0, tiled=True),
    )
    grad_gate = jnp.einsum(
        "rd,rf->df", input_rows, dgate_all, preferred_element_type=jnp.float32
    ).astype(jnp.bfloat16)
    grad_up = jnp.einsum(
        "rd,rf->df", input_rows, dup_all, preferred_element_type=jnp.float32
    ).astype(jnp.bfloat16)
    back_slots = (
        jnp.einsum("rf,df->rd", dgate_all, gate_local, preferred_element_type=jnp.float32)
        + jnp.einsum("rf,df->rd", dup_all, up_local, preferred_element_type=jnp.float32)
    ).astype(jnp.bfloat16)
    out_slots = out_slots.reshape(groups, experts, capacity, part_width)
    back_slots = back_slots.reshape(groups, experts, capacity, part_width)
    returned = (
        lax.all_to_all(out_slots, "expert", split_axis=1, concat_axis=1, tiled=True),
        lax.all_to_all(back_slots, "expert", split_axis=1, concat_axis=1, tiled=True),
    )
    returned = (
        lax.all_to_all(returned[0], "dp", split_axis=0, concat_axis=3, tiled=True),
        lax.all_to_all(returned[1], "dp", split_axis=0, concat_axis=3, tiled=True),
    )
    out_tokens = returned[0].reshape(experts * capacity, features)
    back_tokens = returned[1].reshape(experts * capacity, features)
    layer_out = jnp.dot(
        weighted.T, out_tokens.astype(jnp.float32), precision=lax.Precision.HIGHEST
    ).astype(jnp.bfloat16)
    d_tokens = jnp.dot(
        dispatch.T.astype(jnp.bfloat16), back_tokens, preferred_element_type=jnp.float32
    ).astype(jnp.bfloat16)
    return (layer_out, d_tokens, grad_gate[None], grad_up[None], grad_down[None])


def solution(mesh):
    return jax.shard_map(
        local,
        mesh=mesh,
        in_specs=(
            P(("dp", "expert"), None),
            P(("dp", "expert"), None),
            P(("dp", "expert"), None),
            P(("dp", "expert"), None),
            P("expert", "dp", None),
            P("expert", "dp", None),
            P("expert", None, "dp"),
        ),
        out_specs=(
            P(("dp", "expert"), None),
            P(("dp", "expert"), None),
            P("expert", "dp", None),
            P("expert", "dp", None),
            P("expert", None, "dp"),
        ),
        check_vma=False,
    )
```

profile of v0, /device:TPU:0, one launch (start us, length us, event | category | flops | bytes accessed | tf_op | source)
XLA Modules:
  0.0 298.0 jit_solution(8474563770922269488)
XLA Ops:
  7.2 0.9 copy.34
  8.1 0.1 reshape.87
  8.1 0.2 fusion.26
  8.3 0.2 convolution_convert_fusion.7
  8.5 1.3 convolution_convert_fusion.1
  9.8 8.5 %copy.36 = bf16[1,16,16,2048]{2,1,0,3:T(8,128)(2,1)} copy(bf16[1,16,16,2048]{3,2,1,0:T(8,128)(2,1)S(1)} %bitcast.81) | data formatting | bytes 2097152 | tf_op jit(solution)/shard_map/reshape | solution.py:39
  18.3 11.7 %reshape.96 = bf16[2,2,131072]{2,1,0:T(2,128)(2,1)} reshape(bf16[2048,1,16,16]{3,2,1,0:T(8,128)(2,1)} %bitcast.77) | data formatting | bytes 2097152
  30.0 4.3 %all-to-all-start = ((bf16[2,2,131072]{2,1,0:T(2,128)(2,1)}), bf16[2,2,131072]{2,1,0:T(2,128)(2,1)S(1)}, u32[]{:S(2)}, u32[]{:S(2)}) async-start(bf16[2,2,131072]{2,1,0:T(2,128)(2,1)} %reshape.96), calls=%async_computation | async-start | bytes 2097152 | tf_op jit(solution)/shard_map/all_to_all | solution.py:42
  34.3 0.1 copy.35
  34.4 0.1 mul.54
  34.5 0.1 fusion.31
  34.7 2.0 convolution_convert_fusion
  36.7 9.7 %copy.42 = bf16[1,16,16,2048]{2,1,0,3:T(8,128)(2,1)} copy(bf16[1,16,16,2048]{3,2,1,0:T(8,128)(2,1)} %bitcast.82) | data formatting | bytes 2097152 | tf_op jit(solution)/shard_map/reshape | solution.py:40
  46.4 11.7 %reshape.98 = bf16[2,2,131072]{2,1,0:T(2,128)(2,1)} reshape(bf16[2048,1,16,16]{3,2,1,0:T(8,128)(2,1)} %bitcast.78) | data formatting | bytes 2097152
  58.1 4.7 %all-to-all-start.4 = ((bf16[2,2,131072]{2,1,0:T(2,128)(2,1)}), bf16[2,2,131072]{2,1,0:T(2,128)(2,1)}, u32[]{:S(2)}, u32[]{:S(2)}) async-start(bf16[2,2,131072]{2,1,0:T(2,128)(2,1)} %reshape.98), calls=%async_computation.4 | async-start | bytes 2097152 | tf_op jit(solution)/shard_map/all_to_all | solution.py:43
  62.8 7.8 %reshape.97 = bf16[2048,1,16,16]{3,2,1,0:T(8,128)(2,1)} reshape(bf16[2,2,131072]{2,1,0:T(2,128)(2,1)S(1)} %all-to-all-done) | data formatting | bytes 2097152
  70.5 9.6 %copy.48 = bf16[1,16,16,2,1024]{4,3,2,1,0:T(2,128)(2,1)} copy(bf16[1,16,16,2,1024]{2,1,4,3,0:T(8,128)(2,1)} %bitcast.79) | data formatting | bytes 2097152 | tf_op jit(solution)/shard_map/all_to_all | solution.py:42
  80.1 6.8 %all-to-all-start.1 = ((bf16[2,16,16,1024]{3,0,2,1:T(2,128)(2,1)}), bf16[2,16,16,1024]{3,0,2,1:T(2,128)(2,1)S(1)}, u32[]{:S(2)}, u32[]{:S(2)}) async-start(bf16[2,16,16,1024]{3,0,2,1:T(2,128)(2,1)} %bitcast.3), calls=%async_computation.1 | async-start | bytes 2097152 | tf_op jit(solution)/shard_map/all_to_all | solution.py:46
  86.9 8.7 %reshape.99 = bf16[2048,1,16,16]{3,2,1,0:T(8,128)(2,1)} reshape(bf16[2,2,131072]{2,1,0:T(2,128)(2,1)} %all-to-all-done.4) | data formatting | bytes 2097152
  95.7 9.6 %copy.49 = bf16[1,16,16,2,1024]{4,3,2,1,0:T(2,128)(2,1)} copy(bf16[1,16,16,2,1024]{2,1,4,3,0:T(8,128)(2,1)} %bitcast.80) | data formatting | bytes 2097152 | tf_op jit(solution)/shard_map/all_to_all | solution.py:43
  105.3 4.6 %all-to-all-done.1 = bf16[2,16,16,1024]{3,0,2,1:T(2,128)(2,1)S(1)} async-done(((bf16[2,16,16,1024]{3,0,2,1:T(2,128)(2,1)}), bf16[2,16,16,1024]{3,0,2,1:T(2,128)(2,1)S(1)}, u32[]{:S(2)}, u32[]{:S(2)}) %all-to-all-start.1) | async-done | bytes 1048608 | tf_op jit(solution)/shard_map/all_to_all | solution.py:46
  109.9 1.0 copy-done.2
  110.8 6.9 %all-to-all-start.5 = ((bf16[2,16,16,1024]{3,0,2,1:T(2,128)(2,1)}), bf16[2,16,16,1024]{3,0,2,1:T(2,128)(2,1)S(1)}, u32[]{:S(2)}, u32[]{:S(2)}) async-start(bf16[2,16,16,1024]{3,0,2,1:T(2,128)(2,1)} %bitcast.14), calls=%async_computation.5 | async-start | bytes 2097152 | tf_op jit(solution)/shard_map/all_to_all | solution.py:47
  117.8 1.6 copy.38
  119.4 0.1 copy-done.13
  119.5 1.9 fusion.20
  121.3 1.9 fusion.17
  123.2 0.0 reduce-scatter.2.cloned.1.call-start
  123.3 17.4 %all-to-all-done.5 = bf16[2,16,16,1024]{3,0,2,1:T(2,128)(2,1)S(1)} async-done(((bf16[2,16,16,1024]{3,0,2,1:T(2,128)(2,1)}), bf16[2,16,16,1024]{3,0,2,1:T(2,128)(2,1)S(1)}, u32[]{:S(2)}, u32[]{:S(2)}) %all-to-all-start.5) | async-done | bytes 1048608 | tf_op jit(solution)/shard_map/all_to_all | solution.py:47
  140.6 0.3 copy.44
  140.9 1.0 copy-done.4
  141.9 1.9 fusion.23
  143.9 33.0 %all-reduce.3.cloned.1.call-done = (bf16[512,768]{1,0:T(8,128)(2,1)}, bf16[512,768]{1,0:T(8,128)(2,1)}) async-done(((bf16[512,768]{1,0:T(8,128)(2,1)}, bf16[512,768]{1,0:T(8,128)(2,1)}), (bf16[512,768]{1,0:T(8,128)(2,1)}, bf16[512,768]{1,0:T(8,128)(2,1)})) %all-reduce.3.cloned.1.call-update) | async-done | bytes 1572880 | tf_op jit(solution)/shard_map/psum | solution.py:62
  176.8 2.5 fusion.11
  179.3 1.1 copy.39
  180.4 5.6 %all-to-all-start.2 = ((bf16[2,16,16,1024]{3,2,0,1:T(8,128)(2,1)}), bf16[2,16,16,1024]{3,2,0,1:T(8,128)(2,1)S(1)}, u32[]{:S(2)}, u32[]{:S(2)}) async-start(bf16[2,16,16,1024]{3,2,0,1:T(8,128)(2,1)} %copy.39), calls=%async_computation.2 | async-start | bytes 2097152 | tf_op jit(solution)/shard_map/all_to_all | solution.py:100
  186.1 1.2 convert_element_type.76
  187.3 2.4 convert_element_type.78
  189.7 7.0 %reduce-scatter.2.cloned.1.call-done = bf16[256,768]{1,0:T(8,128)(2,1)} async-done(((bf16[512,768]{1,0:T(8,128)(2,1)}), bf16[256,768]{1,0:T(8,128)(2,1)}) %reduce-scatter.2.cloned.1.call-update) | async-done | bytes 393232 | tf_op jit(solution)/shard_map/reduce_scatter | solution.py:74
  196.7 1.7 fusion.30
  198.3 11.7 %all_gather.6 = bf16[512,768]{1,0:T(8,128)(2,1)S(1)} all-gather(bf16[256,768]{1,0:T(8,128)(2,1)S(1)} %get-tuple-element.8), channel_id=1, replica_groups=mesh['dp'=2,'expert'=16] {'dp'}, dimensions={0}, use_global_device_ids=true | all-gather | bytes 1179648 | tf_op jit(solution)/shard_map/all_gather | solution.py:84
  210.0 10.9 %all_gather.7 = bf16[512,768]{1,0:T(8,128)(2,1)S(1)} all-gather(bf16[256,768]{1,0:T(8,128)(2,1)S(1)} %get-tuple-element.7), channel_id=1, replica_groups=mesh['dp'=2,'expert'=16] {'dp'}, dimensions={0}, use_global_device_ids=true | all-gather | bytes 1179648 | tf_op jit(solution)/shard_map/all_gather | solution.py:85
  220.9 1.0 fusion.7
  221.9 0.4 copy-done.14
  222.3 1.0 add_convert_fusion
  223.3 1.0 copy.45
  224.4 5.6 %all-to-all-start.6 = ((bf16[2,16,16,1024]{3,2,0,1:T(8,128)(2,1)}), bf16[2,16,16,1024]{3,2,0,1:T(8,128)(2,1)S(1)}, u32[]{:S(2)}, u32[]{:S(2)}) async-start(bf16[2,16,16,1024]{3,2,0,1:T(8,128)(2,1)} %copy.45), calls=%async_computation.7 | async-start | bytes 2097152 | tf_op jit(solution)/shard_map/all_to_all | solution.py:101
  230.0 1.1 copy.40
  231.1 21.9 %all-to-all-done.6 = bf16[2,16,16,1024]{3,2,0,1:T(8,128)(2,1)S(1)} async-done(((bf16[2,16,16,1024]{3,2,0,1:T(8,128)(2,1)}), bf16[2,16,16,1024]{3,2,0,1:T(8,128)(2,1)S(1)}, u32[]{:S(2)}, u32[]{:S(2)}) %all-to-all-start.6) | async-done | bytes 1048608 | tf_op jit(solution)/shard_map/all_to_all | solution.py:101
  252.9 3.6 %all-to-all-start.3 = ((bf16[2,16,16,1024]{3,2,1,0:T(8,128)(2,1)}), bf16[2,16,16,1024]{3,2,1,0:T(8,128)(2,1)S(1)}, u32[]{:S(2)}, u32[]{:S(2)}) async-start(bf16[2,16,16,1024]{3,2,1,0:T(8,128)(2,1)} %copy.40), calls=%async_computation.3 | async-start | bytes 2097152 | tf_op jit(solution)/shard_map/all_to_all | solution.py:104
  256.6 3.8 %fusion.14 = bf16[1,1024,768]{2,1,0:T(8,128)(2,1)} fusion(bf16[512,1024]{1,0:T(8,128)(2,1)} %bitcast.91, bf16[512,768]{1,0:T(8,128)(2,1)} %copy-done.6), kind=kOutput, calls=%fused_computation.21 | convolution fusion | flops 806092800 | bytes 3407872 | tf_op jit(solution)/shard_map/rd,rf->df/dot_general | solution.py:87
  260.3 2.3 fusion.16
  262.6 1.1 copy.46
  263.7 7.5 %all-to-all-done.3 = bf16[2,16,16,1024]{3,2,1,0:T(8,128)(2,1)S(1)} async-done(((bf16[2,16,16,1024]{3,2,1,0:T(8,128)(2,1)}), bf16[2,16,16,1024]{3,2,1,0:T(8,128)(2,1)S(1)}, u32[]{:S(2)}, u32[]{:S(2)}) %all-to-all-start.3) | async-done | bytes 1048608 | tf_op jit(solution)/shard_map/all_to_all | solution.py:104
  271.2 3.6 %all-to-all-start.7 = ((bf16[2,16,16,1024]{3,2,1,0:T(8,128)(2,1)}), bf16[2,16,16,1024]{3,2,1,0:T(8,128)(2,1)S(1)}, u32[]{:S(2)}, u32[]{:S(2)}) async-start(bf16[2,16,16,1024]{3,2,1,0:T(8,128)(2,1)} %copy.46), calls=%async_computation.8 | async-start | bytes 2097152 | tf_op jit(solution)/shard_map/all_to_all | solution.py:105
  274.8 3.4 %fusion.15 = bf16[1,1024,768]{2,1,0:T(8,128)(2,1)} fusion(bf16[512,1024]{1,0:T(8,128)(2,1)} %bitcast.92, bf16[512,768]{1,0:T(8,128)(2,1)S(1)} %all_gather.7), kind=kOutput, calls=%fused_computation.22 | convolution fusion | flops 806092800 | bytes 3407872 | tf_op jit(solution)/shard_map/rd,rf->df/dot_general | solution.py:90
  278.1 1.1 copy.41
  279.2 0.3 copy.50
  279.5 1.2 convolution_convert_fusion.3
  280.7 8.0 %all-to-all-done.7 = bf16[2,16,16,1024]{3,2,1,0:T(8,128)(2,1)S(1)} async-done(((bf16[2,16,16,1024]{3,2,1,0:T(8,128)(2,1)}), bf16[2,16,16,1024]{3,2,1,0:T(8,128)(2,1)S(1)}, u32[]{:S(2)}, u32[]{:S(2)}) %all-to-all-start.7) | async-done | bytes 1048608 | tf_op jit(solution)/shard_map/all_to_all | solution.py:105
  288.6 1.1 copy.47
  289.7 0.3 copy.51
  290.0 0.9 convolution_convert_fusion.2
  290.9 0.2 copy-done.1
  (32 shorter events, 0.2 us)
Async XLA Ops:
  7.2 134.7 %copy-start = (bf16[1,768,1024]{2,1,0:T(8,128)(2,1)S(1)}, bf16[1,768,1024]{2,1,0:T(8,128)(2,1)}, u32[]{:S(2)}) copy-start(bf16[1,768,1024]{2,1,0:T(8,128)(2,1)} %param.13) | copy-start | bytes 4718596
  30.0 4.3 %copy-start.10 = (f32[16,8]{0,1:T(8,128)S(1)}, f32[16,8]{0,1:T(8,128)}, u32[]{:S(2)}) copy-start(f32[16,8]{0,1:T(8,128)} %param.9) | copy-start | bytes 1540
  30.0 4.7 %copy-start.9 = (bf16[16,2048]{1,0:T(8,128)(2,1)S(1)}, bf16[16,2048]{1,0:T(8,128)(2,1)}, u32[]{:S(2)}) copy-start(bf16[16,2048]{1,0:T(8,128)(2,1)} %param.10) | copy-start | bytes 196612
  30.0 28.1 %all-to-all-start = ((bf16[2,2,131072]{2,1,0:T(2,128)(2,1)}), bf16[2,2,131072]{2,1,0:T(2,128)(2,1)S(1)}, u32[]{:S(2)}, u32[]{:S(2)}) async-start(bf16[2,2,131072]{2,1,0:T(2,128)(2,1)} %reshape.96), calls=%async_computation | async-start | bytes 2097152 | tf_op jit(solution)/shard_map/all_to_all | solution.py:42
  58.1 22.1 %all-to-all-start.4 = ((bf16[2,2,131072]{2,1,0:T(2,128)(2,1)}), bf16[2,2,131072]{2,1,0:T(2,128)(2,1)}, u32[]{:S(2)}, u32[]{:S(2)}) async-start(bf16[2,2,131072]{2,1,0:T(2,128)(2,1)} %reshape.98), calls=%async_computation.4 | async-start | bytes 2097152 | tf_op jit(solution)/shard_map/all_to_all | solution.py:43
  80.1 29.7 %all-to-all-start.1 = ((bf16[2,16,16,1024]{3,0,2,1:T(2,128)(2,1)}), bf16[2,16,16,1024]{3,0,2,1:T(2,128)(2,1)S(1)}, u32[]{:S(2)}, u32[]{:S(2)}) async-start(bf16[2,16,16,1024]{3,0,2,1:T(2,128)(2,1)} %bitcast.3), calls=%async_computation.1 | async-start | bytes 2097152 | tf_op jit(solution)/shard_map/all_to_all | solution.py:46
  109.9 1.0 copy-start.2
  110.8 29.8 %all-to-all-start.5 = ((bf16[2,16,16,1024]{3,0,2,1:T(2,128)(2,1)}), bf16[2,16,16,1024]{3,0,2,1:T(2,128)(2,1)S(1)}, u32[]{:S(2)}, u32[]{:S(2)}) async-start(bf16[2,16,16,1024]{3,0,2,1:T(2,128)(2,1)} %bitcast.14), calls=%async_computation.5 | async-start | bytes 2097152 | tf_op jit(solution)/shard_map/all_to_all | solution.py:47
  117.7 59.1 %all-reduce.3.cloned.1.call-start = ((), (), s32[]{:S(2)}) async-start(), calls=%async_computation.10 | async-start | bytes 3145728 | tf_op jit(solution)/shard_map/psum | solution.py:62
  117.8 1.7 copy-start.13
  119.4 1.9 copy-start.3
  119.5 1.9 copy-start.11
  123.2 73.4 %reduce-scatter.2.cloned.1.call-start = ((), (), s32[]{:S(2)}) async-start(), calls=%async_computation.9 | async-start | bytes 1179648 | tf_op jit(solution)/shard_map/reduce_scatter | solution.py:74
  140.9 1.0 copy-start.4
  180.4 44.0 %all-to-all-start.2 = ((bf16[2,16,16,1024]{3,2,0,1:T(8,128)(2,1)}), bf16[2,16,16,1024]{3,2,0,1:T(8,128)(2,1)S(1)}, u32[]{:S(2)}, u32[]{:S(2)}) async-start(bf16[2,16,16,1024]{3,2,0,1:T(8,128)(2,1)} %copy.39), calls=%async_computation.2 | async-start | bytes 2097152 | tf_op jit(solution)/shard_map/all_to_all | solution.py:100
  198.3 22.6 %copy-start.12 = (bf16[1,1024,768]{2,1,0:T(8,128)(2,1)S(1)}, bf16[1,1024,768]{2,1,0:T(8,128)(2,1)}, u32[]{:S(2)}) copy-start(bf16[1,1024,768]{2,1,0:T(8,128)(2,1)} %param.11) | copy-start | bytes 4718596
  210.0 10.9 %copy-start.6 = (bf16[512,768]{1,0:T(8,128)(2,1)}, bf16[512,768]{1,0:T(8,128)(2,1)S(1)}, u32[]{:S(2)}) copy-start(bf16[512,768]{1,0:T(8,128)(2,1)S(1)} %all_gather.6) | copy-start | bytes 2359300
  220.9 1.4 copy-start.14
  224.4 28.6 %all-to-all-start.6 = ((bf16[2,16,16,1024]{3,2,0,1:T(8,128)(2,1)}), bf16[2,16,16,1024]{3,2,0,1:T(8,128)(2,1)S(1)}, u32[]{:S(2)}, u32[]{:S(2)}) async-start(bf16[2,16,16,1024]{3,2,0,1:T(8,128)(2,1)} %copy.45), calls=%async_computation.7 | async-start | bytes 2097152 | tf_op jit(solution)/shard_map/all_to_all | solution.py:101
  252.9 18.2 %all-to-all-start.3 = ((bf16[2,16,16,1024]{3,2,1,0:T(8,128)(2,1)}), bf16[2,16,16,1024]{3,2,1,0:T(8,128)(2,1)S(1)}, u32[]{:S(2)}, u32[]{:S(2)}) async-start(bf16[2,16,16,1024]{3,2,1,0:T(8,128)(2,1)} %copy.40), calls=%async_computation.3 | async-start | bytes 2097152 | tf_op jit(solution)/shard_map/all_to_all | solution.py:104
  256.5 3.8 %copy-start.5 = (bf16[2,16,16,1024]{3,2,1,0:T(8,128)(2,1)S(1)}, bf16[2,16,16,1024]{3,2,1,0:T(8,128)(2,1)}, u32[]{:S(2)}) copy-start(bf16[2,16,16,1024]{3,2,1,0:T(8,128)(2,1)} %copy-done.4) | copy-start | bytes 3145732
  256.5 3.8 %copy-start.7 = (bf16[512,768]{1,0:T(8,128)(2,1)S(1)}, bf16[512,768]{1,0:T(8,128)(2,1)}, u32[]{:S(2)}) copy-start(bf16[512,768]{1,0:T(8,128)(2,1)} %get-tuple-element.5) | copy-start | bytes 2359300
  256.6 3.8 %copy-start.8 = (bf16[512,768]{1,0:T(8,128)(2,1)S(1)}, bf16[512,768]{1,0:T(8,128)(2,1)}, u32[]{:S(2)}) copy-start(bf16[512,768]{1,0:T(8,128)(2,1)} %get-tuple-element.6) | copy-start | bytes 2359300
  271.2 17.4 %all-to-all-start.7 = ((bf16[2,16,16,1024]{3,2,1,0:T(8,128)(2,1)}), bf16[2,16,16,1024]{3,2,1,0:T(8,128)(2,1)S(1)}, u32[]{:S(2)}, u32[]{:S(2)}) async-start(bf16[2,16,16,1024]{3,2,1,0:T(8,128)(2,1)} %copy.46), calls=%async_computation.8 | async-start | bytes 2097152 | tf_op jit(solution)/shard_map/all_to_all | solution.py:105
  289.7 1.4 copy-start.1
Sparse Core Ops, SparseCore 0:
  123.3 53.4 all-reduce.2
  179.2 17.4 reduce-scatter.1
where the time goes:
time: 300 us; the launch traced here: 298 us
  waiting for transfers between devices  99.3 us (33%)
  local copies, waits for them, and re-layouts  90 us (30%)
  starting transfers between devices  41.1 us (14%)
  matrix products  25.4 us (8%)
  blocking collectives  22.5 us (8%)
  between operations  14.3 us (5%)
  other arithmetic  5.32 us (2%)
    unnamed x38, local copies, waits for them, and re-layouts  44.1 us
    psum x1, waiting for transfers between devices, local(): lax.psum(up_part.astype(jnp.bfloat16), 'dp').astype(jnp.float32)  33 us
    all_to_all x1, waiting for transfers between devices, local(): lax.all_to_all(back_slots, 'expert', split_axis=1, concat_axis=1, tiled=T...  21.9 us
    all_to_all x1, waiting for transfers between devices, local(): lax.all_to_all(moved[1], 'expert', split_axis=1, concat_axis=1, tiled=True)  17.4 us
    all_gather x1, blocking collectives, local(): lax.all_gather(dgate_own, 'dp', axis=0, tiled=True)  11.7 us
    all_gather x1, blocking collectives, local(): lax.all_gather(dup_own, 'dp', axis=0, tiled=True)  10.9 us
    reshape x1, local copies, waits for them, and re-layouts, local(): send_dout = send_dout.reshape(1, experts, capacity, features)  9.72 us
    all_to_all x1, local copies, waits for them, and re-layouts, local(): lax.all_to_all(send_input, 'dp', split_axis=3, concat_axis=0, tiled=True)  9.59 us
  transfers between devices with their start and end apart: 10, of which 7 were waited for; matrix products, arithmetic and copies ran while one was open for 31% of the time, Pallas kernels for 0%

commit v1 on v0

--- a/solution.py
+++ b/solution.py
@@ -1,10 +1,337 @@
+import functools
+
 import jax
 import jax.numpy as jnp
 from jax import lax
+from jax.experimental import pallas as pl
+from jax.experimental.pallas import tpu as pltpu
 from jax.sharding import PartitionSpec as P
 
 
-def local(tokens, routes, gates, cotangent, w_gate, w_up, w_down):
+def swap(value, dp_bit, expert_bits):
+    groups, experts = lax.axis_size("dp"), lax.axis_size("expert")
+    if dp_bit == 0:
+        pairs = [(e, e ^ expert_bits) for e in range(experts)]
+        return lax.ppermute(value, "expert", pairs)
+    pairs = [
+        (d * experts + e, (d ^ dp_bit) * experts + (e ^ expert_bits))
+        for d in range(groups)
+        for e in range(experts)
+    ]
+    return lax.ppermute(value, ("dp", "expert"), pairs)
+
+
+def prepare_kernel(tokens_ref, routes_ref, gates_ref, cotangent_ref, mine_ref, other_ref, *, experts, part):
+    rows, fanout = tokens_ref.shape[0], routes_ref.shape[0]
+    width = mine_ref.shape[1] - 2 * part
+    routes, gates = routes_ref[...].T, gates_ref[...].T
+    lane = lax.broadcasted_iota(jnp.int32, (rows, width), 1)
+    named = lax.rem(lane, experts)
+    table = jnp.zeros((rows, width), jnp.float32)
+    for k in range(fanout):
+        table = table + jnp.where(routes[:, k : k + 1] == named, gates[:, k : k + 1], 0.0)
+    high = table.astype(jnp.bfloat16).astype(jnp.float32)
+    middle = (table - high).astype(jnp.bfloat16).astype(jnp.float32)
+    low = table - high - middle
+    piece = lane // experts
+    extra = jnp.where(piece == 0, high, jnp.where(piece == 1, middle, jnp.where(piece == 2, low, 0.0)))
+    extra = extra.astype(jnp.bfloat16)
+    dp_index = lax.axis_index("dp")
+    for ref, owner in ((mine_ref, dp_index), (other_ref, 1 - dp_index)):
+        columns = pl.ds(pl.multiple_of(owner * part, part), part)
+        ref[:, :part] = tokens_ref[:, columns]
+        ref[:, part : 2 * part] = cotangent_ref[:, columns]
+        ref[:, 2 * part :] = extra
+
+
+def begin(copies):
+    for copy in copies:
+        copy.start()
+    return copies
+
+
+def partial_kernel(count, parts, experts, part, *refs):
+    f32, bf16 = jnp.float32, jnp.bfloat16
+    pieces, weights = refs[:count], refs[count : count + 3]
+    scale_ref, input_ref, dout_ref = refs[-3:]
+    own_refs = refs[-3 - parts : -3]
+    gate_ref, up_ref, down_ref = (weight.at[0] for weight in weights)
+    units = gate_ref.shape[1]
+    start = 0
+    for piece in pieces:
+        rows = piece.shape[0]
+        here = slice(start, start + rows)
+        start += rows
+        extra = piece[:, 2 * part :].astype(f32)
+        lane = lax.broadcasted_iota(jnp.int32, extra.shape, 1)
+        scale = jnp.sum(
+            jnp.where(lax.rem(lane, experts) == lax.axis_index("expert"), extra, 0.0), axis=1, keepdims=True
+        )
+        scale_ref[here, :] = jnp.broadcast_to(scale, (rows, scale_ref.shape[1]))
+        input_ref[here, :] = piece[:, :part]
+        dout_ref[here, :] = (scale * piece[:, part : 2 * part].astype(f32)).astype(bf16)
+    def store(columns, value):
+        start = 0
+        for ref in own_refs:
+            ref[:, columns] = value[start : start + ref.shape[0]].astype(bf16)
+            start += ref.shape[0]
+
+    for i, weight in enumerate((gate_ref, up_ref)):
+        store(
+            slice(i * units, (i + 1) * units),
+            jnp.dot(input_ref[...], weight[...], preferred_element_type=f32),
+        )
+    across = (((1,), (1,)), ((), ()))
+    store(
+        slice(2 * units, 3 * units),
+        lax.dot_general(dout_ref[...], down_ref[...], across, preferred_element_type=f32),
+    )
+
+
+def expert_kernel(block, skipped, parts, first, own_ref, their_ref, scale_ref, *refs):
+    f32, bf16 = jnp.float32, jnp.bfloat16
+    weights, refs = refs[:3], refs[3 + skipped :]
+    pieces, refs = refs[:parts], refs[parts:]
+    hidden_ref, dgate_ref, dup_ref = refs
+    gate_ref, up_ref, down_ref = (weight.at[0] for weight in weights)
+    rows = own_ref.shape[0]
+    part, units = gate_ref.shape
+    blocks = [their_ref[(i ^ 1) * block : ((i ^ 1) + 1) * block, :] for i in range(rows // block)]
+    total = own_ref[...].astype(f32) + jnp.concatenate(blocks, axis=0).astype(f32)
+    gate, up, dhidden = total[:, :units], total[:, units : 2 * units], total[:, 2 * units :]
+    sigmoid = jax.nn.sigmoid(gate)
+    silu = gate * sigmoid
+    hidden_ref[...] = (silu * up).astype(bf16)
+    dgate_ref[...] = (dhidden * up * sigmoid * (1.0 + gate * (1.0 - sigmoid))).astype(bf16)
+    dup_ref[...] = (dhidden * silu).astype(bf16)
+    half = rows // parts
+    out = scale_ref[first : first + rows, :1] * jnp.dot(hidden_ref[...], down_ref[...], preferred_element_type=f32)
+    for i, ref in enumerate(pieces):
+        ref[:, :part] = out[i * half : (i + 1) * half].astype(bf16)
+    across = (((1,), (1,)), ((), ()))
+    back = lax.dot_general(dgate_ref[...], gate_ref[...], across, preferred_element_type=f32)
+    back = back + lax.dot_general(dup_ref[...], up_ref[...], across, preferred_element_type=f32)
+    for i, ref in enumerate(pieces):
+        ref[:, part:] = back[i * half : (i + 1) * half].astype(bf16)
+
+
+def merge_kernel(count, parts, *refs):
+    terms, pieces = refs[:count], refs[-parts:]
+    start = 0
+    for piece in pieces:
+        rows = piece.shape[0]
+        total = sum(term[start : start + rows, :].astype(jnp.float32) for term in terms)
+        piece[...] = total.astype(piece.dtype)
+        start += rows
+
+
+def gather_kernel(count, *refs):
+    start = 0
+    for piece in refs[:count]:
+        refs[-1][start : start + piece.shape[0], :] = piece[...]
+        start += piece.shape[0]
+
+
+def finish_kernel(count, *refs):
+    f32 = jnp.float32
+    out_ref, back_ref = refs[2 * count :]
+    part = refs[0].shape[1] // 2
+    dp_index = lax.axis_index("dp")
+    for owner, terms in ((dp_index, refs[:count]), (1 - dp_index, refs[count : 2 * count])):
+        columns = pl.ds(pl.multiple_of(owner * part, part), part)
+        for ref, start in ((out_ref, 0), (back_ref, part)):
+            total = sum(term[:, start : start + part].astype(f32) for term in terms)
+            ref[:, columns] = total.astype(ref.dtype)
+
+
+def grad_kernel(counts, *refs):
+    bf16 = jnp.bfloat16
+    groups, start = [], 0
+    for count in counts:
+        groups.append(refs[start : start + count])
+        start += count
+    outs, results, done = refs[-7:-4], refs[-4:-1], refs[-1]
+
+    def rows_of(group):
+        return jnp.concatenate([ref[...] for ref in group], axis=0)
+
+    over_rows = (((0,), (0,)), ((), ()))
+    copies = []
+    for i, (left, right) in enumerate(((0, 3), (0, 4), (2, 1))):
+        results[i][0] = lax.dot_general(
+            rows_of(groups[left]),
+            rows_of(groups[right]),
+            over_rows,
+            preferred_element_type=jnp.float32,
+        ).astype(bf16)
+        copies += begin([pltpu.make_async_copy(results[i], outs[i], done.at[i])])
+    for copy in copies:
+        copy.wait()
+
+
+def dense(tokens, routes, gates, cotangent, w_gate, w_up, w_down):
+    f32, bf16 = jnp.float32, jnp.bfloat16
+    rows, features = tokens.shape
+    experts = lax.axis_size("expert")
+    part, units = w_gate.shape[1:]
+    wide = 2 * part + -(-3 * experts // 128) * 128
+    params = pltpu.CompilerParams(vmem_limit_bytes=20 * 1024 * 1024)
+    largest = pltpu.CompilerParams(vmem_limit_bytes=52 * 1024 * 1024)
+    little = pltpu.CompilerParams(vmem_limit_bytes=4 * 1024 * 1024)
+    long = pl.CostEstimate(flops=int(1e10), bytes_accessed=1000, transcendentals=0)
+    small = pl.CostEstimate(flops=1000, bytes_accessed=1000, transcendentals=0)
+    vmem = pl.BlockSpec(memory_space=pltpu.VMEM)
+    anywhere = pl.BlockSpec(memory_space=pl.ANY)
+    hbm = pl.BlockSpec(memory_space=pltpu.HBM)
+
+    def shape(*dims, dtype=bf16):
+        return jax.ShapeDtypeStruct(dims, dtype)
+
+    mine, other = pl.pallas_call(
+        functools.partial(prepare_kernel, experts=experts, part=part),
+        out_shape=(shape(rows, wide), shape(rows, wide)),
+        in_specs=[vmem] * 4,
+        out_specs=(vmem, vmem),
+        cost_estimate=long,
+        compiler_params=params,
+        name="prepare",
+    )(tokens, routes.T, gates.T, cotangent)
+
+    weights = (w_gate, w_up, w_down)
+    busy = pl.CostEstimate(flops=int(1e3), bytes_accessed=1000, transcendentals=0)
+
+    last, kept = [], []
+
+    def partials(pieces, sizes):
+        nonlocal last
+        count = sum(piece.shape[0] for piece in pieces)
+        outs = pl.pallas_call(
+            functools.partial(partial_kernel, len(pieces), len(sizes), experts, part),
+            out_shape=tuple(shape(size, 3 * units) for size in sizes)
+            + (shape(count, 128, dtype=f32), shape(count, part), shape(count, part)),
+            in_specs=[vmem] * len(pieces) + [vmem] * (3 + len(last)),
+            out_specs=(vmem,) * (len(sizes) + 3),
+            cost_estimate=busy,
+            compiler_params=params,
+            name="partials",
+        )(*pieces, *weights, *last)
+        last = [outs[len(sizes)]]
+        return outs[: len(sizes)], outs[-3:]
+
+    def expert(own, theirs, scale, first, parts):
+        nonlocal last
+        count = own.shape[0]
+        outs = pl.pallas_call(
+            functools.partial(expert_kernel, rows, len(last), parts, first),
+            out_shape=(shape(count // parts, 2 * part),) * parts + (shape(count, units),) * 3,
+            in_specs=[vmem] * 3 + [vmem] * (3 + len(last)),
+            out_specs=(vmem,) * (parts + 3),
+            cost_estimate=busy,
+            compiler_params=params,
+            name="expert",
+        )(own, theirs, scale, *weights, *last)
+        last = [outs[0]]
+        return outs[:parts], outs[parts:]
+
+    def merge(terms, sizes):
+        nonlocal last
+        outs = pl.pallas_call(
+            functools.partial(merge_kernel, len(terms), len(sizes)),
+            out_shape=tuple(shape(size, terms[0].shape[1]) for size in sizes),
+            in_specs=[vmem] * (len(terms) + len(last)),
+            out_specs=(vmem,) * len(sizes),
+            cost_estimate=small,
+            compiler_params=little,
+            name="merge",
+        )(*terms, *last)
+        last = [outs[0]]
+        return list(outs)
+
+    def gather(pieces):
+        nonlocal last
+        out = pl.pallas_call(
+            functools.partial(gather_kernel, len(pieces)),
+            out_shape=shape(sum(piece.shape[0] for piece in pieces), pieces[0].shape[1]),
+            in_specs=[vmem] * (len(pieces) + len(last)),
+            out_specs=vmem,
+            cost_estimate=small if last else long,
+            compiler_params=little,
+            name="gather",
+        )(*pieces, *last)
+        last = [out]
+        return out
+
+    order = [4 * z for z in [0, 1] + list(range(experts // 4 - 1, 1, -1))]
+    steps = len(order)
+    quads = [gather([mine, swap(other, 1, 0), swap(mine, 0, 2), swap(other, 1, 2)])]
+    quads += [swap(quads[0], 0, bits) for bits in order[1:]]
+    sent, saved, near = {}, [], None
+
+    def project(k):
+        quad = gather([quads[k]]) if k > 1 else quads[k]
+        pieces = [quad, swap(quad, 0, 1)]
+        [own], (scale, *rest) = partials(pieces, [8 * rows])
+        sent[k] = (own, swap(own, 1, 0), scale)
+        kept.append(rest)
+
+    def act(k):
+        (keep, send), rest = expert(*sent[k], 0, 2)
+        saved.append(rest)
+        return [keep, swap(send, 0, 1)]
+
+    project(0)
+    project(1)
+    sums = []
+    for k in range(steps):
+        terms = act(k)
+        if k + 2 < steps:
+            relay = gather([quads[k + 2]])
+            across = swap(relay, 0, 1)
+        if k >= 2:
+            near = merge([near, sums[k - 1]], [4 * rows] if k < steps - 1 else [rows] * 4)
+            near = near[0] if k < steps - 1 else near
+        if k == steps - 1:
+            close = merge(terms, [rows] * 4)
+            break
+        [total] = merge(terms, [4 * rows])
+        if k == 0:
+            near = total
+        sums.append(swap(total, 0, order[k]) if k else total)
+        if k + 2 < steps:
+            [own], (scale, *rest) = partials([relay, across], [8 * rows])
+            sent[k + 2] = (own, swap(own, 1, 0), scale)
+            kept.append(rest)
+    moved = [swap(near[i], i % 2, 2 * (i // 2)) if i else near[i] for i in range(4)]
+    arrived = [swap(close[i], i % 2, order[-1] + 2 * (i // 2)) for i in range(4)]
+    layer_out, d_tokens = pl.pallas_call(
+        functools.partial(finish_kernel, 4),
+        out_shape=(shape(rows, features),) * 2,
+        in_specs=[vmem] * 8,
+        out_specs=(vmem,) * 2,
+        cost_estimate=small,
+        compiler_params=little,
+        name="finish",
+    )(moved[0], moved[2], arrived[0], arrived[2], moved[1], moved[3], arrived[1], arrived[3])
+
+    groups = [[arrays[i] for arrays in kept] for i in range(2)]
+    groups += [[arrays[i] for arrays in saved] for i in range(3)]
+    operands = [array for group in groups for array in group]
+    grad_shapes = [(1, part, units), (1, part, units), (1, units, part)]
+    grad_gate, grad_up, grad_down = pl.pallas_call(
+        functools.partial(grad_kernel, [len(group) for group in groups]),
+        out_shape=tuple(shape(*dims) for dims in grad_shapes),
+        in_specs=[vmem] * (len(operands) + len(last)),
+        out_specs=(anywhere,) * 3,
+        scratch_shapes=[pltpu.VMEM(dims, bf16) for dims in grad_shapes]
+        + [pltpu.SemaphoreType.DMA((3,))],
+        cost_estimate=busy,
+        compiler_params=params,
+        name="grads",
+    )(*operands, *last)
+    return (layer_out, d_tokens, grad_gate, grad_up, grad_down)
+
+
+def slots(tokens, routes, gates, cotangent, w_gate, w_up, w_down):
     tok_rows, features = tokens.shape
     fanout = routes.shape[1]
     experts = lax.axis_size("expert")
@@ -115,6 +442,15 @@
     return (layer_out, d_tokens, grad_gate[None], grad_up[None], grad_down[None])
 
 
+def local(tokens, routes, gates, cotangent, w_gate, w_up, w_down):
+    rows, fanout = routes.shape
+    experts, groups = lax.axis_size("expert"), lax.axis_size("dp")
+    capacity = min(rows, max(2, 2 * rows * fanout // experts))
+    bits = experts & (experts - 1) == 0 and experts % 4 == 0
+    form = dense if capacity == rows and groups == 2 and bits else slots
+    return form(tokens, routes, gates, cotangent, w_gate, w_up, w_down)
+
+
 def solution(mesh):
     return jax.shard_map(
         local,

time: 300 us -> 95.4 us (0.32)
  local copies, waits for them, and re-layouts: 90 us -> 3.06 us
  waiting for transfers between devices: 99.3 us -> 39.5 us
  matrix products: 25.4 us -> 0 us
  blocking collectives: 22.5 us -> 0 us
  Pallas kernels: 0 us -> 15.9 us
  between operations: 14.3 us -> 0.88 us
  other arithmetic: 5.32 us -> 0 us
  starting transfers between devices: 41.1 us -> 35.8 us
    all_to_all x8 -> x0, waiting for transfers between devices: 59.3 us -> none  [the longest x1 21.9 us: local(): lax.all_to_all(back_slots, 'expert', split_axis=1, concat_axis=1, tiled=T...]
    all_to_all x8 -> x0, starting transfers between devices: 41 us -> none  [the longest x1 6.86 us: local(): lax.all_to_all(moved[1], 'expert', split_axis=1, concat_axis=1, tiled=True)]
    unnamed x38 -> x14, local copies, waits for them, and re-layouts: 44.1 us -> 3.06 us
    ppermute x0 -> x27, waiting for transfers between devices: none -> 39.5 us  [the longest x17 23.9 us: swap(): return lax.ppermute(value, 'expert', pairs)]
    ppermute x0 -> x27, starting transfers between devices: none -> 35.8 us  [the longest x17 23.6 us: swap(): return lax.ppermute(value, 'expert', pairs)]
    psum x1 -> x0, waiting for transfers between devices: 33 us -> none  [local(): lax.psum(up_part.astype(jnp.bfloat16), 'dp').astype(jnp.float32)]
    dot_general x16 -> x0, matrix products: 25.4 us -> none  [the longest x1 3.76 us: local(): jnp.einsum('rd,rf->df', input_rows, dgate_all, preferred_element_type=jnp...]
    all_to_all x8 -> x0, local copies, waits for them, and re-layouts: 25.4 us -> none  [the longest x1 9.59 us: local(): lax.all_to_all(send_input, 'dp', split_axis=3, concat_axis=0, tiled=True)]
  transfers between devices with their start and end apart: 10 -> 27, of which waited for: 7 -> 13; matrix products, arithmetic and copies ran while one was open for 31% -> 0% of each run, Pallas kernels for 0% -> 16%
where the time goes in v1:
time: 95.4 us; the launch traced here: 95.2 us
  waiting for transfers between devices  39.5 us (41%)
  starting transfers between devices  35.8 us (38%)
  Pallas kernels  15.9 us (17%)
  local copies, waits for them, and re-layouts  3.06 us (3%)
    ppermute x17, waiting for transfers between devices, swap(): return lax.ppermute(value, 'expert', pairs)  23.9 us
    ppermute x17, starting transfers between devices, swap(): return lax.ppermute(value, 'expert', pairs)  23.6 us
    ppermute x10, waiting for transfers between devices, swap(): return lax.ppermute(value, ('dp', 'expert'), pairs)  15.6 us
    ppermute x10, starting transfers between devices, swap(): return lax.ppermute(value, ('dp', 'expert'), pairs)  12.1 us
    pallas_call x4, Pallas kernels, expert(): pl.pallas_call(functools.partial(expert_kernel, rows, len(last), parts, f...  5.77 us
    pallas_call x1, Pallas kernels, dense(): pl.pallas_call(functools.partial(grad_kernel, [len(group) for group in gr...  4.43 us
    pallas_call x4, Pallas kernels, partials(): pl.pallas_call(functools.partial(partial_kernel, len(pieces), len(sizes),...  4.37 us
    unnamed x14, local copies, waits for them, and re-layouts  3.06 us
  transfers between devices with their start and end apart: 27, of which 13 were waited for; matrix products, arithmetic and copies ran while one was open for 0% of the time, Pallas kernels for 16%

profile of v1, /device:TPU:0, one launch (start us, length us, event | category | flops | bytes accessed | tf_op | source)
XLA Modules:
  0.0 95.2 jit_solution(18058341431686188362)
XLA Ops:
  0.6 0.8 copy-done.3
  1.5 0.8 copy-done.4
  2.3 0.7 copy-done.5
  3.0 0.7 copy-done.6
  3.7 0.2 prepare.1
  3.9 3.0 %collective-permute-start.1 = (bf16[16,2176]{1,0:T(8,128)(2,1)S(1)}, bf16[16,2176]{1,0:T(8,128)(2,1)S(1)}, u32[]{:S(2)}, u32[]{:S(2)}) collective-permute-start(bf16[16,2176]{1,0:T(8,128)(2,1)S(1)} %get-tuple-element.56.refs_0_), channel_id=1, source_target_pairs={{0,2},{1,3},{2,0},{3,1},{4,6},{5,7},{6,4},{7,5},{8,10},{9,11},{10,... | collective-permute-start | bytes 208904 | tf_op jit(solution)/shard_map/ppermute | solution.py:15
  6.9 1.4 %collective-permute-start.2 = (bf16[16,2176]{1,0:T(8,128)(2,1)S(1)}, bf16[16,2176]{1,0:T(8,128)(2,1)S(1)}, u32[]{:S(2)}, u32[]{:S(2)}) collective-permute-start(bf16[16,2176]{1,0:T(8,128)(2,1)S(1)} %get-tuple-element.57), channel_id=1, source_target_pairs={{0,18},{1,19},{2,16},{3,17},{4,22},{5,23},{6,20},{7,21},{8,26},{9,... | collective-permute-start | bytes 208904 | tf_op jit(solution)/shard_map/ppermute | solution.py:21
  8.4 0.1 collective-permute-start
  8.5 1.3 %collective-permute-done.1.refs_2_ = bf16[16,2176]{1,0:T(8,128)(2,1)S(1)} collective-permute-done((bf16[16,2176]{1,0:T(8,128)(2,1)S(1)}, bf16[16,2176]{1,0:T(8,128)(2,1)S(1)}, u32[]{:S(2)}, u32[]{:S(2)}) %collective-permute-start.1) | collective-permute-done | bytes 69664 | tf_op jit(solution)/shard_map/ppermute | solution.py:15
  9.8 2.9 %collective-permute-done.2.refs_3_ = bf16[16,2176]{1,0:T(8,128)(2,1)S(1)} collective-permute-done((bf16[16,2176]{1,0:T(8,128)(2,1)S(1)}, bf16[16,2176]{1,0:T(8,128)(2,1)S(1)}, u32[]{:S(2)}, u32[]{:S(2)}) %collective-permute-start.2) | collective-permute-done | bytes 69664 | tf_op jit(solution)/shard_map/ppermute | solution.py:21
  12.7 0.1 collective-permute-start.3
  12.8 1.6 %collective-permute-start.5 = (bf16[64,2176]{1,0:T(8,128)(2,1)S(1)}, bf16[64,2176]{1,0:T(8,128)(2,1)S(1)}, u32[]{:S(2)}, u32[]{:S(2)}) collective-permute-start(bf16[64,2176]{1,0:T(8,128)(2,1)S(1)} %gather.3.refs_0_.refs_5_), channel_id=1, source_target_pairs={{0,4},{1,5},{2,6},{3,7},{4,0},{5,1},{6,2},{7,3},{8,12},{9,13},{10,... | collective-permute-start | bytes 835592 | tf_op jit(solution)/shard_map/ppermute | solution.py:15
  14.4 0.0 collective-permute-done.3.refs_1_
  14.5 1.1 %partials.4 = (bf16[128,2304]{1,0:T(8,128)(2,1)S(1)}, f32[128,128]{1,0:T(8,128)S(1)}, bf16[128,1024]{1,0:T(8,128)(2,1)S(1)}, bf16[128,1024]{1,0:T(8,128)(2,1)S(1)}) custom-call(bf16[64,2176]{1,0:T(8,128)(2,1)S(1)} %gather.3.refs_0_.refs_5_, bf16[64,2176]{1,0:T(8,128)(2,1)S(1)} %collective-permute-done.3.refs_1_, bf16[1,1024,768]{2,1,0:T(8,128)(2,1)S(1)} %copy-done, ...), custom_call_target="tpu_custom_call" | custom-call | flops 1000 | bytes 1000 | tf_op jit(solution)/shard_map/partials/pallas_call | solution.py:208
  15.6 1.1 %collective-permute-start.4 = (bf16[128,2304]{1,0:T(8,128)(2,1)S(1)}, bf16[128,2304]{1,0:T(8,128)(2,1)S(1)}, u32[]{:S(2)}, u32[]{:S(2)}) collective-permute-start(bf16[128,2304]{1,0:T(8,128)(2,1)S(1)} %get-tuple-element.58.own_ref), channel_id=1, source_target_pairs={{0,16},{1,17},{2,18},{3,19},{4,20},{5,21},{6,22},{7,23},{8,24},{9,... | collective-permute-start | bytes 1769480 | tf_op jit(solution)/shard_map/ppermute | solution.py:21
  16.6 5.2 %collective-permute-done.5.refs_0_ = bf16[64,2176]{1,0:T(8,128)(2,1)S(1)} collective-permute-done((bf16[64,2176]{1,0:T(8,128)(2,1)S(1)}, bf16[64,2176]{1,0:T(8,128)(2,1)S(1)}, u32[]{:S(2)}, u32[]{:S(2)}) %collective-permute-start.5) | collective-permute-done | bytes 278560 | tf_op jit(solution)/shard_map/ppermute | solution.py:15
  21.9 3.6 %collective-permute-start.8 = (bf16[64,2176]{1,0:T(8,128)(2,1)S(1)}, bf16[64,2176]{1,0:T(8,128)(2,1)S(1)}, u32[]{:S(2)}, u32[]{:S(2)}) collective-permute-start(bf16[64,2176]{1,0:T(8,128)(2,1)S(1)} %gather.3.refs_0_.refs_5_), channel_id=1, source_target_pairs={{0,12},{1,13},{2,14},{3,15},{4,8},{5,9},{6,10},{7,11},{8,4},{9,5},... | collective-permute-start | bytes 835592 | tf_op jit(solution)/shard_map/ppermute | solution.py:15
  25.5 0.0 collective-permute-done.6.refs_1_
  25.5 1.1 %partials.5 = (bf16[128,2304]{1,0:T(8,128)(2,1)S(1)}, f32[128,128]{1,0:T(8,128)S(1)}, bf16[128,1024]{1,0:T(8,128)(2,1)S(1)}, bf16[128,1024]{1,0:T(8,128)(2,1)S(1)}) custom-call(bf16[64,2176]{1,0:T(8,128)(2,1)S(1)} %collective-permute-done.5.refs_0_, bf16[64,2176]{1,0:T(8,128)(2,1)S(1)} %collective-permute-done.6.refs_1_, bf16[1,1024,768]{2,1,0:T(8,128)(2,1)S(1)} %copy-done, ...), custom_call_target="tpu_custom_call" | custom-call | flops 1000 | bytes 1000 | tf_op jit(solution)/shard_map/partials/pallas_call | solution.py:208
  26.6 1.1 %collective-permute-start.9 = (bf16[128,2304]{1,0:T(8,128)(2,1)S(1)}, bf16[128,2304]{1,0:T(8,128)(2,1)S(1)}, u32[]{:S(2)}, u32[]{:S(2)}) collective-permute-start(bf16[128,2304]{1,0:T(8,128)(2,1)S(1)} %get-tuple-element.63.own_ref), channel_id=1, source_target_pairs={{0,16},{1,17},{2,18},{3,19},{4,20},{5,21},{6,22},{7,23},{8,24},{9,... | collective-permute-start | bytes 1769480 | tf_op jit(solution)/shard_map/ppermute | solution.py:21
  27.7 4.1 %collective-permute-done.4.their_ref = bf16[128,2304]{1,0:T(8,128)(2,1)S(1)} collective-permute-done((bf16[128,2304]{1,0:T(8,128)(2,1)S(1)}, bf16[128,2304]{1,0:T(8,128)(2,1)S(1)}, u32[]{:S(2)}, u32[]{:S(2)}) %collective-permute-start.4) | collective-permute-done | bytes 589856 | tf_op jit(solution)/shard_map/ppermute | solution.py:21
  31.8 1.4 %expert.4 = (bf16[64,2048]{1,0:T(8,128)(2,1)S(1)}, bf16[64,2048]{1,0:T(8,128)(2,1)S(1)}, bf16[128,768]{1,0:T(8,128)(2,1)S(1)}, bf16[128,768]{1,0:T(8,128)(2,1)S(1)}, bf16[128,768]{1,0:T(8,128)(2,1)S(1)}) custom-call(bf16[128,2304]{1,0:T(8,128)(2,1)S(1)} %get-tuple-element.58.own_ref, bf16[128,2304]{1,0:T(8,128)(2,1)S(1)} %collective-permute-done.4.their_ref, ...), custom_call_target="tpu_custom_call" | custom-call | flops 1000 | bytes 1000 | tf_op jit(solution)/shard_map/expert/pallas_call | solution.py:224
  33.3 0.1 collective-permute-start.10
  33.4 0.5 collective-permute-start.7
  33.9 6.2 %collective-permute-start.12 = (bf16[64,2176]{1,0:T(8,128)(2,1)S(1)}, bf16[64,2176]{1,0:T(8,128)(2,1)S(1)}, u32[]{:S(2)}, u32[]{:S(2)}) collective-permute-start(bf16[64,2176]{1,0:T(8,128)(2,1)S(1)} %gather.3.refs_0_.refs_5_), channel_id=1, source_target_pairs={{0,8},{1,9},{2,10},{3,11},{4,12},{5,13},{6,14},{7,15},{8,0},{9,1},... | collective-permute-start | bytes 835592 | tf_op jit(solution)/shard_map/ppermute | solution.py:15
  40.1 0.1 merge.6.refs_5_.refs_0_
  40.2 0.0 collective-permute-done.10.refs_1_
  40.2 1.1 %partials.6 = (bf16[128,2304]{1,0:T(8,128)(2,1)S(1)}, f32[128,128]{1,0:T(8,128)S(1)}, bf16[128,1024]{1,0:T(8,128)(2,1)S(1)}, bf16[128,1024]{1,0:T(8,128)(2,1)S(1)}) custom-call(bf16[64,2176]{1,0:T(8,128)(2,1)S(1)} %gather.4.refs_2_.refs_0_, bf16[64,2176]{1,0:T(8,128)(2,1)S(1)} %collective-permute-done.10.refs_1_, bf16[1,1024,768]{2,1,0:T(8,128)(2,1)S(1)} %copy-done, ...), custom_call_target="tpu_custom_call" | custom-call | flops 1000 | bytes 1000 | tf_op jit(solution)/shard_map/partials/pallas_call | solution.py:208
  41.3 1.1 %collective-permute-start.14 = (bf16[128,2304]{1,0:T(8,128)(2,1)S(1)}, bf16[128,2304]{1,0:T(8,128)(2,1)S(1)}, u32[]{:S(2)}, u32[]{:S(2)}) collective-permute-start(bf16[128,2304]{1,0:T(8,128)(2,1)S(1)} %get-tuple-element.67.own_ref), channel_id=1, source_target_pairs={{0,16},{1,17},{2,18},{3,19},{4,20},{5,21},{6,22},{7,23},{8,24},{9,... | collective-permute-start | bytes 1769480 | tf_op jit(solution)/shard_map/ppermute | solution.py:21
  42.4 1.3 %collective-permute-done.9.their_ref = bf16[128,2304]{1,0:T(8,128)(2,1)S(1)} collective-permute-done((bf16[128,2304]{1,0:T(8,128)(2,1)S(1)}, bf16[128,2304]{1,0:T(8,128)(2,1)S(1)}, u32[]{:S(2)}, u32[]{:S(2)}) %collective-permute-start.9) | collective-permute-done | bytes 589856 | tf_op jit(solution)/shard_map/ppermute | solution.py:21
  43.7 1.4 %expert.5 = (bf16[64,2048]{1,0:T(8,128)(2,1)S(1)}, bf16[64,2048]{1,0:T(8,128)(2,1)S(1)}, bf16[128,768]{1,0:T(8,128)(2,1)S(1)}, bf16[128,768]{1,0:T(8,128)(2,1)S(1)}, bf16[128,768]{1,0:T(8,128)(2,1)S(1)}) custom-call(bf16[128,2304]{1,0:T(8,128)(2,1)S(1)} %get-tuple-element.63.own_ref, bf16[128,2304]{1,0:T(8,128)(2,1)S(1)} %collective-permute-done.9.their_ref, ...), custom_call_target="tpu_custom_call" | custom-call | flops 1000 | bytes 1000 | tf_op jit(solution)/shard_map/expert/pallas_call | solution.py:224
  45.1 7.9 %collective-permute-done.12.refs_0_ = bf16[64,2176]{1,0:T(8,128)(2,1)S(1)} collective-permute-done((bf16[64,2176]{1,0:T(8,128)(2,1)S(1)}, bf16[64,2176]{1,0:T(8,128)(2,1)S(1)}, u32[]{:S(2)}, u32[]{:S(2)}) %collective-permute-start.12) | collective-permute-done | bytes 278560 | tf_op jit(solution)/shard_map/ppermute | solution.py:15
  53.0 0.1 collective-permute-start.15
  53.1 0.5 collective-permute-start.11
  53.6 1.4 %collective-permute-done.11.refs_1_ = bf16[64,2048]{1,0:T(8,128)(2,1)S(1)} collective-permute-done((bf16[64,2048]{1,0:T(8,128)(2,1)S(1)}, bf16[64,2048]{1,0:T(8,128)(2,1)S(1)}, u32[]{:S(2)}, u32[]{:S(2)}) %collective-permute-start.11) | collective-permute-done | bytes 262176 | tf_op jit(solution)/shard_map/ppermute | solution.py:15
  55.0 0.1 merge.7.refs_5_
  55.0 0.0 collective-permute-done.15.refs_1_
  55.1 1.1 %partials.7 = (bf16[128,2304]{1,0:T(8,128)(2,1)S(1)}, f32[128,128]{1,0:T(8,128)S(1)}, bf16[128,1024]{1,0:T(8,128)(2,1)S(1)}, bf16[128,1024]{1,0:T(8,128)(2,1)S(1)}) custom-call(bf16[64,2176]{1,0:T(8,128)(2,1)S(1)} %gather.5.refs_2_.refs_0_, bf16[64,2176]{1,0:T(8,128)(2,1)S(1)} %collective-permute-done.15.refs_1_, bf16[1,1024,768]{2,1,0:T(8,128)(2,1)S(1)} %copy-done, ...), custom_call_target="tpu_custom_call" | custom-call | flops 1000 | bytes 1000 | tf_op jit(solution)/shard_map/partials/pallas_call | solution.py:208
  56.2 1.1 %collective-permute-start.18 = (bf16[128,2304]{1,0:T(8,128)(2,1)S(1)}, bf16[128,2304]{1,0:T(8,128)(2,1)S(1)}, u32[]{:S(2)}, u32[]{:S(2)}) collective-permute-start(bf16[128,2304]{1,0:T(8,128)(2,1)S(1)} %get-tuple-element.71.own_ref), channel_id=1, source_target_pairs={{0,16},{1,17},{2,18},{3,19},{4,20},{5,21},{6,22},{7,23},{8,24},{9,... | collective-permute-start | bytes 1769480 | tf_op jit(solution)/shard_map/ppermute | solution.py:21
  57.3 0.0 collective-permute-start.13
  57.3 0.0 collective-permute-done.14.their_ref
  57.3 1.5 %expert.6 = (bf16[64,2048]{1,0:T(8,128)(2,1)S(1)}, bf16[64,2048]{1,0:T(8,128)(2,1)S(1)}, bf16[128,768]{1,0:T(8,128)(2,1)S(1)}, bf16[128,768]{1,0:T(8,128)(2,1)S(1)}, bf16[128,768]{1,0:T(8,128)(2,1)S(1)}) custom-call(bf16[128,2304]{1,0:T(8,128)(2,1)S(1)} %get-tuple-element.67.own_ref, bf16[128,2304]{1,0:T(8,128)(2,1)S(1)} %collective-permute-done.14.their_ref, ...), custom_call_target="tpu_custom_call" | custom-call | flops 1000 | bytes 1000 | tf_op jit(solution)/shard_map/expert/pallas_call | solution.py:224
  58.7 0.1 collective-permute-start.16
  58.8 6.5 %collective-permute-done.13.refs_1_ = bf16[64,2048]{1,0:T(8,128)(2,1)S(1)} collective-permute-done((bf16[64,2048]{1,0:T(8,128)(2,1)S(1)}, bf16[64,2048]{1,0:T(8,128)(2,1)S(1)}, u32[]{:S(2)}, u32[]{:S(2)}) %collective-permute-start.13) | collective-permute-done | bytes 262176 | tf_op jit(solution)/shard_map/ppermute | solution.py:15
  65.3 0.1 merge.8.refs_2_.refs_0_
  65.4 0.1 merge.9.refs_3_
  65.5 1.4 %collective-permute-start.17 = (bf16[64,2048]{1,0:T(8,128)(2,1)S(1)}, bf16[64,2048]{1,0:T(8,128)(2,1)S(1)}, u32[]{:S(2)}, u32[]{:S(2)}) collective-permute-start(bf16[64,2048]{1,0:T(8,128)(2,1)S(1)} %merge.9.refs_3_), channel_id=1, source_target_pairs={{0,12},{1,13},{2,14},{3,15},{4,8},{5,9},{6,10},{7,11},{8,4},{9,5},... | collective-permute-start | bytes 786440 | tf_op jit(solution)/shard_map/ppermute | solution.py:15
  66.9 4.7 %collective-permute-done.18.their_ref = bf16[128,2304]{1,0:T(8,128)(2,1)S(1)} collective-permute-done((bf16[128,2304]{1,0:T(8,128)(2,1)S(1)}, bf16[128,2304]{1,0:T(8,128)(2,1)S(1)}, u32[]{:S(2)}, u32[]{:S(2)}) %collective-permute-start.18) | collective-permute-done | bytes 589856 | tf_op jit(solution)/shard_map/ppermute | solution.py:21
  71.6 1.4 %expert.7 = (bf16[64,2048]{1,0:T(8,128)(2,1)S(1)}, bf16[64,2048]{1,0:T(8,128)(2,1)S(1)}, bf16[128,768]{1,0:T(8,128)(2,1)S(1)}, bf16[128,768]{1,0:T(8,128)(2,1)S(1)}, bf16[128,768]{1,0:T(8,128)(2,1)S(1)}) custom-call(bf16[128,2304]{1,0:T(8,128)(2,1)S(1)} %get-tuple-element.71.own_ref, bf16[128,2304]{1,0:T(8,128)(2,1)S(1)} %collective-permute-done.18.their_ref, ...), custom_call_target="tpu_custom_call" | custom-call | flops 1000 | bytes 1000 | tf_op jit(solution)/shard_map/expert/pallas_call | solution.py:224
  73.0 0.1 collective-permute-start.20
  73.1 1.5 %collective-permute-done.17.refs_1_ = bf16[64,2048]{1,0:T(8,128)(2,1)S(1)} collective-permute-done((bf16[64,2048]{1,0:T(8,128)(2,1)S(1)}, bf16[64,2048]{1,0:T(8,128)(2,1)S(1)}, u32[]{:S(2)}, u32[]{:S(2)}) %collective-permute-start.17) | collective-permute-done | bytes 262176 | tf_op jit(solution)/shard_map/ppermute | solution.py:15
  74.6 0.1 merge.10
  74.7 1.4 %collective-permute-start.19 = (bf16[16,2048]{1,0:T(8,128)(2,1)S(1)}, bf16[16,2048]{1,0:T(8,128)(2,1)S(1)}, u32[]{:S(2)}, u32[]{:S(2)}) collective-permute-start(bf16[16,2048]{1,0:T(8,128)(2,1)S(1)} %get-tuple-element.74), channel_id=1, source_target_pairs={{0,2},{1,3},{2,0},{3,1},{4,6},{5,7},{6,4},{7,5},{8,10},{9,11},{10,... | collective-permute-start | bytes 196616 | tf_op jit(solution)/shard_map/ppermute | solution.py:15
  76.1 1.2 %collective-permute-start.23 = (bf16[16,2048]{1,0:T(8,128)(2,1)S(1)}, bf16[16,2048]{1,0:T(8,128)(2,1)S(1)}, u32[]{:S(2)}, u32[]{:S(2)}) collective-permute-start(bf16[16,2048]{1,0:T(8,128)(2,1)S(1)} %get-tuple-element.78), channel_id=1, source_target_pairs={{0,16},{1,17},{2,18},{3,19},{4,20},{5,21},{6,22},{7,23},{8,24},{9,... | collective-permute-start | bytes 196616 | tf_op jit(solution)/shard_map/ppermute | solution.py:21
  77.3 1.0 %collective-permute-start.24 = (bf16[16,2048]{1,0:T(8,128)(2,1)S(1)}, bf16[16,2048]{1,0:T(8,128)(2,1)S(1)}, u32[]{:S(2)}, u32[]{:S(2)}) collective-permute-start(bf16[16,2048]{1,0:T(8,128)(2,1)S(1)} %get-tuple-element.79), channel_id=1, source_target_pairs={{0,18},{1,19},{2,16},{3,17},{4,22},{5,23},{6,20},{7,21},{8,26},{9,... | collective-permute-start | bytes 196616 | tf_op jit(solution)/shard_map/ppermute | solution.py:21
  78.3 0.1 merge.11
  78.3 5.0 %collective-permute-start.22 = (bf16[16,2048]{1,0:T(8,128)(2,1)S(1)}, bf16[16,2048]{1,0:T(8,128)(2,1)S(1)}, u32[]{:S(2)}, u32[]{:S(2)}) collective-permute-start(bf16[16,2048]{1,0:T(8,128)(2,1)S(1)} %get-tuple-element.77), channel_id=1, source_target_pairs={{0,10},{1,11},{2,8},{3,9},{4,14},{5,15},{6,12},{7,13},{8,2},{9,3},... | collective-permute-start | bytes 196616 | tf_op jit(solution)/shard_map/ppermute | solution.py:15
  83.3 0.0 collective-permute-start.25
  83.3 4.0 %collective-permute-start.26 = (bf16[16,2048]{1,0:T(8,128)(2,1)S(1)}, bf16[16,2048]{1,0:T(8,128)(2,1)S(1)}, u32[]{:S(2)}, u32[]{:S(2)}) collective-permute-start(bf16[16,2048]{1,0:T(8,128)(2,1)S(1)} %get-tuple-element.81), channel_id=1, source_target_pairs={{0,26},{1,27},{2,24},{3,25},{4,30},{5,31},{6,28},{7,29},{8,18},{9,... | collective-permute-start | bytes 196616 | tf_op jit(solution)/shard_map/ppermute | solution.py:21
  87.3 4.4 %grads.1 = (bf16[1,1024,768]{2,1,0:T(8,128)(2,1)}, bf16[1,1024,768]{2,1,0:T(8,128)(2,1)}, bf16[1,768,1024]{2,1,0:T(8,128)(2,1)}) custom-call(bf16[128,1024]{1,0:T(8,128)(2,1)S(1)} %get-tuple-element.84.refs_0_, bf16[128,1024]{1,0:T(8,128)(2,1)S(1)} %get-tuple-element.85.refs_1_, bf16[128,1024]{1,0:T(8,128)(2,1)S(1)} %get-tuple-element.86.refs_2_, ...), custom_call_target="tpu_custom_call" | custom-call | flops 1000 | bytes 1000 | tf_op jit(solution)/shard_map/grads/pallas_call | solution.py:320
  91.8 1.8 %collective-permute-done.25.refs_6_ = bf16[16,2048]{1,0:T(8,128)(2,1)S(1)} collective-permute-done((bf16[16,2048]{1,0:T(8,128)(2,1)S(1)}, bf16[16,2048]{1,0:T(8,128)(2,1)S(1)}, u32[]{:S(2)}, u32[]{:S(2)}) %collective-permute-start.25) | collective-permute-done | bytes 65568 | tf_op jit(solution)/shard_map/ppermute | solution.py:21
  93.6 0.8 collective-permute-done.26.refs_7_
  94.4 0.1 collective-permute-done.21.refs_2_
  94.4 0.7 finish.1
  (24 shorter events, 0.1 us)
Async XLA Ops:
  0.6 0.8 copy-start.3
  1.5 0.8 copy-start.4
  2.3 0.7 copy-start.5
  3.0 0.7 copy-start.6
  3.9 5.9 %collective-permute-start.1 = (bf16[16,2176]{1,0:T(8,128)(2,1)S(1)}, bf16[16,2176]{1,0:T(8,128)(2,1)S(1)}, u32[]{:S(2)}, u32[]{:S(2)}) collective-permute-start(bf16[16,2176]{1,0:T(8,128)(2,1)S(1)} %get-tuple-element.56.refs_0_), channel_id=1, source_target_pairs={{0,2},{1,3},{2,0},{3,1},{4,6},{5,7},{6,4},{7,5},{8,10},{9,11},{10,... | collective-permute-start | bytes 208904 | tf_op jit(solution)/shard_map/ppermute | solution.py:15
  6.9 7.5 %copy-start = (bf16[1,1024,768]{2,1,0:T(8,128)(2,1)S(1)}, bf16[1,1024,768]{2,1,0:T(8,128)(2,1)}, u32[]{:S(2)}) copy-start(bf16[1,1024,768]{2,1,0:T(8,128)(2,1)} %refs_0_.7) | copy-start | bytes 4718596
  6.9 7.5 %copy-start.1 = (bf16[1,1024,768]{2,1,0:T(8,128)(2,1)S(1)}, bf16[1,1024,768]{2,1,0:T(8,128)(2,1)}, u32[]{:S(2)}) copy-start(bf16[1,1024,768]{2,1,0:T(8,128)(2,1)} %refs_1_.7) | copy-start | bytes 4718596
  6.9 7.5 %copy-start.2 = (bf16[1,768,1024]{2,1,0:T(8,128)(2,1)S(1)}, bf16[1,768,1024]{2,1,0:T(8,128)(2,1)}, u32[]{:S(2)}) copy-start(bf16[1,768,1024]{2,1,0:T(8,128)(2,1)} %refs_2_.15) | copy-start | bytes 4718596
  6.9 5.8 %collective-permute-start.2 = (bf16[16,2176]{1,0:T(8,128)(2,1)S(1)}, bf16[16,2176]{1,0:T(8,128)(2,1)S(1)}, u32[]{:S(2)}, u32[]{:S(2)}) collective-permute-start(bf16[16,2176]{1,0:T(8,128)(2,1)S(1)} %get-tuple-element.57), channel_id=1, source_target_pairs={{0,18},{1,19},{2,16},{3,17},{4,22},{5,23},{6,20},{7,21},{8,26},{9,... | collective-permute-start | bytes 208904 | tf_op jit(solution)/shard_map/ppermute | solution.py:21
  8.4 4.3 %collective-permute-start = (bf16[16,2176]{1,0:T(8,128)(2,1)S(1)}, bf16[16,2176]{1,0:T(8,128)(2,1)S(1)}, u32[]{:S(2)}, u32[]{:S(2)}) collective-permute-start(bf16[16,2176]{1,0:T(8,128)(2,1)S(1)} %get-tuple-element.57), channel_id=1, source_target_pairs={{0,16},{1,17},{2,18},{3,19},{4,20},{5,21},{6,22},{7,23},{8,24},{9,... | collective-permute-start | bytes 208904 | tf_op jit(solution)/shard_map/ppermute | solution.py:21
  12.7 1.7 %collective-permute-start.3 = (bf16[64,2176]{1,0:T(8,128)(2,1)S(1)}, bf16[64,2176]{1,0:T(8,128)(2,1)S(1)}, u32[]{:S(2)}, u32[]{:S(2)}) collective-permute-start(bf16[64,2176]{1,0:T(8,128)(2,1)S(1)} %gather.3.refs_0_.refs_5_), channel_id=1, source_target_pairs={{0,1},{1,0},{2,3},{3,2},{4,5},{5,4},{6,7},{7,6},{8,9},{9,8},{10,11... | collective-permute-start | bytes 835592 | tf_op jit(solution)/shard_map/ppermute | solution.py:15
  12.8 9.1 %collective-permute-start.5 = (bf16[64,2176]{1,0:T(8,128)(2,1)S(1)}, bf16[64,2176]{1,0:T(8,128)(2,1)S(1)}, u32[]{:S(2)}, u32[]{:S(2)}) collective-permute-start(bf16[64,2176]{1,0:T(8,128)(2,1)S(1)} %gather.3.refs_0_.refs_5_), channel_id=1, source_target_pairs={{0,4},{1,5},{2,6},{3,7},{4,0},{5,1},{6,2},{7,3},{8,12},{9,13},{10,... | collective-permute-start | bytes 835592 | tf_op jit(solution)/shard_map/ppermute | solution.py:15
  15.6 16.2 %collective-permute-start.4 = (bf16[128,2304]{1,0:T(8,128)(2,1)S(1)}, bf16[128,2304]{1,0:T(8,128)(2,1)S(1)}, u32[]{:S(2)}, u32[]{:S(2)}) collective-permute-start(bf16[128,2304]{1,0:T(8,128)(2,1)S(1)} %get-tuple-element.58.own_ref), channel_id=1, source_target_pairs={{0,16},{1,17},{2,18},{3,19},{4,20},{5,21},{6,22},{7,23},{8,24},{9,... | collective-permute-start | bytes 1769480 | tf_op jit(solution)/shard_map/ppermute | solution.py:21
  21.9 3.6 %collective-permute-start.6 = (bf16[64,2176]{1,0:T(8,128)(2,1)S(1)}, bf16[64,2176]{1,0:T(8,128)(2,1)S(1)}, u32[]{:S(2)}, u32[]{:S(2)}) collective-permute-start(bf16[64,2176]{1,0:T(8,128)(2,1)S(1)} %collective-permute-done.5.refs_0_), channel_id=1, source_target_pairs={{0,1},{1,0},{2,3},{3,2},{4,5},{5,4},{6,7},{7,6},{8,9},{9,8},{10,11... | collective-permute-start | bytes 835592 | tf_op jit(solution)/shard_map/ppermute | solution.py:15
  21.9 11.4 %collective-permute-start.8 = (bf16[64,2176]{1,0:T(8,128)(2,1)S(1)}, bf16[64,2176]{1,0:T(8,128)(2,1)S(1)}, u32[]{:S(2)}, u32[]{:S(2)}) collective-permute-start(bf16[64,2176]{1,0:T(8,128)(2,1)S(1)} %gather.3.refs_0_.refs_5_), channel_id=1, source_target_pairs={{0,12},{1,13},{2,14},{3,15},{4,8},{5,9},{6,10},{7,11},{8,4},{9,5},... | collective-permute-start | bytes 835592 | tf_op jit(solution)/shard_map/ppermute | solution.py:15
  26.6 17.1 %collective-permute-start.9 = (bf16[128,2304]{1,0:T(8,128)(2,1)S(1)}, bf16[128,2304]{1,0:T(8,128)(2,1)S(1)}, u32[]{:S(2)}, u32[]{:S(2)}) collective-permute-start(bf16[128,2304]{1,0:T(8,128)(2,1)S(1)} %get-tuple-element.63.own_ref), channel_id=1, source_target_pairs={{0,16},{1,17},{2,18},{3,19},{4,20},{5,21},{6,22},{7,23},{8,24},{9,... | collective-permute-start | bytes 1769480 | tf_op jit(solution)/shard_map/ppermute | solution.py:21
  33.3 6.9 %collective-permute-start.10 = (bf16[64,2176]{1,0:T(8,128)(2,1)S(1)}, bf16[64,2176]{1,0:T(8,128)(2,1)S(1)}, u32[]{:S(2)}, u32[]{:S(2)}) collective-permute-start(bf16[64,2176]{1,0:T(8,128)(2,1)S(1)} %gather.4.refs_2_.refs_0_), channel_id=1, source_target_pairs={{0,1},{1,0},{2,3},{3,2},{4,5},{5,4},{6,7},{7,6},{8,9},{9,8},{10,11... | collective-permute-start | bytes 835592 | tf_op jit(solution)/shard_map/ppermute | solution.py:15
  33.4 6.7 %collective-permute-start.7 = (bf16[64,2048]{1,0:T(8,128)(2,1)S(1)}, bf16[64,2048]{1,0:T(8,128)(2,1)S(1)}, u32[]{:S(2)}, u32[]{:S(2)}) collective-permute-start(bf16[64,2048]{1,0:T(8,128)(2,1)S(1)} %get-tuple-element.62), channel_id=1, source_target_pairs={{0,1},{1,0},{2,3},{3,2},{4,5},{5,4},{6,7},{7,6},{8,9},{9,8},{10,11... | collective-permute-start | bytes 786440 | tf_op jit(solution)/shard_map/ppermute | solution.py:15
  33.9 19.1 %collective-permute-start.12 = (bf16[64,2176]{1,0:T(8,128)(2,1)S(1)}, bf16[64,2176]{1,0:T(8,128)(2,1)S(1)}, u32[]{:S(2)}, u32[]{:S(2)}) collective-permute-start(bf16[64,2176]{1,0:T(8,128)(2,1)S(1)} %gather.3.refs_0_.refs_5_), channel_id=1, source_target_pairs={{0,8},{1,9},{2,10},{3,11},{4,12},{5,13},{6,14},{7,15},{8,0},{9,1},... | collective-permute-start | bytes 835592 | tf_op jit(solution)/shard_map/ppermute | solution.py:15
  41.3 16.0 %collective-permute-start.14 = (bf16[128,2304]{1,0:T(8,128)(2,1)S(1)}, bf16[128,2304]{1,0:T(8,128)(2,1)S(1)}, u32[]{:S(2)}, u32[]{:S(2)}) collective-permute-start(bf16[128,2304]{1,0:T(8,128)(2,1)S(1)} %get-tuple-element.67.own_ref), channel_id=1, source_target_pairs={{0,16},{1,17},{2,18},{3,19},{4,20},{5,21},{6,22},{7,23},{8,24},{9,... | collective-permute-start | bytes 1769480 | tf_op jit(solution)/shard_map/ppermute | solution.py:21
  53.0 2.1 %collective-permute-start.15 = (bf16[64,2176]{1,0:T(8,128)(2,1)S(1)}, bf16[64,2176]{1,0:T(8,128)(2,1)S(1)}, u32[]{:S(2)}, u32[]{:S(2)}) collective-permute-start(bf16[64,2176]{1,0:T(8,128)(2,1)S(1)} %gather.5.refs_2_.refs_0_), channel_id=1, source_target_pairs={{0,1},{1,0},{2,3},{3,2},{4,5},{5,4},{6,7},{7,6},{8,9},{9,8},{10,11... | collective-permute-start | bytes 835592 | tf_op jit(solution)/shard_map/ppermute | solution.py:15
  53.1 1.9 %collective-permute-start.11 = (bf16[64,2048]{1,0:T(8,128)(2,1)S(1)}, bf16[64,2048]{1,0:T(8,128)(2,1)S(1)}, u32[]{:S(2)}, u32[]{:S(2)}) collective-permute-start(bf16[64,2048]{1,0:T(8,128)(2,1)S(1)} %get-tuple-element.66), channel_id=1, source_target_pairs={{0,1},{1,0},{2,3},{3,2},{4,5},{5,4},{6,7},{7,6},{8,9},{9,8},{10,11... | collective-permute-start | bytes 786440 | tf_op jit(solution)/shard_map/ppermute | solution.py:15
  56.2 15.4 %collective-permute-start.18 = (bf16[128,2304]{1,0:T(8,128)(2,1)S(1)}, bf16[128,2304]{1,0:T(8,128)(2,1)S(1)}, u32[]{:S(2)}, u32[]{:S(2)}) collective-permute-start(bf16[128,2304]{1,0:T(8,128)(2,1)S(1)} %get-tuple-element.71.own_ref), channel_id=1, source_target_pairs={{0,16},{1,17},{2,18},{3,19},{4,20},{5,21},{6,22},{7,23},{8,24},{9,... | collective-permute-start | bytes 1769480 | tf_op jit(solution)/shard_map/ppermute | solution.py:21
  57.3 8.1 %collective-permute-start.13 = (bf16[64,2048]{1,0:T(8,128)(2,1)S(1)}, bf16[64,2048]{1,0:T(8,128)(2,1)S(1)}, u32[]{:S(2)}, u32[]{:S(2)}) collective-permute-start(bf16[64,2048]{1,0:T(8,128)(2,1)S(1)} %merge.7.refs_5_), channel_id=1, source_target_pairs={{0,4},{1,5},{2,6},{3,7},{4,0},{5,1},{6,2},{7,3},{8,12},{9,13},{10,... | collective-permute-start | bytes 786440 | tf_op jit(solution)/shard_map/ppermute | solution.py:15
  58.7 6.7 %collective-permute-start.16 = (bf16[64,2048]{1,0:T(8,128)(2,1)S(1)}, bf16[64,2048]{1,0:T(8,128)(2,1)S(1)}, u32[]{:S(2)}, u32[]{:S(2)}) collective-permute-start(bf16[64,2048]{1,0:T(8,128)(2,1)S(1)} %get-tuple-element.70), channel_id=1, source_target_pairs={{0,1},{1,0},{2,3},{3,2},{4,5},{5,4},{6,7},{7,6},{8,9},{9,8},{10,11... | collective-permute-start | bytes 786440 | tf_op jit(solution)/shard_map/ppermute | solution.py:15
  65.5 9.2 %collective-permute-start.17 = (bf16[64,2048]{1,0:T(8,128)(2,1)S(1)}, bf16[64,2048]{1,0:T(8,128)(2,1)S(1)}, u32[]{:S(2)}, u32[]{:S(2)}) collective-permute-start(bf16[64,2048]{1,0:T(8,128)(2,1)S(1)} %merge.9.refs_3_), channel_id=1, source_target_pairs={{0,12},{1,13},{2,14},{3,15},{4,8},{5,9},{6,10},{7,11},{8,4},{9,5},... | collective-permute-start | bytes 786440 | tf_op jit(solution)/shard_map/ppermute | solution.py:15
  73.0 5.2 %collective-permute-start.20 = (bf16[64,2048]{1,0:T(8,128)(2,1)S(1)}, bf16[64,2048]{1,0:T(8,128)(2,1)S(1)}, u32[]{:S(2)}, u32[]{:S(2)}) collective-permute-start(bf16[64,2048]{1,0:T(8,128)(2,1)S(1)} %get-tuple-element.75), channel_id=1, source_target_pairs={{0,1},{1,0},{2,3},{3,2},{4,5},{5,4},{6,7},{7,6},{8,9},{9,8},{10,11... | collective-permute-start | bytes 786440 | tf_op jit(solution)/shard_map/ppermute | solution.py:15
  74.7 8.6 %collective-permute-start.19 = (bf16[16,2048]{1,0:T(8,128)(2,1)S(1)}, bf16[16,2048]{1,0:T(8,128)(2,1)S(1)}, u32[]{:S(2)}, u32[]{:S(2)}) collective-permute-start(bf16[16,2048]{1,0:T(8,128)(2,1)S(1)} %get-tuple-element.74), channel_id=1, source_target_pairs={{0,2},{1,3},{2,0},{3,1},{4,6},{5,7},{6,4},{7,5},{8,10},{9,11},{10,... | collective-permute-start | bytes 196616 | tf_op jit(solution)/shard_map/ppermute | solution.py:15
  76.1 11.3 %collective-permute-start.23 = (bf16[16,2048]{1,0:T(8,128)(2,1)S(1)}, bf16[16,2048]{1,0:T(8,128)(2,1)S(1)}, u32[]{:S(2)}, u32[]{:S(2)}) collective-permute-start(bf16[16,2048]{1,0:T(8,128)(2,1)S(1)} %get-tuple-element.78), channel_id=1, source_target_pairs={{0,16},{1,17},{2,18},{3,19},{4,20},{5,21},{6,22},{7,23},{8,24},{9,... | collective-permute-start | bytes 196616 | tf_op jit(solution)/shard_map/ppermute | solution.py:21
  77.3 14.5 %collective-permute-start.24 = (bf16[16,2048]{1,0:T(8,128)(2,1)S(1)}, bf16[16,2048]{1,0:T(8,128)(2,1)S(1)}, u32[]{:S(2)}, u32[]{:S(2)}) collective-permute-start(bf16[16,2048]{1,0:T(8,128)(2,1)S(1)} %get-tuple-element.79), channel_id=1, source_target_pairs={{0,18},{1,19},{2,16},{3,17},{4,22},{5,23},{6,20},{7,21},{8,26},{9,... | collective-permute-start | bytes 196616 | tf_op jit(solution)/shard_map/ppermute | solution.py:21
  78.3 13.4 %collective-permute-start.22 = (bf16[16,2048]{1,0:T(8,128)(2,1)S(1)}, bf16[16,2048]{1,0:T(8,128)(2,1)S(1)}, u32[]{:S(2)}, u32[]{:S(2)}) collective-permute-start(bf16[16,2048]{1,0:T(8,128)(2,1)S(1)} %get-tuple-element.77), channel_id=1, source_target_pairs={{0,10},{1,11},{2,8},{3,9},{4,14},{5,15},{6,12},{7,13},{8,2},{9,3},... | collective-permute-start | bytes 196616 | tf_op jit(solution)/shard_map/ppermute | solution.py:15
  83.3 10.2 %collective-permute-start.25 = (bf16[16,2048]{1,0:T(8,128)(2,1)S(1)}, bf16[16,2048]{1,0:T(8,128)(2,1)S(1)}, u32[]{:S(2)}, u32[]{:S(2)}) collective-permute-start(bf16[16,2048]{1,0:T(8,128)(2,1)S(1)} %get-tuple-element.80), channel_id=1, source_target_pairs={{0,24},{1,25},{2,26},{3,27},{4,28},{5,29},{6,30},{7,31},{8,16},{9,... | collective-permute-start | bytes 196616 | tf_op jit(solution)/shard_map/ppermute | solution.py:21
  83.3 11.0 %collective-permute-start.26 = (bf16[16,2048]{1,0:T(8,128)(2,1)S(1)}, bf16[16,2048]{1,0:T(8,128)(2,1)S(1)}, u32[]{:S(2)}, u32[]{:S(2)}) collective-permute-start(bf16[16,2048]{1,0:T(8,128)(2,1)S(1)} %get-tuple-element.81), channel_id=1, source_target_pairs={{0,26},{1,27},{2,24},{3,25},{4,30},{5,31},{6,28},{7,29},{8,18},{9,... | collective-permute-start | bytes 196616 | tf_op jit(solution)/shard_map/ppermute | solution.py:21
  87.3 7.1 %collective-permute-start.21 = (bf16[16,2048]{1,0:T(8,128)(2,1)S(1)}, bf16[16,2048]{1,0:T(8,128)(2,1)S(1)}, u32[]{:S(2)}, u32[]{:S(2)}) collective-permute-start(bf16[16,2048]{1,0:T(8,128)(2,1)S(1)} %get-tuple-element.76.refs_20_), channel_id=1, source_target_pairs={{0,8},{1,9},{2,10},{3,11},{4,12},{5,13},{6,14},{7,15},{8,0},{9,1},... | collective-permute-start | bytes 196616 | tf_op jit(solution)/shard_map/ppermute | solution.py:15

commit v2 on v1

--- a/solution.py
+++ b/solution.py
@@ -115,20 +115,25 @@
         ref[:, part:] = back[i * half : (i + 1) * half].astype(bf16)
 
 
-def merge_kernel(count, parts, *refs):
-    terms, pieces = refs[:count], refs[-parts:]
+def merge_kernel(counts, parts, *refs):
+    terms, first = [], 0
+    for count in counts:
+        group = refs[first : first + count]
+        terms.append(jnp.concatenate([ref[...].astype(jnp.float32) for ref in group], axis=0))
+        first += count
+    total = sum(terms)
     start = 0
-    for piece in pieces:
+    for piece in refs[-parts:]:
         rows = piece.shape[0]
-        total = sum(term[start : start + rows, :].astype(jnp.float32) for term in terms)
-        piece[...] = total.astype(piece.dtype)
+        piece[...] = total[start : start + rows].astype(piece.dtype)
         start += rows
 
 
-def gather_kernel(count, *refs):
+def gather_kernel(count, parts, *refs):
+    rows = jnp.concatenate([ref[...] for ref in refs[:count]], axis=0)
     start = 0
-    for piece in refs[:count]:
-        refs[-1][start : start + piece.shape[0], :] = piece[...]
+    for piece in refs[-parts:]:
+        piece[...] = rows[start : start + piece.shape[0]]
         start += piece.shape[0]
 
 
@@ -150,7 +155,8 @@
     for count in counts:
         groups.append(refs[start : start + count])
         start += count
-    outs, results, done = refs[-7:-4], refs[-4:-1], refs[-1]
+    outs, token_ref, results, done = refs[-8:-5], refs[-5], refs[-4:-1], refs[-1]
+    token_ref[...] = jnp.zeros_like(token_ref)
 
     def rows_of(group):
         return jnp.concatenate([ref[...] for ref in group], axis=0)
@@ -176,13 +182,11 @@
     part, units = w_gate.shape[1:]
     wide = 2 * part + -(-3 * experts // 128) * 128
     params = pltpu.CompilerParams(vmem_limit_bytes=20 * 1024 * 1024)
-    largest = pltpu.CompilerParams(vmem_limit_bytes=52 * 1024 * 1024)
     little = pltpu.CompilerParams(vmem_limit_bytes=4 * 1024 * 1024)
     long = pl.CostEstimate(flops=int(1e10), bytes_accessed=1000, transcendentals=0)
     small = pl.CostEstimate(flops=1000, bytes_accessed=1000, transcendentals=0)
     vmem = pl.BlockSpec(memory_space=pltpu.VMEM)
     anywhere = pl.BlockSpec(memory_space=pl.ANY)
-    hbm = pl.BlockSpec(memory_space=pltpu.HBM)
 
     def shape(*dims, dtype=bf16):
         return jax.ShapeDtypeStruct(dims, dtype)
@@ -193,13 +197,11 @@
         in_specs=[vmem] * 4,
         out_specs=(vmem, vmem),
         cost_estimate=long,
-        compiler_params=params,
+        compiler_params=pltpu.CompilerParams(vmem_limit_bytes=58 * 1024 * 1024),
         name="prepare",
     )(tokens, routes.T, gates.T, cotangent)
 
     weights = (w_gate, w_up, w_down)
-    busy = pl.CostEstimate(flops=int(1e3), bytes_accessed=1000, transcendentals=0)
-
     last, kept = [], []
 
     def partials(pieces, sizes):
@@ -211,7 +213,7 @@
             + (shape(count, 128, dtype=f32), shape(count, part), shape(count, part)),
             in_specs=[vmem] * len(pieces) + [vmem] * (3 + len(last)),
             out_specs=(vmem,) * (len(sizes) + 3),
-            cost_estimate=busy,
+            cost_estimate=small,
             compiler_params=params,
             name="partials",
         )(*pieces, *weights, *last)
@@ -226,7 +228,7 @@
             out_shape=(shape(count // parts, 2 * part),) * parts + (shape(count, units),) * 3,
             in_specs=[vmem] * 3 + [vmem] * (3 + len(last)),
             out_specs=(vmem,) * (parts + 3),
-            cost_estimate=busy,
+            cost_estimate=small,
             compiler_params=params,
             name="expert",
         )(own, theirs, scale, *weights, *last)
@@ -235,99 +237,121 @@
 
     def merge(terms, sizes):
         nonlocal last
+        pieces = [piece for term in terms for piece in term]
         outs = pl.pallas_call(
-            functools.partial(merge_kernel, len(terms), len(sizes)),
-            out_shape=tuple(shape(size, terms[0].shape[1]) for size in sizes),
-            in_specs=[vmem] * (len(terms) + len(last)),
+            functools.partial(merge_kernel, [len(term) for term in terms], len(sizes)),
+            out_shape=tuple(shape(size, pieces[0].shape[1]) for size in sizes),
+            in_specs=[vmem] * (len(pieces) + len(last)),
             out_specs=(vmem,) * len(sizes),
             cost_estimate=small,
             compiler_params=little,
             name="merge",
-        )(*terms, *last)
+        )(*pieces, *last)
         last = [outs[0]]
         return list(outs)
 
-    def gather(pieces):
+    def gather(pieces, sizes):
         nonlocal last
-        out = pl.pallas_call(
-            functools.partial(gather_kernel, len(pieces)),
-            out_shape=shape(sum(piece.shape[0] for piece in pieces), pieces[0].shape[1]),
+        outs = pl.pallas_call(
+            functools.partial(gather_kernel, len(pieces), len(sizes)),
+            out_shape=tuple(shape(size, pieces[0].shape[1]) for size in sizes),
             in_specs=[vmem] * (len(pieces) + len(last)),
-            out_specs=vmem,
+            out_specs=(vmem,) * len(sizes),
             cost_estimate=small if last else long,
             compiler_params=little,
             name="gather",
         )(*pieces, *last)
-        last = [out]
-        return out
-
-    order = [4 * z for z in [0, 1] + list(range(experts // 4 - 1, 1, -1))]
-    steps = len(order)
-    quads = [gather([mine, swap(other, 1, 0), swap(mine, 0, 2), swap(other, 1, 2)])]
-    quads += [swap(quads[0], 0, bits) for bits in order[1:]]
-    sent, saved, near = {}, [], None
-
-    def project(k):
-        quad = gather([quads[k]]) if k > 1 else quads[k]
-        pieces = [quad, swap(quad, 0, 1)]
-        [own], (scale, *rest) = partials(pieces, [8 * rows])
-        sent[k] = (own, swap(own, 1, 0), scale)
+        last = [outs[0]]
+        return list(outs)
+
+    planes = experts // 4
+    far = list(range(planes - 1, 1, -1))
+    half = 2 * rows
+    [quad] = gather([mine, swap(other, 1, 0), swap(mine, 0, 2), swap(other, 1, 2)], [2 * half])
+    quads = [quad] + [swap(quad, 0, 4 * z) for z in range(1, planes)]
+    order, sent, saved, keeps, received, arrivals, total = [], {}, {}, {}, {}, {}, []
+
+    def project(z, side):
+        piece = swap(quads[z], 0, 1) if side else quads[z]
+        [own], (scale, *rest) = partials([piece], [piece.shape[0]])
+        sent[z, side] = (own, swap(own, 1, 0), scale)
         kept.append(rest)
-
-    def act(k):
-        (keep, send), rest = expert(*sent[k], 0, 2)
-        saved.append(rest)
-        return [keep, swap(send, 0, 1)]
-
-    project(0)
-    project(1)
-    sums = []
-    for k in range(steps):
-        terms = act(k)
-        if k + 2 < steps:
-            relay = gather([quads[k + 2]])
-            across = swap(relay, 0, 1)
-        if k >= 2:
-            near = merge([near, sums[k - 1]], [4 * rows] if k < steps - 1 else [rows] * 4)
-            near = near[0] if k < steps - 1 else near
-        if k == steps - 1:
-            close = merge(terms, [rows] * 4)
-            break
-        [total] = merge(terms, [4 * rows])
-        if k == 0:
-            near = total
-        sums.append(swap(total, 0, order[k]) if k else total)
-        if k + 2 < steps:
-            [own], (scale, *rest) = partials([relay, across], [8 * rows])
-            sent[k + 2] = (own, swap(own, 1, 0), scale)
-            kept.append(rest)
-    moved = [swap(near[i], i % 2, 2 * (i // 2)) if i else near[i] for i in range(4)]
-    arrived = [swap(close[i], i % 2, order[-1] + 2 * (i // 2)) for i in range(4)]
+        order.append((z, side))
+
+    def act(z, side):
+        [piece], saved[z, side] = expert(*sent[z, side], 0, 1)
+        if side:
+            received[z] = swap(piece, 0, 1)
+        else:
+            keeps[z] = piece
+
+    def send_sum(z):
+        [piece] = merge([[keeps[z]], [received[z]]], [2 * half])
+        arrivals[z] = swap(piece, 0, 4 * z)
+
+    def collect(z):
+        total[:] = merge([[piece] for piece in total] + [[arrivals.pop(z)]], [2 * half])
+
+    def run_grads():
+        nonlocal last
+        groups = [[arrays[i] for arrays in kept] for i in range(2)]
+        groups += [[saved[key][i] for key in order] for i in range(3)]
+        operands = [array for group in groups for array in group]
+        grad_shapes = [(1, part, units), (1, part, units), (1, units, part)]
+        grads = pl.pallas_call(
+            functools.partial(grad_kernel, [len(group) for group in groups]),
+            out_shape=tuple(shape(*dims) for dims in grad_shapes) + (shape(8, 128, dtype=f32),),
+            in_specs=[vmem] * (len(operands) + len(last)),
+            out_specs=(anywhere,) * 3 + (vmem,),
+            scratch_shapes=[pltpu.VMEM(dims, bf16) for dims in grad_shapes]
+            + [pltpu.SemaphoreType.DMA((3,))],
+            cost_estimate=small,
+            compiler_params=params,
+            name="grads",
+        )(*operands, *last)
+        last = [grads[3]]
+        return grads[:3]
+
+    project(0, 0)
+    project(1, 0)
+    if far:
+        project(far[0], 0)
+    act(0, 0)
+    act(1, 0)
+    if far:
+        project(far[0], 1)
+    for i, z in enumerate(far):
+        final = i + 1 == len(far)
+        project(1 if final else far[i + 1], 1 if final else 0)
+        act(z, 0)
+        act(z, 1)
+        project(0 if final else far[i + 1], 1)
+        if i > 0:
+            collect(far[i - 1])
+        send_sum(z)
+    if not far:
+        project(1, 1)
+        project(0, 1)
+    act(1, 1)
+    send_sum(1)
+    act(0, 1)
+    grad_gate, grad_up, grad_down = run_grads()
+    for z in [*far[-1:], 1]:
+        collect(z)
+    pieces = merge(
+        [[piece] for piece in (*total, keeps[0], received[0])], [rows] * 4
+    )
+    moved = [swap(pieces[i], i % 2, 2 * (i // 2)) if i else pieces[i] for i in range(4)]
     layer_out, d_tokens = pl.pallas_call(
-        functools.partial(finish_kernel, 4),
+        functools.partial(finish_kernel, 2),
         out_shape=(shape(rows, features),) * 2,
-        in_specs=[vmem] * 8,
+        in_specs=[vmem] * 4,
         out_specs=(vmem,) * 2,
         cost_estimate=small,
         compiler_params=little,
         name="finish",
-    )(moved[0], moved[2], arrived[0], arrived[2], moved[1], moved[3], arrived[1], arrived[3])
-
-    groups = [[arrays[i] for arrays in kept] for i in range(2)]
-    groups += [[arrays[i] for arrays in saved] for i in range(3)]
-    operands = [array for group in groups for array in group]
-    grad_shapes = [(1, part, units), (1, part, units), (1, units, part)]
-    grad_gate, grad_up, grad_down = pl.pallas_call(
-        functools.partial(grad_kernel, [len(group) for group in groups]),
-        out_shape=tuple(shape(*dims) for dims in grad_shapes),
-        in_specs=[vmem] * (len(operands) + len(last)),
-        out_specs=(anywhere,) * 3,
-        scratch_shapes=[pltpu.VMEM(dims, bf16) for dims in grad_shapes]
-        + [pltpu.SemaphoreType.DMA((3,))],
-        cost_estimate=busy,
-        compiler_params=params,
-        name="grads",
-    )(*operands, *last)
+    )(moved[0], moved[2], moved[1], moved[3])
+
     return (layer_out, d_tokens, grad_gate, grad_up, grad_down)
 
 
@@ -446,7 +470,7 @@
     rows, fanout = routes.shape
     experts, groups = lax.axis_size("expert"), lax.axis_size("dp")
     capacity = min(rows, max(2, 2 * rows * fanout // experts))
-    bits = experts & (experts - 1) == 0 and experts % 4 == 0
+    bits = experts & (experts - 1) == 0 and experts >= 8
     form = dense if capacity == rows and groups == 2 and bits else slots
     return form(tokens, routes, gates, cotangent, w_gate, w_up, w_down)
 

time: 95.4 us -> 92.5 us (0.970)
  Pallas kernels: 15.9 us -> 27.4 us
  starting transfers between devices: 35.8 us -> 28.1 us
  waiting for transfers between devices: 39.5 us -> 35.1 us
  local copies, waits for them, and re-layouts: 3.06 us -> 0.89 us
    ppermute x17 -> x16, starting transfers between devices: 23.6 us -> 17.6 us  [swap(): return lax.ppermute(value, 'expert', pairs)]
    pallas_call x4 -> x8, Pallas kernels: 5.77 us -> 10.9 us  [expert(): pl.pallas_call(functools.partial(expert_kernel, rows, len(last), parts, f...]
    pallas_call x4 -> x8, Pallas kernels: 4.37 us -> 9.14 us  [partials(): pl.pallas_call(functools.partial(partial_kernel, len(pieces), len(sizes),...]
    ppermute x17 -> x16, waiting for transfers between devices: 23.9 us -> 21.1 us  [swap(): return lax.ppermute(value, 'expert', pairs)]
    unnamed x14 -> x8, local copies, waits for them, and re-layouts: 3.06 us -> 0.89 us
    ppermute x10 -> x12, waiting for transfers between devices: 15.6 us -> 14 us  [swap(): return lax.ppermute(value, ('dp', 'expert'), pairs)]
    pallas_call x1, Pallas kernels: 0.2 us -> 1.77 us  [dense(): pl.pallas_call(functools.partial(prepare_kernel, experts=experts, part=pa...]
    ppermute x10 -> x12, starting transfers between devices: 12.1 us -> 10.6 us  [swap(): return lax.ppermute(value, ('dp', 'expert'), pairs)]
  transfers between devices with their start and end apart: 27 -> 28, of which waited for: 13 -> 13; matrix products, arithmetic and copies ran while one was open for 0% -> 0% of each run, Pallas kernels for 16% -> 27%
where the time goes in v2:
time: 92.5 us; the launch traced here: 92.3 us
  waiting for transfers between devices  35.1 us (38%)
  starting transfers between devices  28.1 us (30%)
  Pallas kernels  27.4 us (30%)
    ppermute x16, waiting for transfers between devices, swap(): return lax.ppermute(value, 'expert', pairs)  21.1 us
    ppermute x16, starting transfers between devices, swap(): return lax.ppermute(value, 'expert', pairs)  17.6 us
    ppermute x12, waiting for transfers between devices, swap(): return lax.ppermute(value, ('dp', 'expert'), pairs)  14 us
    pallas_call x8, Pallas kernels, expert(): pl.pallas_call(functools.partial(expert_kernel, rows, len(last), parts, f...  10.9 us
    ppermute x12, starting transfers between devices, swap(): return lax.ppermute(value, ('dp', 'expert'), pairs)  10.6 us
    pallas_call x8, Pallas kernels, partials(): pl.pallas_call(functools.partial(partial_kernel, len(pieces), len(sizes),...  9.14 us
    pallas_call x1, Pallas kernels, run_grads(): pl.pallas_call(functools.partial(grad_kernel, [len(group) for group in gr...  4.43 us
  transfers between devices with their start and end apart: 28, of which 13 were waited for; matrix products, arithmetic and copies ran while one was open for 0% of the time, Pallas kernels for 27%

profile of v2, /device:TPU:0, one launch (start us, length us, event | category | flops | bytes accessed | tf_op | source)
XLA Modules:
  0.0 92.3 jit_solution(12108536442144640170)
XLA Ops:
  0.6 1.8 %prepare.1 = (bf16[16,2176]{1,0:T(8,128)(2,1)}, bf16[16,2176]{1,0:T(8,128)(2,1)}) custom-call(bf16[16,2048]{1,0:T(8,128)(2,1)} %tokens_ref.1, s32[8,16]{1,0:T(8,128)} %bitcast.2, f32[8,16]{1,0:T(8,128)} %bitcast.3, bf16[16,2048]{1,0:T(8,128)(2,1)} %cotangent_ref.1), custom_call_target="tpu_custom_call" | custom-call | flops 10000000000 | bytes 1000 | tf_op jit(solution)/shard_map/prepare/pallas_call | solution.py:194
  2.4 3.0 %collective-permute-start.1 = (bf16[16,2176]{1,0:T(8,128)(2,1)}, bf16[16,2176]{1,0:T(8,128)(2,1)S(1)}, u32[]{:S(2)}, u32[]{:S(2)}) collective-permute-start(bf16[16,2176]{1,0:T(8,128)(2,1)} %get-tuple-element.81.refs_0_), channel_id=1, source_target_pairs={{0,2},{1,3},{2,0},{3,1},{4,6},{5,7},{6,4},{7,5},{8,10},{9,11},{10,... | collective-permute-start | bytes 208904 | tf_op jit(solution)/shard_map/ppermute | solution.py:15
  5.4 1.4 %collective-permute-start.2 = (bf16[16,2176]{1,0:T(8,128)(2,1)}, bf16[16,2176]{1,0:T(8,128)(2,1)S(1)}, u32[]{:S(2)}, u32[]{:S(2)}) collective-permute-start(bf16[16,2176]{1,0:T(8,128)(2,1)} %get-tuple-element.82), channel_id=1, source_target_pairs={{0,18},{1,19},{2,16},{3,17},{4,22},{5,23},{6,20},{7,21},{8,26},{9,... | collective-permute-start | bytes 208904 | tf_op jit(solution)/shard_map/ppermute | solution.py:21
  6.8 0.1 collective-permute-start
  6.9 1.6 %collective-permute-done.1.refs_2_ = bf16[16,2176]{1,0:T(8,128)(2,1)S(1)} collective-permute-done((bf16[16,2176]{1,0:T(8,128)(2,1)}, bf16[16,2176]{1,0:T(8,128)(2,1)S(1)}, u32[]{:S(2)}, u32[]{:S(2)}) %collective-permute-start.1) | collective-permute-done | bytes 69664 | tf_op jit(solution)/shard_map/ppermute | solution.py:15
  8.5 2.8 %collective-permute-done.2.refs_3_ = bf16[16,2176]{1,0:T(8,128)(2,1)S(1)} collective-permute-done((bf16[16,2176]{1,0:T(8,128)(2,1)}, bf16[16,2176]{1,0:T(8,128)(2,1)S(1)}, u32[]{:S(2)}, u32[]{:S(2)}) %collective-permute-start.2) | collective-permute-done | bytes 69664 | tf_op jit(solution)/shard_map/ppermute | solution.py:21
  11.3 0.9 copy-done.3
  12.2 1.6 %collective-permute-start.4 = (bf16[64,2176]{1,0:T(8,128)(2,1)S(1)}, bf16[64,2176]{1,0:T(8,128)(2,1)S(1)}, u32[]{:S(2)}, u32[]{:S(2)}) collective-permute-start(bf16[64,2176]{1,0:T(8,128)(2,1)S(1)} %gather.1.refs_0_.refs_4_), channel_id=1, source_target_pairs={{0,4},{1,5},{2,6},{3,7},{4,0},{5,1},{6,2},{7,3},{8,12},{9,13},{10,... | collective-permute-start | bytes 835592 | tf_op jit(solution)/shard_map/ppermute | solution.py:15
  13.9 2.5 %collective-permute-start.3 = (bf16[64,2176]{1,0:T(8,128)(2,1)S(1)}, bf16[64,2176]{1,0:T(8,128)(2,1)S(1)}, u32[]{:S(2)}, u32[]{:S(2)}) collective-permute-start(bf16[64,2176]{1,0:T(8,128)(2,1)S(1)} %gather.1.refs_0_.refs_4_), channel_id=1, source_target_pairs={{0,12},{1,13},{2,14},{3,15},{4,8},{5,9},{6,10},{7,11},{8,4},{9,5},... | collective-permute-start | bytes 835592 | tf_op jit(solution)/shard_map/ppermute | solution.py:15
  16.4 1.1 %partials.8 = (bf16[64,2304]{1,0:T(8,128)(2,1)S(1)}, f32[64,128]{1,0:T(8,128)S(1)}, bf16[64,1024]{1,0:T(8,128)(2,1)S(1)}, bf16[64,1024]{1,0:T(8,128)(2,1)S(1)}) custom-call(bf16[64,2176]{1,0:T(8,128)(2,1)S(1)} %gather.1.refs_0_.refs_4_, bf16[1,1024,768]{2,1,0:T(8,128)(2,1)S(1)} %copy-done, bf16[1,1024,768]{2,1,0:T(8,128)(2,1)S(1)} %copy-done.1, ...), custom_call_target="tpu_custom_call" | custom-call | flops 1000 | bytes 1000 | tf_op jit(solution)/shard_map/partials/pallas_call | solution.py:210
  17.5 1.1 %collective-permute-start.9 = (bf16[64,2304]{1,0:T(8,128)(2,1)S(1)}, bf16[64,2304]{1,0:T(8,128)(2,1)S(1)}, u32[]{:S(2)}, u32[]{:S(2)}) collective-permute-start(bf16[64,2304]{1,0:T(8,128)(2,1)S(1)} %get-tuple-element.88.own_ref), channel_id=1, source_target_pairs={{0,16},{1,17},{2,18},{3,19},{4,20},{5,21},{6,22},{7,23},{8,24},{9,... | collective-permute-start | bytes 884744 | tf_op jit(solution)/shard_map/ppermute | solution.py:21
  18.6 2.4 %collective-permute-done.4.refs_0_ = bf16[64,2176]{1,0:T(8,128)(2,1)S(1)} collective-permute-done((bf16[64,2176]{1,0:T(8,128)(2,1)S(1)}, bf16[64,2176]{1,0:T(8,128)(2,1)S(1)}, u32[]{:S(2)}, u32[]{:S(2)}) %collective-permute-start.4) | collective-permute-done | bytes 278560 | tf_op jit(solution)/shard_map/ppermute | solution.py:15
  21.0 1.1 %partials.9 = (bf16[64,2304]{1,0:T(8,128)(2,1)S(1)}, f32[64,128]{1,0:T(8,128)S(1)}, bf16[64,1024]{1,0:T(8,128)(2,1)S(1)}, bf16[64,1024]{1,0:T(8,128)(2,1)S(1)}) custom-call(bf16[64,2176]{1,0:T(8,128)(2,1)S(1)} %collective-permute-done.4.refs_0_, bf16[1,1024,768]{2,1,0:T(8,128)(2,1)S(1)} %copy-done, bf16[1,1024,768]{2,1,0:T(8,128)(2,1)S(1)} %copy-done.1, ...), custom_call_target="tpu_custom_call" | custom-call | flops 1000 | bytes 1000 | tf_op jit(solution)/shard_map/partials/pallas_call | solution.py:210
  22.1 1.1 %collective-permute-start.8 = (bf16[64,2304]{1,0:T(8,128)(2,1)S(1)}, bf16[64,2304]{1,0:T(8,128)(2,1)S(1)}, u32[]{:S(2)}, u32[]{:S(2)}) collective-permute-start(bf16[64,2304]{1,0:T(8,128)(2,1)S(1)} %get-tuple-element.87.own_ref), channel_id=1, source_target_pairs={{0,16},{1,17},{2,18},{3,19},{4,20},{5,21},{6,22},{7,23},{8,24},{9,... | collective-permute-start | bytes 884744 | tf_op jit(solution)/shard_map/ppermute | solution.py:21
  23.2 4.7 %collective-permute-done.3.refs_0_ = bf16[64,2176]{1,0:T(8,128)(2,1)S(1)} collective-permute-done((bf16[64,2176]{1,0:T(8,128)(2,1)S(1)}, bf16[64,2176]{1,0:T(8,128)(2,1)S(1)}, u32[]{:S(2)}, u32[]{:S(2)}) %collective-permute-start.3) | collective-permute-done | bytes 278560 | tf_op jit(solution)/shard_map/ppermute | solution.py:15
  27.9 1.8 %collective-permute-start.6 = (bf16[64,2176]{1,0:T(8,128)(2,1)S(1)}, bf16[64,2176]{1,0:T(8,128)(2,1)S(1)}, u32[]{:S(2)}, u32[]{:S(2)}) collective-permute-start(bf16[64,2176]{1,0:T(8,128)(2,1)S(1)} %gather.1.refs_0_.refs_4_), channel_id=1, source_target_pairs={{0,8},{1,9},{2,10},{3,11},{4,12},{5,13},{6,14},{7,15},{8,0},{9,1},... | collective-permute-start | bytes 835592 | tf_op jit(solution)/shard_map/ppermute | solution.py:15
  29.7 1.1 %partials.10 = (bf16[64,2304]{1,0:T(8,128)(2,1)S(1)}, f32[64,128]{1,0:T(8,128)S(1)}, bf16[64,1024]{1,0:T(8,128)(2,1)S(1)}, bf16[64,1024]{1,0:T(8,128)(2,1)S(1)}) custom-call(bf16[64,2176]{1,0:T(8,128)(2,1)S(1)} %collective-permute-done.3.refs_0_, bf16[1,1024,768]{2,1,0:T(8,128)(2,1)S(1)} %copy-done, bf16[1,1024,768]{2,1,0:T(8,128)(2,1)S(1)} %copy-done.1, ...), custom_call_target="tpu_custom_call" | custom-call | flops 1000 | bytes 1000 | tf_op jit(solution)/shard_map/partials/pallas_call | solution.py:210
  30.8 0.5 collective-permute-start.5
  31.3 1.3 %expert.8 = (bf16[64,2048]{1,0:T(8,128)(2,1)S(1)}, bf16[64,768]{1,0:T(8,128)(2,1)S(1)}, bf16[64,768]{1,0:T(8,128)(2,1)S(1)}, bf16[64,768]{1,0:T(8,128)(2,1)S(1)}) custom-call(bf16[64,2304]{1,0:T(8,128)(2,1)S(1)} %get-tuple-element.88.own_ref, bf16[64,2304]{1,0:T(8,128)(2,1)S(1)} %collective-permute-done.9.their_ref, ...), custom_call_target="tpu_custom_call" | custom-call | flops 1000 | bytes 1000 | tf_op jit(solution)/shard_map/expert/pallas_call | solution.py:226
  32.6 1.3 %expert.9 = (bf16[64,2048]{1,0:T(8,128)(2,1)S(1)}, bf16[64,768]{1,0:T(8,128)(2,1)S(1)}, bf16[64,768]{1,0:T(8,128)(2,1)S(1)}, bf16[64,768]{1,0:T(8,128)(2,1)S(1)}) custom-call(bf16[64,2304]{1,0:T(8,128)(2,1)S(1)} %get-tuple-element.87.own_ref, bf16[64,2304]{1,0:T(8,128)(2,1)S(1)} %collective-permute-done.8.their_ref, ...), custom_call_target="tpu_custom_call" | custom-call | flops 1000 | bytes 1000 | tf_op jit(solution)/shard_map/expert/pallas_call | solution.py:226
  34.0 1.1 %partials.11 = (bf16[64,2304]{1,0:T(8,128)(2,1)S(1)}, f32[64,128]{1,0:T(8,128)S(1)}, bf16[64,1024]{1,0:T(8,128)(2,1)S(1)}, bf16[64,1024]{1,0:T(8,128)(2,1)S(1)}) custom-call(bf16[64,2176]{1,0:T(8,128)(2,1)S(1)} %collective-permute-done.7.refs_0_, bf16[1,1024,768]{2,1,0:T(8,128)(2,1)S(1)} %copy-done, bf16[1,1024,768]{2,1,0:T(8,128)(2,1)S(1)} %copy-done.1, ...), custom_call_target="tpu_custom_call" | custom-call | flops 1000 | bytes 1000 | tf_op jit(solution)/shard_map/partials/pallas_call | solution.py:210
  35.2 1.7 %collective-permute-start.10 = (bf16[64,2304]{1,0:T(8,128)(2,1)S(1)}, bf16[64,2304]{1,0:T(8,128)(2,1)S(1)}, u32[]{:S(2)}, u32[]{:S(2)}) collective-permute-start(bf16[64,2304]{1,0:T(8,128)(2,1)S(1)} %get-tuple-element.94.own_ref), channel_id=1, source_target_pairs={{0,16},{1,17},{2,18},{3,19},{4,20},{5,21},{6,22},{7,23},{8,24},{9,... | collective-permute-start | bytes 884744 | tf_op jit(solution)/shard_map/ppermute | solution.py:21
  36.8 7.0 %collective-permute-done.6.refs_0_ = bf16[64,2176]{1,0:T(8,128)(2,1)S(1)} collective-permute-done((bf16[64,2176]{1,0:T(8,128)(2,1)S(1)}, bf16[64,2176]{1,0:T(8,128)(2,1)S(1)}, u32[]{:S(2)}, u32[]{:S(2)}) %collective-permute-start.6) | collective-permute-done | bytes 278560 | tf_op jit(solution)/shard_map/ppermute | solution.py:15
  43.9 0.5 collective-permute-start.17
  44.4 1.1 %partials.12 = (bf16[64,2304]{1,0:T(8,128)(2,1)S(1)}, f32[64,128]{1,0:T(8,128)S(1)}, bf16[64,1024]{1,0:T(8,128)(2,1)S(1)}, bf16[64,1024]{1,0:T(8,128)(2,1)S(1)}) custom-call(bf16[64,2176]{1,0:T(8,128)(2,1)S(1)} %collective-permute-done.6.refs_0_, bf16[1,1024,768]{2,1,0:T(8,128)(2,1)S(1)} %copy-done, bf16[1,1024,768]{2,1,0:T(8,128)(2,1)S(1)} %copy-done.1, ...), custom_call_target="tpu_custom_call" | custom-call | flops 1000 | bytes 1000 | tf_op jit(solution)/shard_map/partials/pallas_call | solution.py:210
  45.5 0.5 collective-permute-start.16
  46.0 1.3 %expert.10 = (bf16[64,2048]{1,0:T(8,128)(2,1)S(1)}, bf16[64,768]{1,0:T(8,128)(2,1)S(1)}, bf16[64,768]{1,0:T(8,128)(2,1)S(1)}, bf16[64,768]{1,0:T(8,128)(2,1)S(1)}) custom-call(bf16[64,2304]{1,0:T(8,128)(2,1)S(1)} %get-tuple-element.85.own_ref, bf16[64,2304]{1,0:T(8,128)(2,1)S(1)} %collective-permute-done.5.their_ref, ...), custom_call_target="tpu_custom_call" | custom-call | flops 1000 | bytes 1000 | tf_op jit(solution)/shard_map/expert/pallas_call | solution.py:226
  47.3 1.3 %expert.11 = (bf16[64,2048]{1,0:T(8,128)(2,1)S(1)}, bf16[64,768]{1,0:T(8,128)(2,1)S(1)}, bf16[64,768]{1,0:T(8,128)(2,1)S(1)}, bf16[64,768]{1,0:T(8,128)(2,1)S(1)}) custom-call(bf16[64,2304]{1,0:T(8,128)(2,1)S(1)} %get-tuple-element.94.own_ref, bf16[64,2304]{1,0:T(8,128)(2,1)S(1)} %collective-permute-done.10.their_ref, ...), custom_call_target="tpu_custom_call" | custom-call | flops 1000 | bytes 1000 | tf_op jit(solution)/shard_map/expert/pallas_call | solution.py:226
  48.7 0.1 collective-permute-start.11
  48.8 1.1 %partials.13 = (bf16[64,2304]{1,0:T(8,128)(2,1)S(1)}, f32[64,128]{1,0:T(8,128)S(1)}, bf16[64,1024]{1,0:T(8,128)(2,1)S(1)}, bf16[64,1024]{1,0:T(8,128)(2,1)S(1)}) custom-call(bf16[64,2176]{1,0:T(8,128)(2,1)S(1)} %collective-permute-done.12.refs_0_, bf16[1,1024,768]{2,1,0:T(8,128)(2,1)S(1)} %copy-done, bf16[1,1024,768]{2,1,0:T(8,128)(2,1)S(1)} %copy-done.1, ...), custom_call_target="tpu_custom_call" | custom-call | flops 1000 | bytes 1000 | tf_op jit(solution)/shard_map/partials/pallas_call | solution.py:210
  49.9 1.7 %collective-permute-start.15 = (bf16[64,2304]{1,0:T(8,128)(2,1)S(1)}, bf16[64,2304]{1,0:T(8,128)(2,1)S(1)}, u32[]{:S(2)}, u32[]{:S(2)}) collective-permute-start(bf16[64,2304]{1,0:T(8,128)(2,1)S(1)} %get-tuple-element.97.own_ref), channel_id=1, source_target_pairs={{0,16},{1,17},{2,18},{3,19},{4,20},{5,21},{6,22},{7,23},{8,24},{9,... | collective-permute-start | bytes 884744 | tf_op jit(solution)/shard_map/ppermute | solution.py:21
  51.6 0.2 collective-permute-start.14
  51.8 0.1 merge.7.refs_4_
  51.9 1.1 %partials.14 = (bf16[64,2304]{1,0:T(8,128)(2,1)S(1)}, f32[64,128]{1,0:T(8,128)S(1)}, bf16[64,1024]{1,0:T(8,128)(2,1)S(1)}, bf16[64,1024]{1,0:T(8,128)(2,1)S(1)}) custom-call(bf16[64,2176]{1,0:T(8,128)(2,1)S(1)} %collective-permute-done.17.refs_0_, bf16[1,1024,768]{2,1,0:T(8,128)(2,1)S(1)} %copy-done, bf16[1,1024,768]{2,1,0:T(8,128)(2,1)S(1)} %copy-done.1, ...), custom_call_target="tpu_custom_call" | custom-call | flops 1000 | bytes 1000 | tf_op jit(solution)/shard_map/partials/pallas_call | solution.py:210
  53.0 0.5 collective-permute-start.20
  53.5 2.7 %collective-permute-start.13 = (bf16[64,2048]{1,0:T(8,128)(2,1)S(1)}, bf16[64,2048]{1,0:T(8,128)(2,1)S(1)}, u32[]{:S(2)}, u32[]{:S(2)}) collective-permute-start(bf16[64,2048]{1,0:T(8,128)(2,1)S(1)} %merge.7.refs_4_), channel_id=1, source_target_pairs={{0,12},{1,13},{2,14},{3,15},{4,8},{5,9},{6,10},{7,11},{8,4},{9,5},... | collective-permute-start | bytes 786440 | tf_op jit(solution)/shard_map/ppermute | solution.py:15
  56.2 1.3 %expert.12 = (bf16[64,2048]{1,0:T(8,128)(2,1)S(1)}, bf16[64,768]{1,0:T(8,128)(2,1)S(1)}, bf16[64,768]{1,0:T(8,128)(2,1)S(1)}, bf16[64,768]{1,0:T(8,128)(2,1)S(1)}) custom-call(bf16[64,2304]{1,0:T(8,128)(2,1)S(1)} %get-tuple-element.98.own_ref, bf16[64,2304]{1,0:T(8,128)(2,1)S(1)} %collective-permute-done.16.their_ref, ...), custom_call_target="tpu_custom_call" | custom-call | flops 1000 | bytes 1000 | tf_op jit(solution)/shard_map/expert/pallas_call | solution.py:226
  57.5 4.3 %collective-permute-done.15.their_ref = bf16[64,2304]{1,0:T(8,128)(2,1)S(1)} collective-permute-done((bf16[64,2304]{1,0:T(8,128)(2,1)S(1)}, bf16[64,2304]{1,0:T(8,128)(2,1)S(1)}, u32[]{:S(2)}, u32[]{:S(2)}) %collective-permute-start.15) | collective-permute-done | bytes 294944 | tf_op jit(solution)/shard_map/ppermute | solution.py:21
  61.8 1.3 %expert.13 = (bf16[64,2048]{1,0:T(8,128)(2,1)S(1)}, bf16[64,768]{1,0:T(8,128)(2,1)S(1)}, bf16[64,768]{1,0:T(8,128)(2,1)S(1)}, bf16[64,768]{1,0:T(8,128)(2,1)S(1)}) custom-call(bf16[64,2304]{1,0:T(8,128)(2,1)S(1)} %get-tuple-element.97.own_ref, bf16[64,2304]{1,0:T(8,128)(2,1)S(1)} %collective-permute-done.15.their_ref, ...), custom_call_target="tpu_custom_call" | custom-call | flops 1000 | bytes 1000 | tf_op jit(solution)/shard_map/expert/pallas_call | solution.py:226
  63.1 0.1 collective-permute-start.18
  63.2 1.1 %partials.15 = (bf16[64,2304]{1,0:T(8,128)(2,1)S(1)}, f32[64,128]{1,0:T(8,128)S(1)}, bf16[64,1024]{1,0:T(8,128)(2,1)S(1)}, bf16[64,1024]{1,0:T(8,128)(2,1)S(1)}) custom-call(bf16[64,2176]{1,0:T(8,128)(2,1)S(1)} %collective-permute-done.14.refs_0_, bf16[1,1024,768]{2,1,0:T(8,128)(2,1)S(1)} %copy-done, bf16[1,1024,768]{2,1,0:T(8,128)(2,1)S(1)} %copy-done.1, ...), custom_call_target="tpu_custom_call" | custom-call | flops 1000 | bytes 1000 | tf_op jit(solution)/shard_map/partials/pallas_call | solution.py:210
  64.3 0.1 collective-permute-start.21
  64.5 0.3 collective-permute-done.18.refs_1_
  64.7 0.1 merge.9.refs_3_
  64.8 2.4 %collective-permute-done.20.their_ref = bf16[64,2304]{1,0:T(8,128)(2,1)S(1)} collective-permute-done((bf16[64,2304]{1,0:T(8,128)(2,1)S(1)}, bf16[64,2304]{1,0:T(8,128)(2,1)S(1)}, u32[]{:S(2)}, u32[]{:S(2)}) %collective-permute-start.20) | collective-permute-done | bytes 294944 | tf_op jit(solution)/shard_map/ppermute | solution.py:21
  67.1 1.5 %expert.14 = (bf16[64,2048]{1,0:T(8,128)(2,1)S(1)}, bf16[64,768]{1,0:T(8,128)(2,1)S(1)}, bf16[64,768]{1,0:T(8,128)(2,1)S(1)}, bf16[64,768]{1,0:T(8,128)(2,1)S(1)}) custom-call(bf16[64,2304]{1,0:T(8,128)(2,1)S(1)} %get-tuple-element.125.own_ref, bf16[64,2304]{1,0:T(8,128)(2,1)S(1)} %collective-permute-done.20.their_ref, ...), custom_call_target="tpu_custom_call" | custom-call | flops 1000 | bytes 1000 | tf_op jit(solution)/shard_map/expert/pallas_call | solution.py:226
  68.7 0.1 collective-permute-start.22
  68.7 1.7 %collective-permute-start.19 = (bf16[64,2048]{1,0:T(8,128)(2,1)S(1)}, bf16[64,2048]{1,0:T(8,128)(2,1)S(1)}, u32[]{:S(2)}, u32[]{:S(2)}) collective-permute-start(bf16[64,2048]{1,0:T(8,128)(2,1)S(1)} %merge.9.refs_3_), channel_id=1, source_target_pairs={{0,8},{1,9},{2,10},{3,11},{4,12},{5,13},{6,14},{7,15},{8,0},{9,1},... | collective-permute-start | bytes 786440 | tf_op jit(solution)/shard_map/ppermute | solution.py:15
  70.5 1.8 %collective-permute-start.23 = (bf16[64,2048]{1,0:T(8,128)(2,1)S(1)}, bf16[64,2048]{1,0:T(8,128)(2,1)S(1)}, u32[]{:S(2)}, u32[]{:S(2)}) collective-permute-start(bf16[64,2048]{1,0:T(8,128)(2,1)S(1)} %merge.10.refs_3_), channel_id=1, source_target_pairs={{0,4},{1,5},{2,6},{3,7},{4,0},{5,1},{6,2},{7,3},{8,12},{9,13},{10,... | collective-permute-start | bytes 786440 | tf_op jit(solution)/shard_map/ppermute | solution.py:15
  72.3 1.5 %collective-permute-done.21.their_ref = bf16[64,2304]{1,0:T(8,128)(2,1)S(1)} collective-permute-done((bf16[64,2304]{1,0:T(8,128)(2,1)S(1)}, bf16[64,2304]{1,0:T(8,128)(2,1)S(1)}, u32[]{:S(2)}, u32[]{:S(2)}) %collective-permute-start.21) | collective-permute-done | bytes 294944 | tf_op jit(solution)/shard_map/ppermute | solution.py:21
  73.8 1.3 %expert.15 = (bf16[64,2048]{1,0:T(8,128)(2,1)S(1)}, bf16[64,768]{1,0:T(8,128)(2,1)S(1)}, bf16[64,768]{1,0:T(8,128)(2,1)S(1)}, bf16[64,768]{1,0:T(8,128)(2,1)S(1)}) custom-call(bf16[64,2304]{1,0:T(8,128)(2,1)S(1)} %get-tuple-element.127.own_ref, bf16[64,2304]{1,0:T(8,128)(2,1)S(1)} %collective-permute-done.21.their_ref, ...), custom_call_target="tpu_custom_call" | custom-call | flops 1000 | bytes 1000 | tf_op jit(solution)/shard_map/expert/pallas_call | solution.py:226
  75.2 0.1 collective-permute-start.24
  75.2 4.4 %grads.1 = (bf16[1,1024,768]{2,1,0:T(8,128)(2,1)}, bf16[1,1024,768]{2,1,0:T(8,128)(2,1)}, bf16[1,768,1024]{2,1,0:T(8,128)(2,1)}, f32[8,128]{1,0:T(8,128)S(1)}) custom-call(bf16[64,1024]{1,0:T(8,128)(2,1)S(1)} %get-tuple-element.103.refs_0_, bf16[64,1024]{1,0:T(8,128)(2,1)S(1)} %get-tuple-element.104.refs_1_, ...), custom_call_target="tpu_custom_call" | custom-call | flops 1000 | bytes 1000 | tf_op jit(solution)/shard_map/grads/pallas_call | solution.py:301
  79.7 4.3 %collective-permute-done.19.refs_1_ = bf16[64,2048]{1,0:T(8,128)(2,1)S(1)} collective-permute-done((bf16[64,2048]{1,0:T(8,128)(2,1)S(1)}, bf16[64,2048]{1,0:T(8,128)(2,1)S(1)}, u32[]{:S(2)}, u32[]{:S(2)}) %collective-permute-start.19) | collective-permute-done | bytes 262176 | tf_op jit(solution)/shard_map/ppermute | solution.py:15
  84.0 0.1 merge.11.refs_0_.refs_2_
  84.1 0.1 merge.12.refs_0_.refs_3_
  84.1 0.1 merge.13
  84.2 1.6 %collective-permute-start.25 = (bf16[16,2048]{1,0:T(8,128)(2,1)S(1)}, bf16[16,2048]{1,0:T(8,128)(2,1)S(1)}, u32[]{:S(2)}, u32[]{:S(2)}) collective-permute-start(bf16[16,2048]{1,0:T(8,128)(2,1)S(1)} %get-tuple-element.149), channel_id=1, source_target_pairs={{0,2},{1,3},{2,0},{3,1},{4,6},{5,7},{6,4},{7,5},{8,10},{9,11},{10,... | collective-permute-start | bytes 196616 | tf_op jit(solution)/shard_map/ppermute | solution.py:15
  85.8 0.6 collective-permute-start.26
  86.5 1.3 %collective-permute-start.27 = (bf16[16,2048]{1,0:T(8,128)(2,1)S(1)}, bf16[16,2048]{1,0:T(8,128)(2,1)S(1)}, u32[]{:S(2)}, u32[]{:S(2)}) collective-permute-start(bf16[16,2048]{1,0:T(8,128)(2,1)S(1)} %get-tuple-element.151), channel_id=1, source_target_pairs={{0,18},{1,19},{2,16},{3,17},{4,22},{5,23},{6,20},{7,21},{8,26},{9,... | collective-permute-start | bytes 196616 | tf_op jit(solution)/shard_map/ppermute | solution.py:21
  87.8 0.8 collective-permute-done.25.refs_1_
  88.6 1.5 %collective-permute-done.26.refs_2_ = bf16[16,2048]{1,0:T(8,128)(2,1)S(1)} collective-permute-done((bf16[16,2048]{1,0:T(8,128)(2,1)S(1)}, bf16[16,2048]{1,0:T(8,128)(2,1)S(1)}, u32[]{:S(2)}, u32[]{:S(2)}) %collective-permute-start.26) | collective-permute-done | bytes 65568 | tf_op jit(solution)/shard_map/ppermute | solution.py:21
  90.1 1.5 %collective-permute-done.27.refs_3_ = bf16[16,2048]{1,0:T(8,128)(2,1)S(1)} collective-permute-done((bf16[16,2048]{1,0:T(8,128)(2,1)S(1)}, bf16[16,2048]{1,0:T(8,128)(2,1)S(1)}, u32[]{:S(2)}, u32[]{:S(2)}) %collective-permute-start.27) | collective-permute-done | bytes 65568 | tf_op jit(solution)/shard_map/ppermute | solution.py:21
  91.6 0.7 finish.1
  (27 shorter events, 0.2 us)
Async XLA Ops:
  2.4 6.1 %collective-permute-start.1 = (bf16[16,2176]{1,0:T(8,128)(2,1)}, bf16[16,2176]{1,0:T(8,128)(2,1)S(1)}, u32[]{:S(2)}, u32[]{:S(2)}) collective-permute-start(bf16[16,2176]{1,0:T(8,128)(2,1)} %get-tuple-element.81.refs_0_), channel_id=1, source_target_pairs={{0,2},{1,3},{2,0},{3,1},{4,6},{5,7},{6,4},{7,5},{8,10},{9,11},{10,... | collective-permute-start | bytes 208904 | tf_op jit(solution)/shard_map/ppermute | solution.py:15
  5.4 11.0 %copy-start = (bf16[1,1024,768]{2,1,0:T(8,128)(2,1)S(1)}, bf16[1,1024,768]{2,1,0:T(8,128)(2,1)}, u32[]{:S(2)}) copy-start(bf16[1,1024,768]{2,1,0:T(8,128)(2,1)} %refs_0_.15) | copy-start | bytes 4718596
  5.4 11.0 %copy-start.1 = (bf16[1,1024,768]{2,1,0:T(8,128)(2,1)S(1)}, bf16[1,1024,768]{2,1,0:T(8,128)(2,1)}, u32[]{:S(2)}) copy-start(bf16[1,1024,768]{2,1,0:T(8,128)(2,1)} %refs_1_.31) | copy-start | bytes 4718596
  5.4 11.0 %copy-start.2 = (bf16[1,768,1024]{2,1,0:T(8,128)(2,1)S(1)}, bf16[1,768,1024]{2,1,0:T(8,128)(2,1)}, u32[]{:S(2)}) copy-start(bf16[1,768,1024]{2,1,0:T(8,128)(2,1)} %refs_2_.31) | copy-start | bytes 4718596
  5.4 6.0 %collective-permute-start.2 = (bf16[16,2176]{1,0:T(8,128)(2,1)}, bf16[16,2176]{1,0:T(8,128)(2,1)S(1)}, u32[]{:S(2)}, u32[]{:S(2)}) collective-permute-start(bf16[16,2176]{1,0:T(8,128)(2,1)} %get-tuple-element.82), channel_id=1, source_target_pairs={{0,18},{1,19},{2,16},{3,17},{4,22},{5,23},{6,20},{7,21},{8,26},{9,... | collective-permute-start | bytes 208904 | tf_op jit(solution)/shard_map/ppermute | solution.py:21
  6.8 4.5 %collective-permute-start = (bf16[16,2176]{1,0:T(8,128)(2,1)}, bf16[16,2176]{1,0:T(8,128)(2,1)S(1)}, u32[]{:S(2)}, u32[]{:S(2)}) collective-permute-start(bf16[16,2176]{1,0:T(8,128)(2,1)} %get-tuple-element.82), channel_id=1, source_target_pairs={{0,16},{1,17},{2,18},{3,19},{4,20},{5,21},{6,22},{7,23},{8,24},{9,... | collective-permute-start | bytes 208904 | tf_op jit(solution)/shard_map/ppermute | solution.py:21
  11.3 0.9 copy-start.3
  12.2 8.8 %collective-permute-start.4 = (bf16[64,2176]{1,0:T(8,128)(2,1)S(1)}, bf16[64,2176]{1,0:T(8,128)(2,1)S(1)}, u32[]{:S(2)}, u32[]{:S(2)}) collective-permute-start(bf16[64,2176]{1,0:T(8,128)(2,1)S(1)} %gather.1.refs_0_.refs_4_), channel_id=1, source_target_pairs={{0,4},{1,5},{2,6},{3,7},{4,0},{5,1},{6,2},{7,3},{8,12},{9,13},{10,... | collective-permute-start | bytes 835592 | tf_op jit(solution)/shard_map/ppermute | solution.py:15
  13.9 14.0 %collective-permute-start.3 = (bf16[64,2176]{1,0:T(8,128)(2,1)S(1)}, bf16[64,2176]{1,0:T(8,128)(2,1)S(1)}, u32[]{:S(2)}, u32[]{:S(2)}) collective-permute-start(bf16[64,2176]{1,0:T(8,128)(2,1)S(1)} %gather.1.refs_0_.refs_4_), channel_id=1, source_target_pairs={{0,12},{1,13},{2,14},{3,15},{4,8},{5,9},{6,10},{7,11},{8,4},{9,5},... | collective-permute-start | bytes 835592 | tf_op jit(solution)/shard_map/ppermute | solution.py:15
  17.5 13.8 %collective-permute-start.9 = (bf16[64,2304]{1,0:T(8,128)(2,1)S(1)}, bf16[64,2304]{1,0:T(8,128)(2,1)S(1)}, u32[]{:S(2)}, u32[]{:S(2)}) collective-permute-start(bf16[64,2304]{1,0:T(8,128)(2,1)S(1)} %get-tuple-element.88.own_ref), channel_id=1, source_target_pairs={{0,16},{1,17},{2,18},{3,19},{4,20},{5,21},{6,22},{7,23},{8,24},{9,... | collective-permute-start | bytes 884744 | tf_op jit(solution)/shard_map/ppermute | solution.py:21
  22.1 10.5 %collective-permute-start.8 = (bf16[64,2304]{1,0:T(8,128)(2,1)S(1)}, bf16[64,2304]{1,0:T(8,128)(2,1)S(1)}, u32[]{:S(2)}, u32[]{:S(2)}) collective-permute-start(bf16[64,2304]{1,0:T(8,128)(2,1)S(1)} %get-tuple-element.87.own_ref), channel_id=1, source_target_pairs={{0,16},{1,17},{2,18},{3,19},{4,20},{5,21},{6,22},{7,23},{8,24},{9,... | collective-permute-start | bytes 884744 | tf_op jit(solution)/shard_map/ppermute | solution.py:21
  27.9 6.1 %collective-permute-start.7 = (bf16[64,2176]{1,0:T(8,128)(2,1)S(1)}, bf16[64,2176]{1,0:T(8,128)(2,1)S(1)}, u32[]{:S(2)}, u32[]{:S(2)}) collective-permute-start(bf16[64,2176]{1,0:T(8,128)(2,1)S(1)} %collective-permute-done.3.refs_0_), channel_id=1, source_target_pairs={{0,1},{1,0},{2,3},{3,2},{4,5},{5,4},{6,7},{7,6},{8,9},{9,8},{10,11... | collective-permute-start | bytes 835592 | tf_op jit(solution)/shard_map/ppermute | solution.py:15
  27.9 15.9 %collective-permute-start.6 = (bf16[64,2176]{1,0:T(8,128)(2,1)S(1)}, bf16[64,2176]{1,0:T(8,128)(2,1)S(1)}, u32[]{:S(2)}, u32[]{:S(2)}) collective-permute-start(bf16[64,2176]{1,0:T(8,128)(2,1)S(1)} %gather.1.refs_0_.refs_4_), channel_id=1, source_target_pairs={{0,8},{1,9},{2,10},{3,11},{4,12},{5,13},{6,14},{7,15},{8,0},{9,1},... | collective-permute-start | bytes 835592 | tf_op jit(solution)/shard_map/ppermute | solution.py:15
  30.8 15.2 %collective-permute-start.5 = (bf16[64,2304]{1,0:T(8,128)(2,1)S(1)}, bf16[64,2304]{1,0:T(8,128)(2,1)S(1)}, u32[]{:S(2)}, u32[]{:S(2)}) collective-permute-start(bf16[64,2304]{1,0:T(8,128)(2,1)S(1)} %get-tuple-element.85.own_ref), channel_id=1, source_target_pairs={{0,16},{1,17},{2,18},{3,19},{4,20},{5,21},{6,22},{7,23},{8,24},{9,... | collective-permute-start | bytes 884744 | tf_op jit(solution)/shard_map/ppermute | solution.py:21
  35.2 12.2 %collective-permute-start.10 = (bf16[64,2304]{1,0:T(8,128)(2,1)S(1)}, bf16[64,2304]{1,0:T(8,128)(2,1)S(1)}, u32[]{:S(2)}, u32[]{:S(2)}) collective-permute-start(bf16[64,2304]{1,0:T(8,128)(2,1)S(1)} %get-tuple-element.94.own_ref), channel_id=1, source_target_pairs={{0,16},{1,17},{2,18},{3,19},{4,20},{5,21},{6,22},{7,23},{8,24},{9,... | collective-permute-start | bytes 884744 | tf_op jit(solution)/shard_map/ppermute | solution.py:21
  43.9 4.9 %collective-permute-start.12 = (bf16[64,2176]{1,0:T(8,128)(2,1)S(1)}, bf16[64,2176]{1,0:T(8,128)(2,1)S(1)}, u32[]{:S(2)}, u32[]{:S(2)}) collective-permute-start(bf16[64,2176]{1,0:T(8,128)(2,1)S(1)} %collective-permute-done.6.refs_0_), channel_id=1, source_target_pairs={{0,1},{1,0},{2,3},{3,2},{4,5},{5,4},{6,7},{7,6},{8,9},{9,8},{10,11... | collective-permute-start | bytes 835592 | tf_op jit(solution)/shard_map/ppermute | solution.py:15
  43.9 8.0 %collective-permute-start.17 = (bf16[64,2176]{1,0:T(8,128)(2,1)S(1)}, bf16[64,2176]{1,0:T(8,128)(2,1)S(1)}, u32[]{:S(2)}, u32[]{:S(2)}) collective-permute-start(bf16[64,2176]{1,0:T(8,128)(2,1)S(1)} %collective-permute-done.4.refs_0_), channel_id=1, source_target_pairs={{0,1},{1,0},{2,3},{3,2},{4,5},{5,4},{6,7},{7,6},{8,9},{9,8},{10,11... | collective-permute-start | bytes 835592 | tf_op jit(solution)/shard_map/ppermute | solution.py:15
  45.5 10.7 %collective-permute-start.16 = (bf16[64,2304]{1,0:T(8,128)(2,1)S(1)}, bf16[64,2304]{1,0:T(8,128)(2,1)S(1)}, u32[]{:S(2)}, u32[]{:S(2)}) collective-permute-start(bf16[64,2304]{1,0:T(8,128)(2,1)S(1)} %get-tuple-element.98.own_ref), channel_id=1, source_target_pairs={{0,16},{1,17},{2,18},{3,19},{4,20},{5,21},{6,22},{7,23},{8,24},{9,... | collective-permute-start | bytes 884744 | tf_op jit(solution)/shard_map/ppermute | solution.py:21
  48.7 3.1 %collective-permute-start.11 = (bf16[64,2048]{1,0:T(8,128)(2,1)S(1)}, bf16[64,2048]{1,0:T(8,128)(2,1)S(1)}, u32[]{:S(2)}, u32[]{:S(2)}) collective-permute-start(bf16[64,2048]{1,0:T(8,128)(2,1)S(1)} %get-tuple-element.95.refs_4_), channel_id=1, source_target_pairs={{0,1},{1,0},{2,3},{3,2},{4,5},{5,4},{6,7},{7,6},{8,9},{9,8},{10,11... | collective-permute-start | bytes 786440 | tf_op jit(solution)/shard_map/ppermute | solution.py:15
  49.9 11.9 %collective-permute-start.15 = (bf16[64,2304]{1,0:T(8,128)(2,1)S(1)}, bf16[64,2304]{1,0:T(8,128)(2,1)S(1)}, u32[]{:S(2)}, u32[]{:S(2)}) collective-permute-start(bf16[64,2304]{1,0:T(8,128)(2,1)S(1)} %get-tuple-element.97.own_ref), channel_id=1, source_target_pairs={{0,16},{1,17},{2,18},{3,19},{4,20},{5,21},{6,22},{7,23},{8,24},{9,... | collective-permute-start | bytes 884744 | tf_op jit(solution)/shard_map/ppermute | solution.py:21
  51.6 11.6 %collective-permute-start.14 = (bf16[64,2176]{1,0:T(8,128)(2,1)S(1)}, bf16[64,2176]{1,0:T(8,128)(2,1)S(1)}, u32[]{:S(2)}, u32[]{:S(2)}) collective-permute-start(bf16[64,2176]{1,0:T(8,128)(2,1)S(1)} %gather.1.refs_0_.refs_4_), channel_id=1, source_target_pairs={{0,1},{1,0},{2,3},{3,2},{4,5},{5,4},{6,7},{7,6},{8,9},{9,8},{10,11... | collective-permute-start | bytes 835592 | tf_op jit(solution)/shard_map/ppermute | solution.py:15
  53.0 14.1 %collective-permute-start.20 = (bf16[64,2304]{1,0:T(8,128)(2,1)S(1)}, bf16[64,2304]{1,0:T(8,128)(2,1)S(1)}, u32[]{:S(2)}, u32[]{:S(2)}) collective-permute-start(bf16[64,2304]{1,0:T(8,128)(2,1)S(1)} %get-tuple-element.125.own_ref), channel_id=1, source_target_pairs={{0,16},{1,17},{2,18},{3,19},{4,20},{5,21},{6,22},{7,23},{8,24},{9,... | collective-permute-start | bytes 884744 | tf_op jit(solution)/shard_map/ppermute | solution.py:21
  53.5 10.9 %collective-permute-start.13 = (bf16[64,2048]{1,0:T(8,128)(2,1)S(1)}, bf16[64,2048]{1,0:T(8,128)(2,1)S(1)}, u32[]{:S(2)}, u32[]{:S(2)}) collective-permute-start(bf16[64,2048]{1,0:T(8,128)(2,1)S(1)} %merge.7.refs_4_), channel_id=1, source_target_pairs={{0,12},{1,13},{2,14},{3,15},{4,8},{5,9},{6,10},{7,11},{8,4},{9,5},... | collective-permute-start | bytes 786440 | tf_op jit(solution)/shard_map/ppermute | solution.py:15
  63.1 1.6 %collective-permute-start.18 = (bf16[64,2048]{1,0:T(8,128)(2,1)S(1)}, bf16[64,2048]{1,0:T(8,128)(2,1)S(1)}, u32[]{:S(2)}, u32[]{:S(2)}) collective-permute-start(bf16[64,2048]{1,0:T(8,128)(2,1)S(1)} %get-tuple-element.101.refs_4_), channel_id=1, source_target_pairs={{0,1},{1,0},{2,3},{3,2},{4,5},{5,4},{6,7},{7,6},{8,9},{9,8},{10,11... | collective-permute-start | bytes 786440 | tf_op jit(solution)/shard_map/ppermute | solution.py:15
  64.3 9.5 %collective-permute-start.21 = (bf16[64,2304]{1,0:T(8,128)(2,1)S(1)}, bf16[64,2304]{1,0:T(8,128)(2,1)S(1)}, u32[]{:S(2)}, u32[]{:S(2)}) collective-permute-start(bf16[64,2304]{1,0:T(8,128)(2,1)S(1)} %get-tuple-element.127.own_ref), channel_id=1, source_target_pairs={{0,16},{1,17},{2,18},{3,19},{4,20},{5,21},{6,22},{7,23},{8,24},{9,... | collective-permute-start | bytes 884744 | tf_op jit(solution)/shard_map/ppermute | solution.py:21
  68.7 1.8 %collective-permute-start.22 = (bf16[64,2048]{1,0:T(8,128)(2,1)S(1)}, bf16[64,2048]{1,0:T(8,128)(2,1)S(1)}, u32[]{:S(2)}, u32[]{:S(2)}) collective-permute-start(bf16[64,2048]{1,0:T(8,128)(2,1)S(1)} %get-tuple-element.128.refs_2_), channel_id=1, source_target_pairs={{0,1},{1,0},{2,3},{3,2},{4,5},{5,4},{6,7},{7,6},{8,9},{9,8},{10,11... | collective-permute-start | bytes 786440 | tf_op jit(solution)/shard_map/ppermute | solution.py:15
  68.7 15.2 %collective-permute-start.19 = (bf16[64,2048]{1,0:T(8,128)(2,1)S(1)}, bf16[64,2048]{1,0:T(8,128)(2,1)S(1)}, u32[]{:S(2)}, u32[]{:S(2)}) collective-permute-start(bf16[64,2048]{1,0:T(8,128)(2,1)S(1)} %merge.9.refs_3_), channel_id=1, source_target_pairs={{0,8},{1,9},{2,10},{3,11},{4,12},{5,13},{6,14},{7,15},{8,0},{9,1},... | collective-permute-start | bytes 786440 | tf_op jit(solution)/shard_map/ppermute | solution.py:15
  70.5 13.6 %collective-permute-start.23 = (bf16[64,2048]{1,0:T(8,128)(2,1)S(1)}, bf16[64,2048]{1,0:T(8,128)(2,1)S(1)}, u32[]{:S(2)}, u32[]{:S(2)}) collective-permute-start(bf16[64,2048]{1,0:T(8,128)(2,1)S(1)} %merge.10.refs_3_), channel_id=1, source_target_pairs={{0,4},{1,5},{2,6},{3,7},{4,0},{5,1},{6,2},{7,3},{8,12},{9,13},{10,... | collective-permute-start | bytes 786440 | tf_op jit(solution)/shard_map/ppermute | solution.py:15
  75.2 9.0 %collective-permute-start.24 = (bf16[64,2048]{1,0:T(8,128)(2,1)S(1)}, bf16[64,2048]{1,0:T(8,128)(2,1)S(1)}, u32[]{:S(2)}, u32[]{:S(2)}) collective-permute-start(bf16[64,2048]{1,0:T(8,128)(2,1)S(1)} %get-tuple-element.146.refs_40_), channel_id=1, source_target_pairs={{0,1},{1,0},{2,3},{3,2},{4,5},{5,4},{6,7},{7,6},{8,9},{9,8},{10,11... | collective-permute-start | bytes 786440 | tf_op jit(solution)/shard_map/ppermute | solution.py:15
  84.2 4.3 %collective-permute-start.25 = (bf16[16,2048]{1,0:T(8,128)(2,1)S(1)}, bf16[16,2048]{1,0:T(8,128)(2,1)S(1)}, u32[]{:S(2)}, u32[]{:S(2)}) collective-permute-start(bf16[16,2048]{1,0:T(8,128)(2,1)S(1)} %get-tuple-element.149), channel_id=1, source_target_pairs={{0,2},{1,3},{2,0},{3,1},{4,6},{5,7},{6,4},{7,5},{8,10},{9,11},{10,... | collective-permute-start | bytes 196616 | tf_op jit(solution)/shard_map/ppermute | solution.py:15
  85.8 4.3 %collective-permute-start.26 = (bf16[16,2048]{1,0:T(8,128)(2,1)S(1)}, bf16[16,2048]{1,0:T(8,128)(2,1)S(1)}, u32[]{:S(2)}, u32[]{:S(2)}) collective-permute-start(bf16[16,2048]{1,0:T(8,128)(2,1)S(1)} %get-tuple-element.150), channel_id=1, source_target_pairs={{0,16},{1,17},{2,18},{3,19},{4,20},{5,21},{6,22},{7,23},{8,24},{9,... | collective-permute-start | bytes 196616 | tf_op jit(solution)/shard_map/ppermute | solution.py:21
  86.5 5.2 %collective-permute-start.27 = (bf16[16,2048]{1,0:T(8,128)(2,1)S(1)}, bf16[16,2048]{1,0:T(8,128)(2,1)S(1)}, u32[]{:S(2)}, u32[]{:S(2)}) collective-permute-start(bf16[16,2048]{1,0:T(8,128)(2,1)S(1)} %get-tuple-element.151), channel_id=1, source_target_pairs={{0,18},{1,19},{2,16},{3,17},{4,22},{5,23},{6,20},{7,21},{8,26},{9,... | collective-permute-start | bytes 196616 | tf_op jit(solution)/shard_map/ppermute | solution.py:21

commit v3 on v2

--- a/solution.py
+++ b/solution.py
@@ -336,11 +336,8 @@
     send_sum(1)
     act(0, 1)
     grad_gate, grad_up, grad_down = run_grads()
-    for z in [*far[-1:], 1]:
-        collect(z)
-    pieces = merge(
-        [[piece] for piece in (*total, keeps[0], received[0])], [rows] * 4
-    )
+    last_terms = (*total, keeps[0], received[0], *(arrivals[z] for z in [*far[-1:], 1]))
+    pieces = merge([[piece] for piece in last_terms], [rows] * 4)
     moved = [swap(pieces[i], i % 2, 2 * (i // 2)) if i else pieces[i] for i in range(4)]
     layer_out, d_tokens = pl.pallas_call(
         functools.partial(finish_kernel, 2),

time: 92.5 us -> 92.4 us (level)
  no operation moved by 1% of the time
where the time goes in v3:
time: 92.4 us; the launch traced here: 92.2 us
  waiting for transfers between devices  35.1 us (38%)
  starting transfers between devices  28.1 us (30%)
  Pallas kernels  27.3 us (30%)
    ppermute x16, waiting for transfers between devices, swap(): return lax.ppermute(value, 'expert', pairs)  21.1 us
    ppermute x16, starting transfers between devices, swap(): return lax.ppermute(value, 'expert', pairs)  17.6 us
    ppermute x12, waiting for transfers between devices, swap(): return lax.ppermute(value, ('dp', 'expert'), pairs)  14 us
    pallas_call x8, Pallas kernels, expert(): pl.pallas_call(functools.partial(expert_kernel, rows, len(last), parts, f...  10.9 us
    ppermute x12, starting transfers between devices, swap(): return lax.ppermute(value, ('dp', 'expert'), pairs)  10.6 us
    pallas_call x8, Pallas kernels, partials(): pl.pallas_call(functools.partial(partial_kernel, len(pieces), len(sizes),...  9.14 us
    pallas_call x1, Pallas kernels, run_grads(): pl.pallas_call(functools.partial(grad_kernel, [len(group) for group in gr...  4.43 us
  transfers between devices with their start and end apart: 28, of which 13 were waited for; matrix products, arithmetic and copies ran while one was open for 0% of the time, Pallas kernels for 27%

profile of v3, /device:TPU:0, one launch (start us, length us, event | category | flops | bytes accessed | tf_op | source)
XLA Modules:
  0.0 92.2 jit_solution(15846789381415962048)
XLA Ops:
  0.6 1.8 %prepare.1 = (bf16[16,2176]{1,0:T(8,128)(2,1)}, bf16[16,2176]{1,0:T(8,128)(2,1)}) custom-call(bf16[16,2048]{1,0:T(8,128)(2,1)} %tokens_ref.1, s32[8,16]{1,0:T(8,128)} %bitcast.2, f32[8,16]{1,0:T(8,128)} %bitcast.3, bf16[16,2048]{1,0:T(8,128)(2,1)} %cotangent_ref.1), custom_call_target="tpu_custom_call" | custom-call | flops 10000000000 | bytes 1000 | tf_op jit(solution)/shard_map/prepare/pallas_call | solution.py:194
  2.4 3.0 %collective-permute-start.1 = (bf16[16,2176]{1,0:T(8,128)(2,1)}, bf16[16,2176]{1,0:T(8,128)(2,1)S(1)}, u32[]{:S(2)}, u32[]{:S(2)}) collective-permute-start(bf16[16,2176]{1,0:T(8,128)(2,1)} %get-tuple-element.81.refs_0_), channel_id=1, source_target_pairs={{0,2},{1,3},{2,0},{3,1},{4,6},{5,7},{6,4},{7,5},{8,10},{9,11},{10,... | collective-permute-start | bytes 208904 | tf_op jit(solution)/shard_map/ppermute | solution.py:15
  5.4 1.4 %collective-permute-start.2 = (bf16[16,2176]{1,0:T(8,128)(2,1)}, bf16[16,2176]{1,0:T(8,128)(2,1)S(1)}, u32[]{:S(2)}, u32[]{:S(2)}) collective-permute-start(bf16[16,2176]{1,0:T(8,128)(2,1)} %get-tuple-element.82), channel_id=1, source_target_pairs={{0,18},{1,19},{2,16},{3,17},{4,22},{5,23},{6,20},{7,21},{8,26},{9,... | collective-permute-start | bytes 208904 | tf_op jit(solution)/shard_map/ppermute | solution.py:21
  6.8 0.1 collective-permute-start
  6.9 1.6 %collective-permute-done.1.refs_2_ = bf16[16,2176]{1,0:T(8,128)(2,1)S(1)} collective-permute-done((bf16[16,2176]{1,0:T(8,128)(2,1)}, bf16[16,2176]{1,0:T(8,128)(2,1)S(1)}, u32[]{:S(2)}, u32[]{:S(2)}) %collective-permute-start.1) | collective-permute-done | bytes 69664 | tf_op jit(solution)/shard_map/ppermute | solution.py:15
  8.5 2.8 %collective-permute-done.2.refs_3_ = bf16[16,2176]{1,0:T(8,128)(2,1)S(1)} collective-permute-done((bf16[16,2176]{1,0:T(8,128)(2,1)}, bf16[16,2176]{1,0:T(8,128)(2,1)S(1)}, u32[]{:S(2)}, u32[]{:S(2)}) %collective-permute-start.2) | collective-permute-done | bytes 69664 | tf_op jit(solution)/shard_map/ppermute | solution.py:21
  11.3 0.9 copy-done.3
  12.2 1.6 %collective-permute-start.4 = (bf16[64,2176]{1,0:T(8,128)(2,1)S(1)}, bf16[64,2176]{1,0:T(8,128)(2,1)S(1)}, u32[]{:S(2)}, u32[]{:S(2)}) collective-permute-start(bf16[64,2176]{1,0:T(8,128)(2,1)S(1)} %gather.1.refs_0_.refs_4_), channel_id=1, source_target_pairs={{0,4},{1,5},{2,6},{3,7},{4,0},{5,1},{6,2},{7,3},{8,12},{9,13},{10,... | collective-permute-start | bytes 835592 | tf_op jit(solution)/shard_map/ppermute | solution.py:15
  13.9 2.5 %collective-permute-start.3 = (bf16[64,2176]{1,0:T(8,128)(2,1)S(1)}, bf16[64,2176]{1,0:T(8,128)(2,1)S(1)}, u32[]{:S(2)}, u32[]{:S(2)}) collective-permute-start(bf16[64,2176]{1,0:T(8,128)(2,1)S(1)} %gather.1.refs_0_.refs_4_), channel_id=1, source_target_pairs={{0,12},{1,13},{2,14},{3,15},{4,8},{5,9},{6,10},{7,11},{8,4},{9,5},... | collective-permute-start | bytes 835592 | tf_op jit(solution)/shard_map/ppermute | solution.py:15
  16.4 1.1 %partials.8 = (bf16[64,2304]{1,0:T(8,128)(2,1)S(1)}, f32[64,128]{1,0:T(8,128)S(1)}, bf16[64,1024]{1,0:T(8,128)(2,1)S(1)}, bf16[64,1024]{1,0:T(8,128)(2,1)S(1)}) custom-call(bf16[64,2176]{1,0:T(8,128)(2,1)S(1)} %gather.1.refs_0_.refs_4_, bf16[1,1024,768]{2,1,0:T(8,128)(2,1)S(1)} %copy-done, bf16[1,1024,768]{2,1,0:T(8,128)(2,1)S(1)} %copy-done.1, ...), custom_call_target="tpu_custom_call" | custom-call | flops 1000 | bytes 1000 | tf_op jit(solution)/shard_map/partials/pallas_call | solution.py:210
  17.5 1.1 %collective-permute-start.9 = (bf16[64,2304]{1,0:T(8,128)(2,1)S(1)}, bf16[64,2304]{1,0:T(8,128)(2,1)S(1)}, u32[]{:S(2)}, u32[]{:S(2)}) collective-permute-start(bf16[64,2304]{1,0:T(8,128)(2,1)S(1)} %get-tuple-element.88.own_ref), channel_id=1, source_target_pairs={{0,16},{1,17},{2,18},{3,19},{4,20},{5,21},{6,22},{7,23},{8,24},{9,... | collective-permute-start | bytes 884744 | tf_op jit(solution)/shard_map/ppermute | solution.py:21
  18.6 2.4 %collective-permute-done.4.refs_0_ = bf16[64,2176]{1,0:T(8,128)(2,1)S(1)} collective-permute-done((bf16[64,2176]{1,0:T(8,128)(2,1)S(1)}, bf16[64,2176]{1,0:T(8,128)(2,1)S(1)}, u32[]{:S(2)}, u32[]{:S(2)}) %collective-permute-start.4) | collective-permute-done | bytes 278560 | tf_op jit(solution)/shard_map/ppermute | solution.py:15
  21.0 1.1 %partials.9 = (bf16[64,2304]{1,0:T(8,128)(2,1)S(1)}, f32[64,128]{1,0:T(8,128)S(1)}, bf16[64,1024]{1,0:T(8,128)(2,1)S(1)}, bf16[64,1024]{1,0:T(8,128)(2,1)S(1)}) custom-call(bf16[64,2176]{1,0:T(8,128)(2,1)S(1)} %collective-permute-done.4.refs_0_, bf16[1,1024,768]{2,1,0:T(8,128)(2,1)S(1)} %copy-done, bf16[1,1024,768]{2,1,0:T(8,128)(2,1)S(1)} %copy-done.1, ...), custom_call_target="tpu_custom_call" | custom-call | flops 1000 | bytes 1000 | tf_op jit(solution)/shard_map/partials/pallas_call | solution.py:210
  22.1 1.1 %collective-permute-start.8 = (bf16[64,2304]{1,0:T(8,128)(2,1)S(1)}, bf16[64,2304]{1,0:T(8,128)(2,1)S(1)}, u32[]{:S(2)}, u32[]{:S(2)}) collective-permute-start(bf16[64,2304]{1,0:T(8,128)(2,1)S(1)} %get-tuple-element.87.own_ref), channel_id=1, source_target_pairs={{0,16},{1,17},{2,18},{3,19},{4,20},{5,21},{6,22},{7,23},{8,24},{9,... | collective-permute-start | bytes 884744 | tf_op jit(solution)/shard_map/ppermute | solution.py:21
  23.2 4.7 %collective-permute-done.3.refs_0_ = bf16[64,2176]{1,0:T(8,128)(2,1)S(1)} collective-permute-done((bf16[64,2176]{1,0:T(8,128)(2,1)S(1)}, bf16[64,2176]{1,0:T(8,128)(2,1)S(1)}, u32[]{:S(2)}, u32[]{:S(2)}) %collective-permute-start.3) | collective-permute-done | bytes 278560 | tf_op jit(solution)/shard_map/ppermute | solution.py:15
  27.9 1.8 %collective-permute-start.6 = (bf16[64,2176]{1,0:T(8,128)(2,1)S(1)}, bf16[64,2176]{1,0:T(8,128)(2,1)S(1)}, u32[]{:S(2)}, u32[]{:S(2)}) collective-permute-start(bf16[64,2176]{1,0:T(8,128)(2,1)S(1)} %gather.1.refs_0_.refs_4_), channel_id=1, source_target_pairs={{0,8},{1,9},{2,10},{3,11},{4,12},{5,13},{6,14},{7,15},{8,0},{9,1},... | collective-permute-start | bytes 835592 | tf_op jit(solution)/shard_map/ppermute | solution.py:15
  29.7 1.1 %partials.10 = (bf16[64,2304]{1,0:T(8,128)(2,1)S(1)}, f32[64,128]{1,0:T(8,128)S(1)}, bf16[64,1024]{1,0:T(8,128)(2,1)S(1)}, bf16[64,1024]{1,0:T(8,128)(2,1)S(1)}) custom-call(bf16[64,2176]{1,0:T(8,128)(2,1)S(1)} %collective-permute-done.3.refs_0_, bf16[1,1024,768]{2,1,0:T(8,128)(2,1)S(1)} %copy-done, bf16[1,1024,768]{2,1,0:T(8,128)(2,1)S(1)} %copy-done.1, ...), custom_call_target="tpu_custom_call" | custom-call | flops 1000 | bytes 1000 | tf_op jit(solution)/shard_map/partials/pallas_call | solution.py:210
  30.8 0.5 collective-permute-start.5
  31.3 0.0 collective-permute-done.9.their_ref
  31.3 1.3 %expert.8 = (bf16[64,2048]{1,0:T(8,128)(2,1)S(1)}, bf16[64,768]{1,0:T(8,128)(2,1)S(1)}, bf16[64,768]{1,0:T(8,128)(2,1)S(1)}, bf16[64,768]{1,0:T(8,128)(2,1)S(1)}) custom-call(bf16[64,2304]{1,0:T(8,128)(2,1)S(1)} %get-tuple-element.88.own_ref, bf16[64,2304]{1,0:T(8,128)(2,1)S(1)} %collective-permute-done.9.their_ref, ...), custom_call_target="tpu_custom_call" | custom-call | flops 1000 | bytes 1000 | tf_op jit(solution)/shard_map/expert/pallas_call | solution.py:226
  32.6 1.3 %expert.9 = (bf16[64,2048]{1,0:T(8,128)(2,1)S(1)}, bf16[64,768]{1,0:T(8,128)(2,1)S(1)}, bf16[64,768]{1,0:T(8,128)(2,1)S(1)}, bf16[64,768]{1,0:T(8,128)(2,1)S(1)}) custom-call(bf16[64,2304]{1,0:T(8,128)(2,1)S(1)} %get-tuple-element.87.own_ref, bf16[64,2304]{1,0:T(8,128)(2,1)S(1)} %collective-permute-done.8.their_ref, ...), custom_call_target="tpu_custom_call" | custom-call | flops 1000 | bytes 1000 | tf_op jit(solution)/shard_map/expert/pallas_call | solution.py:226
  34.0 1.1 %partials.11 = (bf16[64,2304]{1,0:T(8,128)(2,1)S(1)}, f32[64,128]{1,0:T(8,128)S(1)}, bf16[64,1024]{1,0:T(8,128)(2,1)S(1)}, bf16[64,1024]{1,0:T(8,128)(2,1)S(1)}) custom-call(bf16[64,2176]{1,0:T(8,128)(2,1)S(1)} %collective-permute-done.7.refs_0_, bf16[1,1024,768]{2,1,0:T(8,128)(2,1)S(1)} %copy-done, bf16[1,1024,768]{2,1,0:T(8,128)(2,1)S(1)} %copy-done.1, ...), custom_call_target="tpu_custom_call" | custom-call | flops 1000 | bytes 1000 | tf_op jit(solution)/shard_map/partials/pallas_call | solution.py:210
  35.2 1.7 %collective-permute-start.10 = (bf16[64,2304]{1,0:T(8,128)(2,1)S(1)}, bf16[64,2304]{1,0:T(8,128)(2,1)S(1)}, u32[]{:S(2)}, u32[]{:S(2)}) collective-permute-start(bf16[64,2304]{1,0:T(8,128)(2,1)S(1)} %get-tuple-element.94.own_ref), channel_id=1, source_target_pairs={{0,16},{1,17},{2,18},{3,19},{4,20},{5,21},{6,22},{7,23},{8,24},{9,... | collective-permute-start | bytes 884744 | tf_op jit(solution)/shard_map/ppermute | solution.py:21
  36.8 7.0 %collective-permute-done.6.refs_0_ = bf16[64,2176]{1,0:T(8,128)(2,1)S(1)} collective-permute-done((bf16[64,2176]{1,0:T(8,128)(2,1)S(1)}, bf16[64,2176]{1,0:T(8,128)(2,1)S(1)}, u32[]{:S(2)}, u32[]{:S(2)}) %collective-permute-start.6) | collective-permute-done | bytes 278560 | tf_op jit(solution)/shard_map/ppermute | solution.py:15
  43.9 0.5 collective-permute-start.17
  44.4 1.1 %partials.12 = (bf16[64,2304]{1,0:T(8,128)(2,1)S(1)}, f32[64,128]{1,0:T(8,128)S(1)}, bf16[64,1024]{1,0:T(8,128)(2,1)S(1)}, bf16[64,1024]{1,0:T(8,128)(2,1)S(1)}) custom-call(bf16[64,2176]{1,0:T(8,128)(2,1)S(1)} %collective-permute-done.6.refs_0_, bf16[1,1024,768]{2,1,0:T(8,128)(2,1)S(1)} %copy-done, bf16[1,1024,768]{2,1,0:T(8,128)(2,1)S(1)} %copy-done.1, ...), custom_call_target="tpu_custom_call" | custom-call | flops 1000 | bytes 1000 | tf_op jit(solution)/shard_map/partials/pallas_call | solution.py:210
  45.5 0.5 collective-permute-start.16
  46.0 1.3 %expert.10 = (bf16[64,2048]{1,0:T(8,128)(2,1)S(1)}, bf16[64,768]{1,0:T(8,128)(2,1)S(1)}, bf16[64,768]{1,0:T(8,128)(2,1)S(1)}, bf16[64,768]{1,0:T(8,128)(2,1)S(1)}) custom-call(bf16[64,2304]{1,0:T(8,128)(2,1)S(1)} %get-tuple-element.85.own_ref, bf16[64,2304]{1,0:T(8,128)(2,1)S(1)} %collective-permute-done.5.their_ref, ...), custom_call_target="tpu_custom_call" | custom-call | flops 1000 | bytes 1000 | tf_op jit(solution)/shard_map/expert/pallas_call | solution.py:226
  47.3 1.3 %expert.11 = (bf16[64,2048]{1,0:T(8,128)(2,1)S(1)}, bf16[64,768]{1,0:T(8,128)(2,1)S(1)}, bf16[64,768]{1,0:T(8,128)(2,1)S(1)}, bf16[64,768]{1,0:T(8,128)(2,1)S(1)}) custom-call(bf16[64,2304]{1,0:T(8,128)(2,1)S(1)} %get-tuple-element.94.own_ref, bf16[64,2304]{1,0:T(8,128)(2,1)S(1)} %collective-permute-done.10.their_ref, ...), custom_call_target="tpu_custom_call" | custom-call | flops 1000 | bytes 1000 | tf_op jit(solution)/shard_map/expert/pallas_call | solution.py:226
  48.7 0.1 collective-permute-start.11
  48.8 1.1 %partials.13 = (bf16[64,2304]{1,0:T(8,128)(2,1)S(1)}, f32[64,128]{1,0:T(8,128)S(1)}, bf16[64,1024]{1,0:T(8,128)(2,1)S(1)}, bf16[64,1024]{1,0:T(8,128)(2,1)S(1)}) custom-call(bf16[64,2176]{1,0:T(8,128)(2,1)S(1)} %collective-permute-done.12.refs_0_, bf16[1,1024,768]{2,1,0:T(8,128)(2,1)S(1)} %copy-done, bf16[1,1024,768]{2,1,0:T(8,128)(2,1)S(1)} %copy-done.1, ...), custom_call_target="tpu_custom_call" | custom-call | flops 1000 | bytes 1000 | tf_op jit(solution)/shard_map/partials/pallas_call | solution.py:210
  49.9 1.7 %collective-permute-start.15 = (bf16[64,2304]{1,0:T(8,128)(2,1)S(1)}, bf16[64,2304]{1,0:T(8,128)(2,1)S(1)}, u32[]{:S(2)}, u32[]{:S(2)}) collective-permute-start(bf16[64,2304]{1,0:T(8,128)(2,1)S(1)} %get-tuple-element.97.own_ref), channel_id=1, source_target_pairs={{0,16},{1,17},{2,18},{3,19},{4,20},{5,21},{6,22},{7,23},{8,24},{9,... | collective-permute-start | bytes 884744 | tf_op jit(solution)/shard_map/ppermute | solution.py:21
  51.6 0.2 collective-permute-start.14
  51.8 0.1 merge.5.refs_4_
  51.9 1.1 %partials.14 = (bf16[64,2304]{1,0:T(8,128)(2,1)S(1)}, f32[64,128]{1,0:T(8,128)S(1)}, bf16[64,1024]{1,0:T(8,128)(2,1)S(1)}, bf16[64,1024]{1,0:T(8,128)(2,1)S(1)}) custom-call(bf16[64,2176]{1,0:T(8,128)(2,1)S(1)} %collective-permute-done.17.refs_0_, bf16[1,1024,768]{2,1,0:T(8,128)(2,1)S(1)} %copy-done, bf16[1,1024,768]{2,1,0:T(8,128)(2,1)S(1)} %copy-done.1, ...), custom_call_target="tpu_custom_call" | custom-call | flops 1000 | bytes 1000 | tf_op jit(solution)/shard_map/partials/pallas_call | solution.py:210
  53.0 0.5 collective-permute-start.19
  53.5 2.7 %collective-permute-start.13 = (bf16[64,2048]{1,0:T(8,128)(2,1)S(1)}, bf16[64,2048]{1,0:T(8,128)(2,1)S(1)}, u32[]{:S(2)}, u32[]{:S(2)}) collective-permute-start(bf16[64,2048]{1,0:T(8,128)(2,1)S(1)} %merge.5.refs_4_), channel_id=1, source_target_pairs={{0,12},{1,13},{2,14},{3,15},{4,8},{5,9},{6,10},{7,11},{8,4},{9,5},... | collective-permute-start | bytes 786440 | tf_op jit(solution)/shard_map/ppermute | solution.py:15
  56.2 1.3 %expert.12 = (bf16[64,2048]{1,0:T(8,128)(2,1)S(1)}, bf16[64,768]{1,0:T(8,128)(2,1)S(1)}, bf16[64,768]{1,0:T(8,128)(2,1)S(1)}, bf16[64,768]{1,0:T(8,128)(2,1)S(1)}) custom-call(bf16[64,2304]{1,0:T(8,128)(2,1)S(1)} %get-tuple-element.98.own_ref, bf16[64,2304]{1,0:T(8,128)(2,1)S(1)} %collective-permute-done.16.their_ref, ...), custom_call_target="tpu_custom_call" | custom-call | flops 1000 | bytes 1000 | tf_op jit(solution)/shard_map/expert/pallas_call | solution.py:226
  57.5 4.3 %collective-permute-done.15.their_ref = bf16[64,2304]{1,0:T(8,128)(2,1)S(1)} collective-permute-done((bf16[64,2304]{1,0:T(8,128)(2,1)S(1)}, bf16[64,2304]{1,0:T(8,128)(2,1)S(1)}, u32[]{:S(2)}, u32[]{:S(2)}) %collective-permute-start.15) | collective-permute-done | bytes 294944 | tf_op jit(solution)/shard_map/ppermute | solution.py:21
  61.8 1.3 %expert.13 = (bf16[64,2048]{1,0:T(8,128)(2,1)S(1)}, bf16[64,768]{1,0:T(8,128)(2,1)S(1)}, bf16[64,768]{1,0:T(8,128)(2,1)S(1)}, bf16[64,768]{1,0:T(8,128)(2,1)S(1)}) custom-call(bf16[64,2304]{1,0:T(8,128)(2,1)S(1)} %get-tuple-element.97.own_ref, bf16[64,2304]{1,0:T(8,128)(2,1)S(1)} %collective-permute-done.15.their_ref, ...), custom_call_target="tpu_custom_call" | custom-call | flops 1000 | bytes 1000 | tf_op jit(solution)/shard_map/expert/pallas_call | solution.py:226
  63.1 0.1 collective-permute-start.20
  63.2 1.1 %partials.15 = (bf16[64,2304]{1,0:T(8,128)(2,1)S(1)}, f32[64,128]{1,0:T(8,128)S(1)}, bf16[64,1024]{1,0:T(8,128)(2,1)S(1)}, bf16[64,1024]{1,0:T(8,128)(2,1)S(1)}) custom-call(bf16[64,2176]{1,0:T(8,128)(2,1)S(1)} %collective-permute-done.14.refs_0_, bf16[1,1024,768]{2,1,0:T(8,128)(2,1)S(1)} %copy-done, bf16[1,1024,768]{2,1,0:T(8,128)(2,1)S(1)} %copy-done.1, ...), custom_call_target="tpu_custom_call" | custom-call | flops 1000 | bytes 1000 | tf_op jit(solution)/shard_map/partials/pallas_call | solution.py:210
  64.3 0.1 collective-permute-start.18
  64.5 0.3 collective-permute-done.20.refs_1_
  64.7 0.1 merge.7.refs_3_
  64.8 2.4 %collective-permute-done.19.their_ref = bf16[64,2304]{1,0:T(8,128)(2,1)S(1)} collective-permute-done((bf16[64,2304]{1,0:T(8,128)(2,1)S(1)}, bf16[64,2304]{1,0:T(8,128)(2,1)S(1)}, u32[]{:S(2)}, u32[]{:S(2)}) %collective-permute-start.19) | collective-permute-done | bytes 294944 | tf_op jit(solution)/shard_map/ppermute | solution.py:21
  67.1 1.5 %expert.14 = (bf16[64,2048]{1,0:T(8,128)(2,1)S(1)}, bf16[64,768]{1,0:T(8,128)(2,1)S(1)}, bf16[64,768]{1,0:T(8,128)(2,1)S(1)}, bf16[64,768]{1,0:T(8,128)(2,1)S(1)}) custom-call(bf16[64,2304]{1,0:T(8,128)(2,1)S(1)} %get-tuple-element.104.own_ref, bf16[64,2304]{1,0:T(8,128)(2,1)S(1)} %collective-permute-done.19.their_ref, ...), custom_call_target="tpu_custom_call" | custom-call | flops 1000 | bytes 1000 | tf_op jit(solution)/shard_map/expert/pallas_call | solution.py:226
  68.7 0.1 collective-permute-start.21
  68.7 1.7 %collective-permute-start.23 = (bf16[64,2048]{1,0:T(8,128)(2,1)S(1)}, bf16[64,2048]{1,0:T(8,128)(2,1)S(1)}, u32[]{:S(2)}, u32[]{:S(2)}) collective-permute-start(bf16[64,2048]{1,0:T(8,128)(2,1)S(1)} %merge.7.refs_3_), channel_id=1, source_target_pairs={{0,8},{1,9},{2,10},{3,11},{4,12},{5,13},{6,14},{7,15},{8,0},{9,1},... | collective-permute-start | bytes 786440 | tf_op jit(solution)/shard_map/ppermute | solution.py:15
  70.4 0.1 merge.8.refs_3_
  70.5 1.8 %collective-permute-start.24 = (bf16[64,2048]{1,0:T(8,128)(2,1)S(1)}, bf16[64,2048]{1,0:T(8,128)(2,1)S(1)}, u32[]{:S(2)}, u32[]{:S(2)}) collective-permute-start(bf16[64,2048]{1,0:T(8,128)(2,1)S(1)} %merge.8.refs_3_), channel_id=1, source_target_pairs={{0,4},{1,5},{2,6},{3,7},{4,0},{5,1},{6,2},{7,3},{8,12},{9,13},{10,... | collective-permute-start | bytes 786440 | tf_op jit(solution)/shard_map/ppermute | solution.py:15
  72.3 1.5 %collective-permute-done.18.their_ref = bf16[64,2304]{1,0:T(8,128)(2,1)S(1)} collective-permute-done((bf16[64,2304]{1,0:T(8,128)(2,1)S(1)}, bf16[64,2304]{1,0:T(8,128)(2,1)S(1)}, u32[]{:S(2)}, u32[]{:S(2)}) %collective-permute-start.18) | collective-permute-done | bytes 294944 | tf_op jit(solution)/shard_map/ppermute | solution.py:21
  73.8 1.3 %expert.15 = (bf16[64,2048]{1,0:T(8,128)(2,1)S(1)}, bf16[64,768]{1,0:T(8,128)(2,1)S(1)}, bf16[64,768]{1,0:T(8,128)(2,1)S(1)}, bf16[64,768]{1,0:T(8,128)(2,1)S(1)}) custom-call(bf16[64,2304]{1,0:T(8,128)(2,1)S(1)} %get-tuple-element.103.own_ref, bf16[64,2304]{1,0:T(8,128)(2,1)S(1)} %collective-permute-done.18.their_ref, ...), custom_call_target="tpu_custom_call" | custom-call | flops 1000 | bytes 1000 | tf_op jit(solution)/shard_map/expert/pallas_call | solution.py:226
  75.2 0.1 collective-permute-start.22
  75.2 4.4 %grads.1 = (bf16[1,1024,768]{2,1,0:T(8,128)(2,1)}, bf16[1,1024,768]{2,1,0:T(8,128)(2,1)}, bf16[1,768,1024]{2,1,0:T(8,128)(2,1)}, f32[8,128]{1,0:T(8,128)S(1)}) custom-call(bf16[64,1024]{1,0:T(8,128)(2,1)S(1)} %get-tuple-element.107.refs_0_, bf16[64,1024]{1,0:T(8,128)(2,1)S(1)} %get-tuple-element.108.refs_1_, ...), custom_call_target="tpu_custom_call" | custom-call | flops 1000 | bytes 1000 | tf_op jit(solution)/shard_map/grads/pallas_call | solution.py:301
  79.7 4.3 %collective-permute-done.23.refs_3_ = bf16[64,2048]{1,0:T(8,128)(2,1)S(1)} collective-permute-done((bf16[64,2048]{1,0:T(8,128)(2,1)S(1)}, bf16[64,2048]{1,0:T(8,128)(2,1)S(1)}, u32[]{:S(2)}, u32[]{:S(2)}) %collective-permute-start.23) | collective-permute-done | bytes 262176 | tf_op jit(solution)/shard_map/ppermute | solution.py:15
  84.0 0.2 merge.9
  84.2 1.6 %collective-permute-start.25 = (bf16[16,2048]{1,0:T(8,128)(2,1)S(1)}, bf16[16,2048]{1,0:T(8,128)(2,1)S(1)}, u32[]{:S(2)}, u32[]{:S(2)}) collective-permute-start(bf16[16,2048]{1,0:T(8,128)(2,1)S(1)} %get-tuple-element.149), channel_id=1, source_target_pairs={{0,2},{1,3},{2,0},{3,1},{4,6},{5,7},{6,4},{7,5},{8,10},{9,11},{10,... | collective-permute-start | bytes 196616 | tf_op jit(solution)/shard_map/ppermute | solution.py:15
  85.7 0.6 collective-permute-start.26
  86.4 1.3 %collective-permute-start.27 = (bf16[16,2048]{1,0:T(8,128)(2,1)S(1)}, bf16[16,2048]{1,0:T(8,128)(2,1)S(1)}, u32[]{:S(2)}, u32[]{:S(2)}) collective-permute-start(bf16[16,2048]{1,0:T(8,128)(2,1)S(1)} %get-tuple-element.151), channel_id=1, source_target_pairs={{0,18},{1,19},{2,16},{3,17},{4,22},{5,23},{6,20},{7,21},{8,26},{9,... | collective-permute-start | bytes 196616 | tf_op jit(solution)/shard_map/ppermute | solution.py:21
  87.7 0.8 collective-permute-done.25.refs_1_
  88.5 1.5 %collective-permute-done.26.refs_2_ = bf16[16,2048]{1,0:T(8,128)(2,1)S(1)} collective-permute-done((bf16[16,2048]{1,0:T(8,128)(2,1)S(1)}, bf16[16,2048]{1,0:T(8,128)(2,1)S(1)}, u32[]{:S(2)}, u32[]{:S(2)}) %collective-permute-start.26) | collective-permute-done | bytes 65568 | tf_op jit(solution)/shard_map/ppermute | solution.py:21
  90.0 1.5 %collective-permute-done.27.refs_3_ = bf16[16,2048]{1,0:T(8,128)(2,1)S(1)} collective-permute-done((bf16[16,2048]{1,0:T(8,128)(2,1)S(1)}, bf16[16,2048]{1,0:T(8,128)(2,1)S(1)}, u32[]{:S(2)}, u32[]{:S(2)}) %collective-permute-start.27) | collective-permute-done | bytes 65568 | tf_op jit(solution)/shard_map/ppermute | solution.py:21
  91.5 0.7 finish.1
  (25 shorter events, 0.1 us)
Async XLA Ops:
  2.4 6.1 %collective-permute-start.1 = (bf16[16,2176]{1,0:T(8,128)(2,1)}, bf16[16,2176]{1,0:T(8,128)(2,1)S(1)}, u32[]{:S(2)}, u32[]{:S(2)}) collective-permute-start(bf16[16,2176]{1,0:T(8,128)(2,1)} %get-tuple-element.81.refs_0_), channel_id=1, source_target_pairs={{0,2},{1,3},{2,0},{3,1},{4,6},{5,7},{6,4},{7,5},{8,10},{9,11},{10,... | collective-permute-start | bytes 208904 | tf_op jit(solution)/shard_map/ppermute | solution.py:15
  5.4 11.0 %copy-start = (bf16[1,1024,768]{2,1,0:T(8,128)(2,1)S(1)}, bf16[1,1024,768]{2,1,0:T(8,128)(2,1)}, u32[]{:S(2)}) copy-start(bf16[1,1024,768]{2,1,0:T(8,128)(2,1)} %refs_0_.15) | copy-start | bytes 4718596
  5.4 11.0 %copy-start.1 = (bf16[1,1024,768]{2,1,0:T(8,128)(2,1)S(1)}, bf16[1,1024,768]{2,1,0:T(8,128)(2,1)}, u32[]{:S(2)}) copy-start(bf16[1,1024,768]{2,1,0:T(8,128)(2,1)} %refs_1_.31) | copy-start | bytes 4718596
  5.4 11.0 %copy-start.2 = (bf16[1,768,1024]{2,1,0:T(8,128)(2,1)S(1)}, bf16[1,768,1024]{2,1,0:T(8,128)(2,1)}, u32[]{:S(2)}) copy-start(bf16[1,768,1024]{2,1,0:T(8,128)(2,1)} %refs_2_.31) | copy-start | bytes 4718596
  5.4 6.0 %collective-permute-start.2 = (bf16[16,2176]{1,0:T(8,128)(2,1)}, bf16[16,2176]{1,0:T(8,128)(2,1)S(1)}, u32[]{:S(2)}, u32[]{:S(2)}) collective-permute-start(bf16[16,2176]{1,0:T(8,128)(2,1)} %get-tuple-element.82), channel_id=1, source_target_pairs={{0,18},{1,19},{2,16},{3,17},{4,22},{5,23},{6,20},{7,21},{8,26},{9,... | collective-permute-start | bytes 208904 | tf_op jit(solution)/shard_map/ppermute | solution.py:21
  6.8 4.5 %collective-permute-start = (bf16[16,2176]{1,0:T(8,128)(2,1)}, bf16[16,2176]{1,0:T(8,128)(2,1)S(1)}, u32[]{:S(2)}, u32[]{:S(2)}) collective-permute-start(bf16[16,2176]{1,0:T(8,128)(2,1)} %get-tuple-element.82), channel_id=1, source_target_pairs={{0,16},{1,17},{2,18},{3,19},{4,20},{5,21},{6,22},{7,23},{8,24},{9,... | collective-permute-start | bytes 208904 | tf_op jit(solution)/shard_map/ppermute | solution.py:21
  11.3 0.9 copy-start.3
  12.2 8.8 %collective-permute-start.4 = (bf16[64,2176]{1,0:T(8,128)(2,1)S(1)}, bf16[64,2176]{1,0:T(8,128)(2,1)S(1)}, u32[]{:S(2)}, u32[]{:S(2)}) collective-permute-start(bf16[64,2176]{1,0:T(8,128)(2,1)S(1)} %gather.1.refs_0_.refs_4_), channel_id=1, source_target_pairs={{0,4},{1,5},{2,6},{3,7},{4,0},{5,1},{6,2},{7,3},{8,12},{9,13},{10,... | collective-permute-start | bytes 835592 | tf_op jit(solution)/shard_map/ppermute | solution.py:15
  13.9 14.0 %collective-permute-start.3 = (bf16[64,2176]{1,0:T(8,128)(2,1)S(1)}, bf16[64,2176]{1,0:T(8,128)(2,1)S(1)}, u32[]{:S(2)}, u32[]{:S(2)}) collective-permute-start(bf16[64,2176]{1,0:T(8,128)(2,1)S(1)} %gather.1.refs_0_.refs_4_), channel_id=1, source_target_pairs={{0,12},{1,13},{2,14},{3,15},{4,8},{5,9},{6,10},{7,11},{8,4},{9,5},... | collective-permute-start | bytes 835592 | tf_op jit(solution)/shard_map/ppermute | solution.py:15
  17.5 13.8 %collective-permute-start.9 = (bf16[64,2304]{1,0:T(8,128)(2,1)S(1)}, bf16[64,2304]{1,0:T(8,128)(2,1)S(1)}, u32[]{:S(2)}, u32[]{:S(2)}) collective-permute-start(bf16[64,2304]{1,0:T(8,128)(2,1)S(1)} %get-tuple-element.88.own_ref), channel_id=1, source_target_pairs={{0,16},{1,17},{2,18},{3,19},{4,20},{5,21},{6,22},{7,23},{8,24},{9,... | collective-permute-start | bytes 884744 | tf_op jit(solution)/shard_map/ppermute | solution.py:21
  22.1 10.5 %collective-permute-start.8 = (bf16[64,2304]{1,0:T(8,128)(2,1)S(1)}, bf16[64,2304]{1,0:T(8,128)(2,1)S(1)}, u32[]{:S(2)}, u32[]{:S(2)}) collective-permute-start(bf16[64,2304]{1,0:T(8,128)(2,1)S(1)} %get-tuple-element.87.own_ref), channel_id=1, source_target_pairs={{0,16},{1,17},{2,18},{3,19},{4,20},{5,21},{6,22},{7,23},{8,24},{9,... | collective-permute-start | bytes 884744 | tf_op jit(solution)/shard_map/ppermute | solution.py:21
  27.9 6.1 %collective-permute-start.7 = (bf16[64,2176]{1,0:T(8,128)(2,1)S(1)}, bf16[64,2176]{1,0:T(8,128)(2,1)S(1)}, u32[]{:S(2)}, u32[]{:S(2)}) collective-permute-start(bf16[64,2176]{1,0:T(8,128)(2,1)S(1)} %collective-permute-done.3.refs_0_), channel_id=1, source_target_pairs={{0,1},{1,0},{2,3},{3,2},{4,5},{5,4},{6,7},{7,6},{8,9},{9,8},{10,11... | collective-permute-start | bytes 835592 | tf_op jit(solution)/shard_map/ppermute | solution.py:15
  27.9 15.9 %collective-permute-start.6 = (bf16[64,2176]{1,0:T(8,128)(2,1)S(1)}, bf16[64,2176]{1,0:T(8,128)(2,1)S(1)}, u32[]{:S(2)}, u32[]{:S(2)}) collective-permute-start(bf16[64,2176]{1,0:T(8,128)(2,1)S(1)} %gather.1.refs_0_.refs_4_), channel_id=1, source_target_pairs={{0,8},{1,9},{2,10},{3,11},{4,12},{5,13},{6,14},{7,15},{8,0},{9,1},... | collective-permute-start | bytes 835592 | tf_op jit(solution)/shard_map/ppermute | solution.py:15
  30.8 15.2 %collective-permute-start.5 = (bf16[64,2304]{1,0:T(8,128)(2,1)S(1)}, bf16[64,2304]{1,0:T(8,128)(2,1)S(1)}, u32[]{:S(2)}, u32[]{:S(2)}) collective-permute-start(bf16[64,2304]{1,0:T(8,128)(2,1)S(1)} %get-tuple-element.85.own_ref), channel_id=1, source_target_pairs={{0,16},{1,17},{2,18},{3,19},{4,20},{5,21},{6,22},{7,23},{8,24},{9,... | collective-permute-start | bytes 884744 | tf_op jit(solution)/shard_map/ppermute | solution.py:21
  35.2 12.2 %collective-permute-start.10 = (bf16[64,2304]{1,0:T(8,128)(2,1)S(1)}, bf16[64,2304]{1,0:T(8,128)(2,1)S(1)}, u32[]{:S(2)}, u32[]{:S(2)}) collective-permute-start(bf16[64,2304]{1,0:T(8,128)(2,1)S(1)} %get-tuple-element.94.own_ref), channel_id=1, source_target_pairs={{0,16},{1,17},{2,18},{3,19},{4,20},{5,21},{6,22},{7,23},{8,24},{9,... | collective-permute-start | bytes 884744 | tf_op jit(solution)/shard_map/ppermute | solution.py:21
  43.9 4.9 %collective-permute-start.12 = (bf16[64,2176]{1,0:T(8,128)(2,1)S(1)}, bf16[64,2176]{1,0:T(8,128)(2,1)S(1)}, u32[]{:S(2)}, u32[]{:S(2)}) collective-permute-start(bf16[64,2176]{1,0:T(8,128)(2,1)S(1)} %collective-permute-done.6.refs_0_), channel_id=1, source_target_pairs={{0,1},{1,0},{2,3},{3,2},{4,5},{5,4},{6,7},{7,6},{8,9},{9,8},{10,11... | collective-permute-start | bytes 835592 | tf_op jit(solution)/shard_map/ppermute | solution.py:15
  43.9 8.0 %collective-permute-start.17 = (bf16[64,2176]{1,0:T(8,128)(2,1)S(1)}, bf16[64,2176]{1,0:T(8,128)(2,1)S(1)}, u32[]{:S(2)}, u32[]{:S(2)}) collective-permute-start(bf16[64,2176]{1,0:T(8,128)(2,1)S(1)} %collective-permute-done.4.refs_0_), channel_id=1, source_target_pairs={{0,1},{1,0},{2,3},{3,2},{4,5},{5,4},{6,7},{7,6},{8,9},{9,8},{10,11... | collective-permute-start | bytes 835592 | tf_op jit(solution)/shard_map/ppermute | solution.py:15
  45.5 10.7 %collective-permute-start.16 = (bf16[64,2304]{1,0:T(8,128)(2,1)S(1)}, bf16[64,2304]{1,0:T(8,128)(2,1)S(1)}, u32[]{:S(2)}, u32[]{:S(2)}) collective-permute-start(bf16[64,2304]{1,0:T(8,128)(2,1)S(1)} %get-tuple-element.98.own_ref), channel_id=1, source_target_pairs={{0,16},{1,17},{2,18},{3,19},{4,20},{5,21},{6,22},{7,23},{8,24},{9,... | collective-permute-start | bytes 884744 | tf_op jit(solution)/shard_map/ppermute | solution.py:21
  48.7 3.1 %collective-permute-start.11 = (bf16[64,2048]{1,0:T(8,128)(2,1)S(1)}, bf16[64,2048]{1,0:T(8,128)(2,1)S(1)}, u32[]{:S(2)}, u32[]{:S(2)}) collective-permute-start(bf16[64,2048]{1,0:T(8,128)(2,1)S(1)} %get-tuple-element.95.refs_4_), channel_id=1, source_target_pairs={{0,1},{1,0},{2,3},{3,2},{4,5},{5,4},{6,7},{7,6},{8,9},{9,8},{10,11... | collective-permute-start | bytes 786440 | tf_op jit(solution)/shard_map/ppermute | solution.py:15
  49.9 11.9 %collective-permute-start.15 = (bf16[64,2304]{1,0:T(8,128)(2,1)S(1)}, bf16[64,2304]{1,0:T(8,128)(2,1)S(1)}, u32[]{:S(2)}, u32[]{:S(2)}) collective-permute-start(bf16[64,2304]{1,0:T(8,128)(2,1)S(1)} %get-tuple-element.97.own_ref), channel_id=1, source_target_pairs={{0,16},{1,17},{2,18},{3,19},{4,20},{5,21},{6,22},{7,23},{8,24},{9,... | collective-permute-start | bytes 884744 | tf_op jit(solution)/shard_map/ppermute | solution.py:21
  51.6 11.6 %collective-permute-start.14 = (bf16[64,2176]{1,0:T(8,128)(2,1)S(1)}, bf16[64,2176]{1,0:T(8,128)(2,1)S(1)}, u32[]{:S(2)}, u32[]{:S(2)}) collective-permute-start(bf16[64,2176]{1,0:T(8,128)(2,1)S(1)} %gather.1.refs_0_.refs_4_), channel_id=1, source_target_pairs={{0,1},{1,0},{2,3},{3,2},{4,5},{5,4},{6,7},{7,6},{8,9},{9,8},{10,11... | collective-permute-start | bytes 835592 | tf_op jit(solution)/shard_map/ppermute | solution.py:15
  53.0 14.1 %collective-permute-start.19 = (bf16[64,2304]{1,0:T(8,128)(2,1)S(1)}, bf16[64,2304]{1,0:T(8,128)(2,1)S(1)}, u32[]{:S(2)}, u32[]{:S(2)}) collective-permute-start(bf16[64,2304]{1,0:T(8,128)(2,1)S(1)} %get-tuple-element.104.own_ref), channel_id=1, source_target_pairs={{0,16},{1,17},{2,18},{3,19},{4,20},{5,21},{6,22},{7,23},{8,24},{9,... | collective-permute-start | bytes 884744 | tf_op jit(solution)/shard_map/ppermute | solution.py:21
  53.5 10.9 %collective-permute-start.13 = (bf16[64,2048]{1,0:T(8,128)(2,1)S(1)}, bf16[64,2048]{1,0:T(8,128)(2,1)S(1)}, u32[]{:S(2)}, u32[]{:S(2)}) collective-permute-start(bf16[64,2048]{1,0:T(8,128)(2,1)S(1)} %merge.5.refs_4_), channel_id=1, source_target_pairs={{0,12},{1,13},{2,14},{3,15},{4,8},{5,9},{6,10},{7,11},{8,4},{9,5},... | collective-permute-start | bytes 786440 | tf_op jit(solution)/shard_map/ppermute | solution.py:15
  63.1 1.6 %collective-permute-start.20 = (bf16[64,2048]{1,0:T(8,128)(2,1)S(1)}, bf16[64,2048]{1,0:T(8,128)(2,1)S(1)}, u32[]{:S(2)}, u32[]{:S(2)}) collective-permute-start(bf16[64,2048]{1,0:T(8,128)(2,1)S(1)} %get-tuple-element.101.refs_4_), channel_id=1, source_target_pairs={{0,1},{1,0},{2,3},{3,2},{4,5},{5,4},{6,7},{7,6},{8,9},{9,8},{10,11... | collective-permute-start | bytes 786440 | tf_op jit(solution)/shard_map/ppermute | solution.py:15
  64.3 9.5 %collective-permute-start.18 = (bf16[64,2304]{1,0:T(8,128)(2,1)S(1)}, bf16[64,2304]{1,0:T(8,128)(2,1)S(1)}, u32[]{:S(2)}, u32[]{:S(2)}) collective-permute-start(bf16[64,2304]{1,0:T(8,128)(2,1)S(1)} %get-tuple-element.103.own_ref), channel_id=1, source_target_pairs={{0,16},{1,17},{2,18},{3,19},{4,20},{5,21},{6,22},{7,23},{8,24},{9,... | collective-permute-start | bytes 884744 | tf_op jit(solution)/shard_map/ppermute | solution.py:21
  68.7 1.8 %collective-permute-start.21 = (bf16[64,2048]{1,0:T(8,128)(2,1)S(1)}, bf16[64,2048]{1,0:T(8,128)(2,1)S(1)}, u32[]{:S(2)}, u32[]{:S(2)}) collective-permute-start(bf16[64,2048]{1,0:T(8,128)(2,1)S(1)} %get-tuple-element.105.refs_2_), channel_id=1, source_target_pairs={{0,1},{1,0},{2,3},{3,2},{4,5},{5,4},{6,7},{7,6},{8,9},{9,8},{10,11... | collective-permute-start | bytes 786440 | tf_op jit(solution)/shard_map/ppermute | solution.py:15
  68.7 15.2 %collective-permute-start.23 = (bf16[64,2048]{1,0:T(8,128)(2,1)S(1)}, bf16[64,2048]{1,0:T(8,128)(2,1)S(1)}, u32[]{:S(2)}, u32[]{:S(2)}) collective-permute-start(bf16[64,2048]{1,0:T(8,128)(2,1)S(1)} %merge.7.refs_3_), channel_id=1, source_target_pairs={{0,8},{1,9},{2,10},{3,11},{4,12},{5,13},{6,14},{7,15},{8,0},{9,1},... | collective-permute-start | bytes 786440 | tf_op jit(solution)/shard_map/ppermute | solution.py:15
  70.5 13.5 %collective-permute-start.24 = (bf16[64,2048]{1,0:T(8,128)(2,1)S(1)}, bf16[64,2048]{1,0:T(8,128)(2,1)S(1)}, u32[]{:S(2)}, u32[]{:S(2)}) collective-permute-start(bf16[64,2048]{1,0:T(8,128)(2,1)S(1)} %merge.8.refs_3_), channel_id=1, source_target_pairs={{0,4},{1,5},{2,6},{3,7},{4,0},{5,1},{6,2},{7,3},{8,12},{9,13},{10,... | collective-permute-start | bytes 786440 | tf_op jit(solution)/shard_map/ppermute | solution.py:15
  75.2 8.8 %collective-permute-start.22 = (bf16[64,2048]{1,0:T(8,128)(2,1)S(1)}, bf16[64,2048]{1,0:T(8,128)(2,1)S(1)}, u32[]{:S(2)}, u32[]{:S(2)}) collective-permute-start(bf16[64,2048]{1,0:T(8,128)(2,1)S(1)} %get-tuple-element.106.refs_40_), channel_id=1, source_target_pairs={{0,1},{1,0},{2,3},{3,2},{4,5},{5,4},{6,7},{7,6},{8,9},{9,8},{10,11... | collective-permute-start | bytes 786440 | tf_op jit(solution)/shard_map/ppermute | solution.py:15
  84.2 4.3 %collective-permute-start.25 = (bf16[16,2048]{1,0:T(8,128)(2,1)S(1)}, bf16[16,2048]{1,0:T(8,128)(2,1)S(1)}, u32[]{:S(2)}, u32[]{:S(2)}) collective-permute-start(bf16[16,2048]{1,0:T(8,128)(2,1)S(1)} %get-tuple-element.149), channel_id=1, source_target_pairs={{0,2},{1,3},{2,0},{3,1},{4,6},{5,7},{6,4},{7,5},{8,10},{9,11},{10,... | collective-permute-start | bytes 196616 | tf_op jit(solution)/shard_map/ppermute | solution.py:15
  85.7 4.3 %collective-permute-start.26 = (bf16[16,2048]{1,0:T(8,128)(2,1)S(1)}, bf16[16,2048]{1,0:T(8,128)(2,1)S(1)}, u32[]{:S(2)}, u32[]{:S(2)}) collective-permute-start(bf16[16,2048]{1,0:T(8,128)(2,1)S(1)} %get-tuple-element.150), channel_id=1, source_target_pairs={{0,16},{1,17},{2,18},{3,19},{4,20},{5,21},{6,22},{7,23},{8,24},{9,... | collective-permute-start | bytes 196616 | tf_op jit(solution)/shard_map/ppermute | solution.py:21
  86.4 5.2 %collective-permute-start.27 = (bf16[16,2048]{1,0:T(8,128)(2,1)S(1)}, bf16[16,2048]{1,0:T(8,128)(2,1)S(1)}, u32[]{:S(2)}, u32[]{:S(2)}) collective-permute-start(bf16[16,2048]{1,0:T(8,128)(2,1)S(1)} %get-tuple-element.151), channel_id=1, source_target_pairs={{0,18},{1,19},{2,16},{3,17},{4,22},{5,23},{6,20},{7,21},{8,26},{9,... | collective-permute-start | bytes 196616 | tf_op jit(solution)/shard_map/ppermute | solution.py:21

commit v4 on v3

--- a/solution.py
+++ b/solution.py
@@ -197,7 +197,7 @@
         in_specs=[vmem] * 4,
         out_specs=(vmem, vmem),
         cost_estimate=long,
-        compiler_params=pltpu.CompilerParams(vmem_limit_bytes=58 * 1024 * 1024),
+        compiler_params=pltpu.CompilerParams(vmem_limit_bytes=55 * 1024 * 1024),
         name="prepare",
     )(tokens, routes.T, gates.T, cotangent)
 

time: 92.4 us -> 92.4 us (level)
  no operation moved by 1% of the time
where the time goes in v4:
time: 92.4 us; the launch traced here: 92.2 us
  waiting for transfers between devices  35.1 us (38%)
  starting transfers between devices  28.1 us (30%)
  Pallas kernels  27.3 us (30%)
    ppermute x16, waiting for transfers between devices, swap(): return lax.ppermute(value, 'expert', pairs)  21.1 us
    ppermute x16, starting transfers between devices, swap(): return lax.ppermute(value, 'expert', pairs)  17.6 us
    ppermute x12, waiting for transfers between devices, swap(): return lax.ppermute(value, ('dp', 'expert'), pairs)  14 us
    pallas_call x8, Pallas kernels, expert(): pl.pallas_call(functools.partial(expert_kernel, rows, len(last), parts, f...  10.9 us
    ppermute x12, starting transfers between devices, swap(): return lax.ppermute(value, ('dp', 'expert'), pairs)  10.6 us
    pallas_call x8, Pallas kernels, partials(): pl.pallas_call(functools.partial(partial_kernel, len(pieces), len(sizes),...  9.14 us
    pallas_call x1, Pallas kernels, run_grads(): pl.pallas_call(functools.partial(grad_kernel, [len(group) for group in gr...  4.43 us
  transfers between devices with their start and end apart: 28, of which 13 were waited for; matrix products, arithmetic and copies ran while one was open for 0% of the time, Pallas kernels for 27%

profile of v4, /device:TPU:0, one launch (start us, length us, event | category | flops | bytes accessed | tf_op | source)
XLA Modules:
  0.0 92.2 jit_solution(15846789381415962048)
XLA Ops:
  0.6 1.8 %prepare.1 = (bf16[16,2176]{1,0:T(8,128)(2,1)}, bf16[16,2176]{1,0:T(8,128)(2,1)}) custom-call(bf16[16,2048]{1,0:T(8,128)(2,1)} %tokens_ref.1, s32[8,16]{1,0:T(8,128)} %bitcast.2, f32[8,16]{1,0:T(8,128)} %bitcast.3, bf16[16,2048]{1,0:T(8,128)(2,1)} %cotangent_ref.1), custom_call_target="tpu_custom_call" | custom-call | flops 10000000000 | bytes 1000 | tf_op jit(solution)/shard_map/prepare/pallas_call | solution.py:194
  2.4 3.0 %collective-permute-start.1 = (bf16[16,2176]{1,0:T(8,128)(2,1)}, bf16[16,2176]{1,0:T(8,128)(2,1)S(1)}, u32[]{:S(2)}, u32[]{:S(2)}) collective-permute-start(bf16[16,2176]{1,0:T(8,128)(2,1)} %get-tuple-element.81.refs_0_), channel_id=1, source_target_pairs={{0,2},{1,3},{2,0},{3,1},{4,6},{5,7},{6,4},{7,5},{8,10},{9,11},{10,... | collective-permute-start | bytes 208904 | tf_op jit(solution)/shard_map/ppermute | solution.py:15
  5.4 1.4 %collective-permute-start.2 = (bf16[16,2176]{1,0:T(8,128)(2,1)}, bf16[16,2176]{1,0:T(8,128)(2,1)S(1)}, u32[]{:S(2)}, u32[]{:S(2)}) collective-permute-start(bf16[16,2176]{1,0:T(8,128)(2,1)} %get-tuple-element.82), channel_id=1, source_target_pairs={{0,18},{1,19},{2,16},{3,17},{4,22},{5,23},{6,20},{7,21},{8,26},{9,... | collective-permute-start | bytes 208904 | tf_op jit(solution)/shard_map/ppermute | solution.py:21
  6.8 0.1 collective-permute-start
  6.9 1.6 %collective-permute-done.1.refs_2_ = bf16[16,2176]{1,0:T(8,128)(2,1)S(1)} collective-permute-done((bf16[16,2176]{1,0:T(8,128)(2,1)}, bf16[16,2176]{1,0:T(8,128)(2,1)S(1)}, u32[]{:S(2)}, u32[]{:S(2)}) %collective-permute-start.1) | collective-permute-done | bytes 69664 | tf_op jit(solution)/shard_map/ppermute | solution.py:15
  8.5 2.8 %collective-permute-done.2.refs_3_ = bf16[16,2176]{1,0:T(8,128)(2,1)S(1)} collective-permute-done((bf16[16,2176]{1,0:T(8,128)(2,1)}, bf16[16,2176]{1,0:T(8,128)(2,1)S(1)}, u32[]{:S(2)}, u32[]{:S(2)}) %collective-permute-start.2) | collective-permute-done | bytes 69664 | tf_op jit(solution)/shard_map/ppermute | solution.py:21
  11.3 0.9 copy-done.3
  12.2 1.6 %collective-permute-start.4 = (bf16[64,2176]{1,0:T(8,128)(2,1)S(1)}, bf16[64,2176]{1,0:T(8,128)(2,1)S(1)}, u32[]{:S(2)}, u32[]{:S(2)}) collective-permute-start(bf16[64,2176]{1,0:T(8,128)(2,1)S(1)} %gather.1.refs_0_.refs_4_), channel_id=1, source_target_pairs={{0,4},{1,5},{2,6},{3,7},{4,0},{5,1},{6,2},{7,3},{8,12},{9,13},{10,... | collective-permute-start | bytes 835592 | tf_op jit(solution)/shard_map/ppermute | solution.py:15
  13.9 2.5 %collective-permute-start.3 = (bf16[64,2176]{1,0:T(8,128)(2,1)S(1)}, bf16[64,2176]{1,0:T(8,128)(2,1)S(1)}, u32[]{:S(2)}, u32[]{:S(2)}) collective-permute-start(bf16[64,2176]{1,0:T(8,128)(2,1)S(1)} %gather.1.refs_0_.refs_4_), channel_id=1, source_target_pairs={{0,12},{1,13},{2,14},{3,15},{4,8},{5,9},{6,10},{7,11},{8,4},{9,5},... | collective-permute-start | bytes 835592 | tf_op jit(solution)/shard_map/ppermute | solution.py:15
  16.4 1.1 %partials.8 = (bf16[64,2304]{1,0:T(8,128)(2,1)S(1)}, f32[64,128]{1,0:T(8,128)S(1)}, bf16[64,1024]{1,0:T(8,128)(2,1)S(1)}, bf16[64,1024]{1,0:T(8,128)(2,1)S(1)}) custom-call(bf16[64,2176]{1,0:T(8,128)(2,1)S(1)} %gather.1.refs_0_.refs_4_, bf16[1,1024,768]{2,1,0:T(8,128)(2,1)S(1)} %copy-done, bf16[1,1024,768]{2,1,0:T(8,128)(2,1)S(1)} %copy-done.1, ...), custom_call_target="tpu_custom_call" | custom-call | flops 1000 | bytes 1000 | tf_op jit(solution)/shard_map/partials/pallas_call | solution.py:210
  17.5 1.1 %collective-permute-start.9 = (bf16[64,2304]{1,0:T(8,128)(2,1)S(1)}, bf16[64,2304]{1,0:T(8,128)(2,1)S(1)}, u32[]{:S(2)}, u32[]{:S(2)}) collective-permute-start(bf16[64,2304]{1,0:T(8,128)(2,1)S(1)} %get-tuple-element.88.own_ref), channel_id=1, source_target_pairs={{0,16},{1,17},{2,18},{3,19},{4,20},{5,21},{6,22},{7,23},{8,24},{9,... | collective-permute-start | bytes 884744 | tf_op jit(solution)/shard_map/ppermute | solution.py:21
  18.6 2.4 %collective-permute-done.4.refs_0_ = bf16[64,2176]{1,0:T(8,128)(2,1)S(1)} collective-permute-done((bf16[64,2176]{1,0:T(8,128)(2,1)S(1)}, bf16[64,2176]{1,0:T(8,128)(2,1)S(1)}, u32[]{:S(2)}, u32[]{:S(2)}) %collective-permute-start.4) | collective-permute-done | bytes 278560 | tf_op jit(solution)/shard_map/ppermute | solution.py:15
  21.0 1.1 %partials.9 = (bf16[64,2304]{1,0:T(8,128)(2,1)S(1)}, f32[64,128]{1,0:T(8,128)S(1)}, bf16[64,1024]{1,0:T(8,128)(2,1)S(1)}, bf16[64,1024]{1,0:T(8,128)(2,1)S(1)}) custom-call(bf16[64,2176]{1,0:T(8,128)(2,1)S(1)} %collective-permute-done.4.refs_0_, bf16[1,1024,768]{2,1,0:T(8,128)(2,1)S(1)} %copy-done, bf16[1,1024,768]{2,1,0:T(8,128)(2,1)S(1)} %copy-done.1, ...), custom_call_target="tpu_custom_call" | custom-call | flops 1000 | bytes 1000 | tf_op jit(solution)/shard_map/partials/pallas_call | solution.py:210
  22.1 1.1 %collective-permute-start.8 = (bf16[64,2304]{1,0:T(8,128)(2,1)S(1)}, bf16[64,2304]{1,0:T(8,128)(2,1)S(1)}, u32[]{:S(2)}, u32[]{:S(2)}) collective-permute-start(bf16[64,2304]{1,0:T(8,128)(2,1)S(1)} %get-tuple-element.87.own_ref), channel_id=1, source_target_pairs={{0,16},{1,17},{2,18},{3,19},{4,20},{5,21},{6,22},{7,23},{8,24},{9,... | collective-permute-start | bytes 884744 | tf_op jit(solution)/shard_map/ppermute | solution.py:21
  23.2 4.7 %collective-permute-done.3.refs_0_ = bf16[64,2176]{1,0:T(8,128)(2,1)S(1)} collective-permute-done((bf16[64,2176]{1,0:T(8,128)(2,1)S(1)}, bf16[64,2176]{1,0:T(8,128)(2,1)S(1)}, u32[]{:S(2)}, u32[]{:S(2)}) %collective-permute-start.3) | collective-permute-done | bytes 278560 | tf_op jit(solution)/shard_map/ppermute | solution.py:15
  27.9 1.8 %collective-permute-start.6 = (bf16[64,2176]{1,0:T(8,128)(2,1)S(1)}, bf16[64,2176]{1,0:T(8,128)(2,1)S(1)}, u32[]{:S(2)}, u32[]{:S(2)}) collective-permute-start(bf16[64,2176]{1,0:T(8,128)(2,1)S(1)} %gather.1.refs_0_.refs_4_), channel_id=1, source_target_pairs={{0,8},{1,9},{2,10},{3,11},{4,12},{5,13},{6,14},{7,15},{8,0},{9,1},... | collective-permute-start | bytes 835592 | tf_op jit(solution)/shard_map/ppermute | solution.py:15
  29.7 1.1 %partials.10 = (bf16[64,2304]{1,0:T(8,128)(2,1)S(1)}, f32[64,128]{1,0:T(8,128)S(1)}, bf16[64,1024]{1,0:T(8,128)(2,1)S(1)}, bf16[64,1024]{1,0:T(8,128)(2,1)S(1)}) custom-call(bf16[64,2176]{1,0:T(8,128)(2,1)S(1)} %collective-permute-done.3.refs_0_, bf16[1,1024,768]{2,1,0:T(8,128)(2,1)S(1)} %copy-done, bf16[1,1024,768]{2,1,0:T(8,128)(2,1)S(1)} %copy-done.1, ...), custom_call_target="tpu_custom_call" | custom-call | flops 1000 | bytes 1000 | tf_op jit(solution)/shard_map/partials/pallas_call | solution.py:210
  30.8 0.5 collective-permute-start.5
  31.3 0.0 collective-permute-done.9.their_ref
  31.3 1.3 %expert.8 = (bf16[64,2048]{1,0:T(8,128)(2,1)S(1)}, bf16[64,768]{1,0:T(8,128)(2,1)S(1)}, bf16[64,768]{1,0:T(8,128)(2,1)S(1)}, bf16[64,768]{1,0:T(8,128)(2,1)S(1)}) custom-call(bf16[64,2304]{1,0:T(8,128)(2,1)S(1)} %get-tuple-element.88.own_ref, bf16[64,2304]{1,0:T(8,128)(2,1)S(1)} %collective-permute-done.9.their_ref, ...), custom_call_target="tpu_custom_call" | custom-call | flops 1000 | bytes 1000 | tf_op jit(solution)/shard_map/expert/pallas_call | solution.py:226
  32.6 1.3 %expert.9 = (bf16[64,2048]{1,0:T(8,128)(2,1)S(1)}, bf16[64,768]{1,0:T(8,128)(2,1)S(1)}, bf16[64,768]{1,0:T(8,128)(2,1)S(1)}, bf16[64,768]{1,0:T(8,128)(2,1)S(1)}) custom-call(bf16[64,2304]{1,0:T(8,128)(2,1)S(1)} %get-tuple-element.87.own_ref, bf16[64,2304]{1,0:T(8,128)(2,1)S(1)} %collective-permute-done.8.their_ref, ...), custom_call_target="tpu_custom_call" | custom-call | flops 1000 | bytes 1000 | tf_op jit(solution)/shard_map/expert/pallas_call | solution.py:226
  34.0 1.1 %partials.11 = (bf16[64,2304]{1,0:T(8,128)(2,1)S(1)}, f32[64,128]{1,0:T(8,128)S(1)}, bf16[64,1024]{1,0:T(8,128)(2,1)S(1)}, bf16[64,1024]{1,0:T(8,128)(2,1)S(1)}) custom-call(bf16[64,2176]{1,0:T(8,128)(2,1)S(1)} %collective-permute-done.7.refs_0_, bf16[1,1024,768]{2,1,0:T(8,128)(2,1)S(1)} %copy-done, bf16[1,1024,768]{2,1,0:T(8,128)(2,1)S(1)} %copy-done.1, ...), custom_call_target="tpu_custom_call" | custom-call | flops 1000 | bytes 1000 | tf_op jit(solution)/shard_map/partials/pallas_call | solution.py:210
  35.2 1.7 %collective-permute-start.10 = (bf16[64,2304]{1,0:T(8,128)(2,1)S(1)}, bf16[64,2304]{1,0:T(8,128)(2,1)S(1)}, u32[]{:S(2)}, u32[]{:S(2)}) collective-permute-start(bf16[64,2304]{1,0:T(8,128)(2,1)S(1)} %get-tuple-element.94.own_ref), channel_id=1, source_target_pairs={{0,16},{1,17},{2,18},{3,19},{4,20},{5,21},{6,22},{7,23},{8,24},{9,... | collective-permute-start | bytes 884744 | tf_op jit(solution)/shard_map/ppermute | solution.py:21
  36.8 7.0 %collective-permute-done.6.refs_0_ = bf16[64,2176]{1,0:T(8,128)(2,1)S(1)} collective-permute-done((bf16[64,2176]{1,0:T(8,128)(2,1)S(1)}, bf16[64,2176]{1,0:T(8,128)(2,1)S(1)}, u32[]{:S(2)}, u32[]{:S(2)}) %collective-permute-start.6) | collective-permute-done | bytes 278560 | tf_op jit(solution)/shard_map/ppermute | solution.py:15
  43.9 0.5 collective-permute-start.17
  44.4 1.1 %partials.12 = (bf16[64,2304]{1,0:T(8,128)(2,1)S(1)}, f32[64,128]{1,0:T(8,128)S(1)}, bf16[64,1024]{1,0:T(8,128)(2,1)S(1)}, bf16[64,1024]{1,0:T(8,128)(2,1)S(1)}) custom-call(bf16[64,2176]{1,0:T(8,128)(2,1)S(1)} %collective-permute-done.6.refs_0_, bf16[1,1024,768]{2,1,0:T(8,128)(2,1)S(1)} %copy-done, bf16[1,1024,768]{2,1,0:T(8,128)(2,1)S(1)} %copy-done.1, ...), custom_call_target="tpu_custom_call" | custom-call | flops 1000 | bytes 1000 | tf_op jit(solution)/shard_map/partials/pallas_call | solution.py:210
  45.5 0.5 collective-permute-start.16
  46.0 1.3 %expert.10 = (bf16[64,2048]{1,0:T(8,128)(2,1)S(1)}, bf16[64,768]{1,0:T(8,128)(2,1)S(1)}, bf16[64,768]{1,0:T(8,128)(2,1)S(1)}, bf16[64,768]{1,0:T(8,128)(2,1)S(1)}) custom-call(bf16[64,2304]{1,0:T(8,128)(2,1)S(1)} %get-tuple-element.85.own_ref, bf16[64,2304]{1,0:T(8,128)(2,1)S(1)} %collective-permute-done.5.their_ref, ...), custom_call_target="tpu_custom_call" | custom-call | flops 1000 | bytes 1000 | tf_op jit(solution)/shard_map/expert/pallas_call | solution.py:226
  47.3 1.3 %expert.11 = (bf16[64,2048]{1,0:T(8,128)(2,1)S(1)}, bf16[64,768]{1,0:T(8,128)(2,1)S(1)}, bf16[64,768]{1,0:T(8,128)(2,1)S(1)}, bf16[64,768]{1,0:T(8,128)(2,1)S(1)}) custom-call(bf16[64,2304]{1,0:T(8,128)(2,1)S(1)} %get-tuple-element.94.own_ref, bf16[64,2304]{1,0:T(8,128)(2,1)S(1)} %collective-permute-done.10.their_ref, ...), custom_call_target="tpu_custom_call" | custom-call | flops 1000 | bytes 1000 | tf_op jit(solution)/shard_map/expert/pallas_call | solution.py:226
  48.7 0.1 collective-permute-start.11
  48.8 1.1 %partials.13 = (bf16[64,2304]{1,0:T(8,128)(2,1)S(1)}, f32[64,128]{1,0:T(8,128)S(1)}, bf16[64,1024]{1,0:T(8,128)(2,1)S(1)}, bf16[64,1024]{1,0:T(8,128)(2,1)S(1)}) custom-call(bf16[64,2176]{1,0:T(8,128)(2,1)S(1)} %collective-permute-done.12.refs_0_, bf16[1,1024,768]{2,1,0:T(8,128)(2,1)S(1)} %copy-done, bf16[1,1024,768]{2,1,0:T(8,128)(2,1)S(1)} %copy-done.1, ...), custom_call_target="tpu_custom_call" | custom-call | flops 1000 | bytes 1000 | tf_op jit(solution)/shard_map/partials/pallas_call | solution.py:210
  49.9 1.7 %collective-permute-start.15 = (bf16[64,2304]{1,0:T(8,128)(2,1)S(1)}, bf16[64,2304]{1,0:T(8,128)(2,1)S(1)}, u32[]{:S(2)}, u32[]{:S(2)}) collective-permute-start(bf16[64,2304]{1,0:T(8,128)(2,1)S(1)} %get-tuple-element.97.own_ref), channel_id=1, source_target_pairs={{0,16},{1,17},{2,18},{3,19},{4,20},{5,21},{6,22},{7,23},{8,24},{9,... | collective-permute-start | bytes 884744 | tf_op jit(solution)/shard_map/ppermute | solution.py:21
  51.6 0.2 collective-permute-start.14
  51.8 0.1 merge.5.refs_4_
  51.9 1.1 %partials.14 = (bf16[64,2304]{1,0:T(8,128)(2,1)S(1)}, f32[64,128]{1,0:T(8,128)S(1)}, bf16[64,1024]{1,0:T(8,128)(2,1)S(1)}, bf16[64,1024]{1,0:T(8,128)(2,1)S(1)}) custom-call(bf16[64,2176]{1,0:T(8,128)(2,1)S(1)} %collective-permute-done.17.refs_0_, bf16[1,1024,768]{2,1,0:T(8,128)(2,1)S(1)} %copy-done, bf16[1,1024,768]{2,1,0:T(8,128)(2,1)S(1)} %copy-done.1, ...), custom_call_target="tpu_custom_call" | custom-call | flops 1000 | bytes 1000 | tf_op jit(solution)/shard_map/partials/pallas_call | solution.py:210
  53.0 0.5 collective-permute-start.19
  53.5 2.7 %collective-permute-start.13 = (bf16[64,2048]{1,0:T(8,128)(2,1)S(1)}, bf16[64,2048]{1,0:T(8,128)(2,1)S(1)}, u32[]{:S(2)}, u32[]{:S(2)}) collective-permute-start(bf16[64,2048]{1,0:T(8,128)(2,1)S(1)} %merge.5.refs_4_), channel_id=1, source_target_pairs={{0,12},{1,13},{2,14},{3,15},{4,8},{5,9},{6,10},{7,11},{8,4},{9,5},... | collective-permute-start | bytes 786440 | tf_op jit(solution)/shard_map/ppermute | solution.py:15
  56.2 1.3 %expert.12 = (bf16[64,2048]{1,0:T(8,128)(2,1)S(1)}, bf16[64,768]{1,0:T(8,128)(2,1)S(1)}, bf16[64,768]{1,0:T(8,128)(2,1)S(1)}, bf16[64,768]{1,0:T(8,128)(2,1)S(1)}) custom-call(bf16[64,2304]{1,0:T(8,128)(2,1)S(1)} %get-tuple-element.98.own_ref, bf16[64,2304]{1,0:T(8,128)(2,1)S(1)} %collective-permute-done.16.their_ref, ...), custom_call_target="tpu_custom_call" | custom-call | flops 1000 | bytes 1000 | tf_op jit(solution)/shard_map/expert/pallas_call | solution.py:226
  57.5 4.3 %collective-permute-done.15.their_ref = bf16[64,2304]{1,0:T(8,128)(2,1)S(1)} collective-permute-done((bf16[64,2304]{1,0:T(8,128)(2,1)S(1)}, bf16[64,2304]{1,0:T(8,128)(2,1)S(1)}, u32[]{:S(2)}, u32[]{:S(2)}) %collective-permute-start.15) | collective-permute-done | bytes 294944 | tf_op jit(solution)/shard_map/ppermute | solution.py:21
  61.8 1.3 %expert.13 = (bf16[64,2048]{1,0:T(8,128)(2,1)S(1)}, bf16[64,768]{1,0:T(8,128)(2,1)S(1)}, bf16[64,768]{1,0:T(8,128)(2,1)S(1)}, bf16[64,768]{1,0:T(8,128)(2,1)S(1)}) custom-call(bf16[64,2304]{1,0:T(8,128)(2,1)S(1)} %get-tuple-element.97.own_ref, bf16[64,2304]{1,0:T(8,128)(2,1)S(1)} %collective-permute-done.15.their_ref, ...), custom_call_target="tpu_custom_call" | custom-call | flops 1000 | bytes 1000 | tf_op jit(solution)/shard_map/expert/pallas_call | solution.py:226
  63.1 0.1 collective-permute-start.20
  63.2 1.1 %partials.15 = (bf16[64,2304]{1,0:T(8,128)(2,1)S(1)}, f32[64,128]{1,0:T(8,128)S(1)}, bf16[64,1024]{1,0:T(8,128)(2,1)S(1)}, bf16[64,1024]{1,0:T(8,128)(2,1)S(1)}) custom-call(bf16[64,2176]{1,0:T(8,128)(2,1)S(1)} %collective-permute-done.14.refs_0_, bf16[1,1024,768]{2,1,0:T(8,128)(2,1)S(1)} %copy-done, bf16[1,1024,768]{2,1,0:T(8,128)(2,1)S(1)} %copy-done.1, ...), custom_call_target="tpu_custom_call" | custom-call | flops 1000 | bytes 1000 | tf_op jit(solution)/shard_map/partials/pallas_call | solution.py:210
  64.3 0.1 collective-permute-start.18
  64.5 0.3 collective-permute-done.20.refs_1_
  64.7 0.1 merge.7.refs_3_
  64.8 2.4 %collective-permute-done.19.their_ref = bf16[64,2304]{1,0:T(8,128)(2,1)S(1)} collective-permute-done((bf16[64,2304]{1,0:T(8,128)(2,1)S(1)}, bf16[64,2304]{1,0:T(8,128)(2,1)S(1)}, u32[]{:S(2)}, u32[]{:S(2)}) %collective-permute-start.19) | collective-permute-done | bytes 294944 | tf_op jit(solution)/shard_map/ppermute | solution.py:21
  67.1 1.5 %expert.14 = (bf16[64,2048]{1,0:T(8,128)(2,1)S(1)}, bf16[64,768]{1,0:T(8,128)(2,1)S(1)}, bf16[64,768]{1,0:T(8,128)(2,1)S(1)}, bf16[64,768]{1,0:T(8,128)(2,1)S(1)}) custom-call(bf16[64,2304]{1,0:T(8,128)(2,1)S(1)} %get-tuple-element.104.own_ref, bf16[64,2304]{1,0:T(8,128)(2,1)S(1)} %collective-permute-done.19.their_ref, ...), custom_call_target="tpu_custom_call" | custom-call | flops 1000 | bytes 1000 | tf_op jit(solution)/shard_map/expert/pallas_call | solution.py:226
  68.7 0.1 collective-permute-start.21
  68.7 1.7 %collective-permute-start.23 = (bf16[64,2048]{1,0:T(8,128)(2,1)S(1)}, bf16[64,2048]{1,0:T(8,128)(2,1)S(1)}, u32[]{:S(2)}, u32[]{:S(2)}) collective-permute-start(bf16[64,2048]{1,0:T(8,128)(2,1)S(1)} %merge.7.refs_3_), channel_id=1, source_target_pairs={{0,8},{1,9},{2,10},{3,11},{4,12},{5,13},{6,14},{7,15},{8,0},{9,1},... | collective-permute-start | bytes 786440 | tf_op jit(solution)/shard_map/ppermute | solution.py:15
  70.4 0.1 merge.8.refs_3_
  70.5 1.8 %collective-permute-start.24 = (bf16[64,2048]{1,0:T(8,128)(2,1)S(1)}, bf16[64,2048]{1,0:T(8,128)(2,1)S(1)}, u32[]{:S(2)}, u32[]{:S(2)}) collective-permute-start(bf16[64,2048]{1,0:T(8,128)(2,1)S(1)} %merge.8.refs_3_), channel_id=1, source_target_pairs={{0,4},{1,5},{2,6},{3,7},{4,0},{5,1},{6,2},{7,3},{8,12},{9,13},{10,... | collective-permute-start | bytes 786440 | tf_op jit(solution)/shard_map/ppermute | solution.py:15
  72.3 1.5 %collective-permute-done.18.their_ref = bf16[64,2304]{1,0:T(8,128)(2,1)S(1)} collective-permute-done((bf16[64,2304]{1,0:T(8,128)(2,1)S(1)}, bf16[64,2304]{1,0:T(8,128)(2,1)S(1)}, u32[]{:S(2)}, u32[]{:S(2)}) %collective-permute-start.18) | collective-permute-done | bytes 294944 | tf_op jit(solution)/shard_map/ppermute | solution.py:21
  73.8 1.3 %expert.15 = (bf16[64,2048]{1,0:T(8,128)(2,1)S(1)}, bf16[64,768]{1,0:T(8,128)(2,1)S(1)}, bf16[64,768]{1,0:T(8,128)(2,1)S(1)}, bf16[64,768]{1,0:T(8,128)(2,1)S(1)}) custom-call(bf16[64,2304]{1,0:T(8,128)(2,1)S(1)} %get-tuple-element.103.own_ref, bf16[64,2304]{1,0:T(8,128)(2,1)S(1)} %collective-permute-done.18.their_ref, ...), custom_call_target="tpu_custom_call" | custom-call | flops 1000 | bytes 1000 | tf_op jit(solution)/shard_map/expert/pallas_call | solution.py:226
  75.2 0.1 collective-permute-start.22
  75.2 4.4 %grads.1 = (bf16[1,1024,768]{2,1,0:T(8,128)(2,1)}, bf16[1,1024,768]{2,1,0:T(8,128)(2,1)}, bf16[1,768,1024]{2,1,0:T(8,128)(2,1)}, f32[8,128]{1,0:T(8,128)S(1)}) custom-call(bf16[64,1024]{1,0:T(8,128)(2,1)S(1)} %get-tuple-element.107.refs_0_, bf16[64,1024]{1,0:T(8,128)(2,1)S(1)} %get-tuple-element.108.refs_1_, ...), custom_call_target="tpu_custom_call" | custom-call | flops 1000 | bytes 1000 | tf_op jit(solution)/shard_map/grads/pallas_call | solution.py:301
  79.7 4.3 %collective-permute-done.23.refs_3_ = bf16[64,2048]{1,0:T(8,128)(2,1)S(1)} collective-permute-done((bf16[64,2048]{1,0:T(8,128)(2,1)S(1)}, bf16[64,2048]{1,0:T(8,128)(2,1)S(1)}, u32[]{:S(2)}, u32[]{:S(2)}) %collective-permute-start.23) | collective-permute-done | bytes 262176 | tf_op jit(solution)/shard_map/ppermute | solution.py:15
  84.0 0.2 merge.9
  84.2 1.6 %collective-permute-start.25 = (bf16[16,2048]{1,0:T(8,128)(2,1)S(1)}, bf16[16,2048]{1,0:T(8,128)(2,1)S(1)}, u32[]{:S(2)}, u32[]{:S(2)}) collective-permute-start(bf16[16,2048]{1,0:T(8,128)(2,1)S(1)} %get-tuple-element.149), channel_id=1, source_target_pairs={{0,2},{1,3},{2,0},{3,1},{4,6},{5,7},{6,4},{7,5},{8,10},{9,11},{10,... | collective-permute-start | bytes 196616 | tf_op jit(solution)/shard_map/ppermute | solution.py:15
  85.7 0.6 collective-permute-start.26
  86.4 1.3 %collective-permute-start.27 = (bf16[16,2048]{1,0:T(8,128)(2,1)S(1)}, bf16[16,2048]{1,0:T(8,128)(2,1)S(1)}, u32[]{:S(2)}, u32[]{:S(2)}) collective-permute-start(bf16[16,2048]{1,0:T(8,128)(2,1)S(1)} %get-tuple-element.151), channel_id=1, source_target_pairs={{0,18},{1,19},{2,16},{3,17},{4,22},{5,23},{6,20},{7,21},{8,26},{9,... | collective-permute-start | bytes 196616 | tf_op jit(solution)/shard_map/ppermute | solution.py:21
  87.7 0.8 collective-permute-done.25.refs_1_
  88.5 1.5 %collective-permute-done.26.refs_2_ = bf16[16,2048]{1,0:T(8,128)(2,1)S(1)} collective-permute-done((bf16[16,2048]{1,0:T(8,128)(2,1)S(1)}, bf16[16,2048]{1,0:T(8,128)(2,1)S(1)}, u32[]{:S(2)}, u32[]{:S(2)}) %collective-permute-start.26) | collective-permute-done | bytes 65568 | tf_op jit(solution)/shard_map/ppermute | solution.py:21
  90.0 1.5 %collective-permute-done.27.refs_3_ = bf16[16,2048]{1,0:T(8,128)(2,1)S(1)} collective-permute-done((bf16[16,2048]{1,0:T(8,128)(2,1)S(1)}, bf16[16,2048]{1,0:T(8,128)(2,1)S(1)}, u32[]{:S(2)}, u32[]{:S(2)}) %collective-permute-start.27) | collective-permute-done | bytes 65568 | tf_op jit(solution)/shard_map/ppermute | solution.py:21
  91.5 0.7 finish.1
  (25 shorter events, 0.1 us)
Async XLA Ops:
  2.4 6.1 %collective-permute-start.1 = (bf16[16,2176]{1,0:T(8,128)(2,1)}, bf16[16,2176]{1,0:T(8,128)(2,1)S(1)}, u32[]{:S(2)}, u32[]{:S(2)}) collective-permute-start(bf16[16,2176]{1,0:T(8,128)(2,1)} %get-tuple-element.81.refs_0_), channel_id=1, source_target_pairs={{0,2},{1,3},{2,0},{3,1},{4,6},{5,7},{6,4},{7,5},{8,10},{9,11},{10,... | collective-permute-start | bytes 208904 | tf_op jit(solution)/shard_map/ppermute | solution.py:15
  5.4 11.0 %copy-start = (bf16[1,1024,768]{2,1,0:T(8,128)(2,1)S(1)}, bf16[1,1024,768]{2,1,0:T(8,128)(2,1)}, u32[]{:S(2)}) copy-start(bf16[1,1024,768]{2,1,0:T(8,128)(2,1)} %refs_0_.15) | copy-start | bytes 4718596
  5.4 11.0 %copy-start.1 = (bf16[1,1024,768]{2,1,0:T(8,128)(2,1)S(1)}, bf16[1,1024,768]{2,1,0:T(8,128)(2,1)}, u32[]{:S(2)}) copy-start(bf16[1,1024,768]{2,1,0:T(8,128)(2,1)} %refs_1_.31) | copy-start | bytes 4718596
  5.4 11.0 %copy-start.2 = (bf16[1,768,1024]{2,1,0:T(8,128)(2,1)S(1)}, bf16[1,768,1024]{2,1,0:T(8,128)(2,1)}, u32[]{:S(2)}) copy-start(bf16[1,768,1024]{2,1,0:T(8,128)(2,1)} %refs_2_.31) | copy-start | bytes 4718596
  5.4 6.0 %collective-permute-start.2 = (bf16[16,2176]{1,0:T(8,128)(2,1)}, bf16[16,2176]{1,0:T(8,128)(2,1)S(1)}, u32[]{:S(2)}, u32[]{:S(2)}) collective-permute-start(bf16[16,2176]{1,0:T(8,128)(2,1)} %get-tuple-element.82), channel_id=1, source_target_pairs={{0,18},{1,19},{2,16},{3,17},{4,22},{5,23},{6,20},{7,21},{8,26},{9,... | collective-permute-start | bytes 208904 | tf_op jit(solution)/shard_map/ppermute | solution.py:21
  6.8 4.5 %collective-permute-start = (bf16[16,2176]{1,0:T(8,128)(2,1)}, bf16[16,2176]{1,0:T(8,128)(2,1)S(1)}, u32[]{:S(2)}, u32[]{:S(2)}) collective-permute-start(bf16[16,2176]{1,0:T(8,128)(2,1)} %get-tuple-element.82), channel_id=1, source_target_pairs={{0,16},{1,17},{2,18},{3,19},{4,20},{5,21},{6,22},{7,23},{8,24},{9,... | collective-permute-start | bytes 208904 | tf_op jit(solution)/shard_map/ppermute | solution.py:21
  11.3 0.9 copy-start.3
  12.2 8.8 %collective-permute-start.4 = (bf16[64,2176]{1,0:T(8,128)(2,1)S(1)}, bf16[64,2176]{1,0:T(8,128)(2,1)S(1)}, u32[]{:S(2)}, u32[]{:S(2)}) collective-permute-start(bf16[64,2176]{1,0:T(8,128)(2,1)S(1)} %gather.1.refs_0_.refs_4_), channel_id=1, source_target_pairs={{0,4},{1,5},{2,6},{3,7},{4,0},{5,1},{6,2},{7,3},{8,12},{9,13},{10,... | collective-permute-start | bytes 835592 | tf_op jit(solution)/shard_map/ppermute | solution.py:15
  13.9 14.0 %collective-permute-start.3 = (bf16[64,2176]{1,0:T(8,128)(2,1)S(1)}, bf16[64,2176]{1,0:T(8,128)(2,1)S(1)}, u32[]{:S(2)}, u32[]{:S(2)}) collective-permute-start(bf16[64,2176]{1,0:T(8,128)(2,1)S(1)} %gather.1.refs_0_.refs_4_), channel_id=1, source_target_pairs={{0,12},{1,13},{2,14},{3,15},{4,8},{5,9},{6,10},{7,11},{8,4},{9,5},... | collective-permute-start | bytes 835592 | tf_op jit(solution)/shard_map/ppermute | solution.py:15
  17.5 13.8 %collective-permute-start.9 = (bf16[64,2304]{1,0:T(8,128)(2,1)S(1)}, bf16[64,2304]{1,0:T(8,128)(2,1)S(1)}, u32[]{:S(2)}, u32[]{:S(2)}) collective-permute-start(bf16[64,2304]{1,0:T(8,128)(2,1)S(1)} %get-tuple-element.88.own_ref), channel_id=1, source_target_pairs={{0,16},{1,17},{2,18},{3,19},{4,20},{5,21},{6,22},{7,23},{8,24},{9,... | collective-permute-start | bytes 884744 | tf_op jit(solution)/shard_map/ppermute | solution.py:21
  22.1 10.5 %collective-permute-start.8 = (bf16[64,2304]{1,0:T(8,128)(2,1)S(1)}, bf16[64,2304]{1,0:T(8,128)(2,1)S(1)}, u32[]{:S(2)}, u32[]{:S(2)}) collective-permute-start(bf16[64,2304]{1,0:T(8,128)(2,1)S(1)} %get-tuple-element.87.own_ref), channel_id=1, source_target_pairs={{0,16},{1,17},{2,18},{3,19},{4,20},{5,21},{6,22},{7,23},{8,24},{9,... | collective-permute-start | bytes 884744 | tf_op jit(solution)/shard_map/ppermute | solution.py:21
  27.9 6.1 %collective-permute-start.7 = (bf16[64,2176]{1,0:T(8,128)(2,1)S(1)}, bf16[64,2176]{1,0:T(8,128)(2,1)S(1)}, u32[]{:S(2)}, u32[]{:S(2)}) collective-permute-start(bf16[64,2176]{1,0:T(8,128)(2,1)S(1)} %collective-permute-done.3.refs_0_), channel_id=1, source_target_pairs={{0,1},{1,0},{2,3},{3,2},{4,5},{5,4},{6,7},{7,6},{8,9},{9,8},{10,11... | collective-permute-start | bytes 835592 | tf_op jit(solution)/shard_map/ppermute | solution.py:15
  27.9 15.9 %collective-permute-start.6 = (bf16[64,2176]{1,0:T(8,128)(2,1)S(1)}, bf16[64,2176]{1,0:T(8,128)(2,1)S(1)}, u32[]{:S(2)}, u32[]{:S(2)}) collective-permute-start(bf16[64,2176]{1,0:T(8,128)(2,1)S(1)} %gather.1.refs_0_.refs_4_), channel_id=1, source_target_pairs={{0,8},{1,9},{2,10},{3,11},{4,12},{5,13},{6,14},{7,15},{8,0},{9,1},... | collective-permute-start | bytes 835592 | tf_op jit(solution)/shard_map/ppermute | solution.py:15
  30.8 15.2 %collective-permute-start.5 = (bf16[64,2304]{1,0:T(8,128)(2,1)S(1)}, bf16[64,2304]{1,0:T(8,128)(2,1)S(1)}, u32[]{:S(2)}, u32[]{:S(2)}) collective-permute-start(bf16[64,2304]{1,0:T(8,128)(2,1)S(1)} %get-tuple-element.85.own_ref), channel_id=1, source_target_pairs={{0,16},{1,17},{2,18},{3,19},{4,20},{5,21},{6,22},{7,23},{8,24},{9,... | collective-permute-start | bytes 884744 | tf_op jit(solution)/shard_map/ppermute | solution.py:21
  35.2 12.2 %collective-permute-start.10 = (bf16[64,2304]{1,0:T(8,128)(2,1)S(1)}, bf16[64,2304]{1,0:T(8,128)(2,1)S(1)}, u32[]{:S(2)}, u32[]{:S(2)}) collective-permute-start(bf16[64,2304]{1,0:T(8,128)(2,1)S(1)} %get-tuple-element.94.own_ref), channel_id=1, source_target_pairs={{0,16},{1,17},{2,18},{3,19},{4,20},{5,21},{6,22},{7,23},{8,24},{9,... | collective-permute-start | bytes 884744 | tf_op jit(solution)/shard_map/ppermute | solution.py:21
  43.9 4.9 %collective-permute-start.12 = (bf16[64,2176]{1,0:T(8,128)(2,1)S(1)}, bf16[64,2176]{1,0:T(8,128)(2,1)S(1)}, u32[]{:S(2)}, u32[]{:S(2)}) collective-permute-start(bf16[64,2176]{1,0:T(8,128)(2,1)S(1)} %collective-permute-done.6.refs_0_), channel_id=1, source_target_pairs={{0,1},{1,0},{2,3},{3,2},{4,5},{5,4},{6,7},{7,6},{8,9},{9,8},{10,11... | collective-permute-start | bytes 835592 | tf_op jit(solution)/shard_map/ppermute | solution.py:15
  43.9 8.0 %collective-permute-start.17 = (bf16[64,2176]{1,0:T(8,128)(2,1)S(1)}, bf16[64,2176]{1,0:T(8,128)(2,1)S(1)}, u32[]{:S(2)}, u32[]{:S(2)}) collective-permute-start(bf16[64,2176]{1,0:T(8,128)(2,1)S(1)} %collective-permute-done.4.refs_0_), channel_id=1, source_target_pairs={{0,1},{1,0},{2,3},{3,2},{4,5},{5,4},{6,7},{7,6},{8,9},{9,8},{10,11... | collective-permute-start | bytes 835592 | tf_op jit(solution)/shard_map/ppermute | solution.py:15
  45.5 10.7 %collective-permute-start.16 = (bf16[64,2304]{1,0:T(8,128)(2,1)S(1)}, bf16[64,2304]{1,0:T(8,128)(2,1)S(1)}, u32[]{:S(2)}, u32[]{:S(2)}) collective-permute-start(bf16[64,2304]{1,0:T(8,128)(2,1)S(1)} %get-tuple-element.98.own_ref), channel_id=1, source_target_pairs={{0,16},{1,17},{2,18},{3,19},{4,20},{5,21},{6,22},{7,23},{8,24},{9,... | collective-permute-start | bytes 884744 | tf_op jit(solution)/shard_map/ppermute | solution.py:21
  48.7 3.1 %collective-permute-start.11 = (bf16[64,2048]{1,0:T(8,128)(2,1)S(1)}, bf16[64,2048]{1,0:T(8,128)(2,1)S(1)}, u32[]{:S(2)}, u32[]{:S(2)}) collective-permute-start(bf16[64,2048]{1,0:T(8,128)(2,1)S(1)} %get-tuple-element.95.refs_4_), channel_id=1, source_target_pairs={{0,1},{1,0},{2,3},{3,2},{4,5},{5,4},{6,7},{7,6},{8,9},{9,8},{10,11... | collective-permute-start | bytes 786440 | tf_op jit(solution)/shard_map/ppermute | solution.py:15
  49.9 11.9 %collective-permute-start.15 = (bf16[64,2304]{1,0:T(8,128)(2,1)S(1)}, bf16[64,2304]{1,0:T(8,128)(2,1)S(1)}, u32[]{:S(2)}, u32[]{:S(2)}) collective-permute-start(bf16[64,2304]{1,0:T(8,128)(2,1)S(1)} %get-tuple-element.97.own_ref), channel_id=1, source_target_pairs={{0,16},{1,17},{2,18},{3,19},{4,20},{5,21},{6,22},{7,23},{8,24},{9,... | collective-permute-start | bytes 884744 | tf_op jit(solution)/shard_map/ppermute | solution.py:21
  51.6 11.6 %collective-permute-start.14 = (bf16[64,2176]{1,0:T(8,128)(2,1)S(1)}, bf16[64,2176]{1,0:T(8,128)(2,1)S(1)}, u32[]{:S(2)}, u32[]{:S(2)}) collective-permute-start(bf16[64,2176]{1,0:T(8,128)(2,1)S(1)} %gather.1.refs_0_.refs_4_), channel_id=1, source_target_pairs={{0,1},{1,0},{2,3},{3,2},{4,5},{5,4},{6,7},{7,6},{8,9},{9,8},{10,11... | collective-permute-start | bytes 835592 | tf_op jit(solution)/shard_map/ppermute | solution.py:15
  53.0 14.1 %collective-permute-start.19 = (bf16[64,2304]{1,0:T(8,128)(2,1)S(1)}, bf16[64,2304]{1,0:T(8,128)(2,1)S(1)}, u32[]{:S(2)}, u32[]{:S(2)}) collective-permute-start(bf16[64,2304]{1,0:T(8,128)(2,1)S(1)} %get-tuple-element.104.own_ref), channel_id=1, source_target_pairs={{0,16},{1,17},{2,18},{3,19},{4,20},{5,21},{6,22},{7,23},{8,24},{9,... | collective-permute-start | bytes 884744 | tf_op jit(solution)/shard_map/ppermute | solution.py:21
  53.5 10.9 %collective-permute-start.13 = (bf16[64,2048]{1,0:T(8,128)(2,1)S(1)}, bf16[64,2048]{1,0:T(8,128)(2,1)S(1)}, u32[]{:S(2)}, u32[]{:S(2)}) collective-permute-start(bf16[64,2048]{1,0:T(8,128)(2,1)S(1)} %merge.5.refs_4_), channel_id=1, source_target_pairs={{0,12},{1,13},{2,14},{3,15},{4,8},{5,9},{6,10},{7,11},{8,4},{9,5},... | collective-permute-start | bytes 786440 | tf_op jit(solution)/shard_map/ppermute | solution.py:15
  63.1 1.6 %collective-permute-start.20 = (bf16[64,2048]{1,0:T(8,128)(2,1)S(1)}, bf16[64,2048]{1,0:T(8,128)(2,1)S(1)}, u32[]{:S(2)}, u32[]{:S(2)}) collective-permute-start(bf16[64,2048]{1,0:T(8,128)(2,1)S(1)} %get-tuple-element.101.refs_4_), channel_id=1, source_target_pairs={{0,1},{1,0},{2,3},{3,2},{4,5},{5,4},{6,7},{7,6},{8,9},{9,8},{10,11... | collective-permute-start | bytes 786440 | tf_op jit(solution)/shard_map/ppermute | solution.py:15
  64.3 9.5 %collective-permute-start.18 = (bf16[64,2304]{1,0:T(8,128)(2,1)S(1)}, bf16[64,2304]{1,0:T(8,128)(2,1)S(1)}, u32[]{:S(2)}, u32[]{:S(2)}) collective-permute-start(bf16[64,2304]{1,0:T(8,128)(2,1)S(1)} %get-tuple-element.103.own_ref), channel_id=1, source_target_pairs={{0,16},{1,17},{2,18},{3,19},{4,20},{5,21},{6,22},{7,23},{8,24},{9,... | collective-permute-start | bytes 884744 | tf_op jit(solution)/shard_map/ppermute | solution.py:21
  68.7 1.8 %collective-permute-start.21 = (bf16[64,2048]{1,0:T(8,128)(2,1)S(1)}, bf16[64,2048]{1,0:T(8,128)(2,1)S(1)}, u32[]{:S(2)}, u32[]{:S(2)}) collective-permute-start(bf16[64,2048]{1,0:T(8,128)(2,1)S(1)} %get-tuple-element.105.refs_2_), channel_id=1, source_target_pairs={{0,1},{1,0},{2,3},{3,2},{4,5},{5,4},{6,7},{7,6},{8,9},{9,8},{10,11... | collective-permute-start | bytes 786440 | tf_op jit(solution)/shard_map/ppermute | solution.py:15
  68.7 15.2 %collective-permute-start.23 = (bf16[64,2048]{1,0:T(8,128)(2,1)S(1)}, bf16[64,2048]{1,0:T(8,128)(2,1)S(1)}, u32[]{:S(2)}, u32[]{:S(2)}) collective-permute-start(bf16[64,2048]{1,0:T(8,128)(2,1)S(1)} %merge.7.refs_3_), channel_id=1, source_target_pairs={{0,8},{1,9},{2,10},{3,11},{4,12},{5,13},{6,14},{7,15},{8,0},{9,1},... | collective-permute-start | bytes 786440 | tf_op jit(solution)/shard_map/ppermute | solution.py:15
  70.5 13.5 %collective-permute-start.24 = (bf16[64,2048]{1,0:T(8,128)(2,1)S(1)}, bf16[64,2048]{1,0:T(8,128)(2,1)S(1)}, u32[]{:S(2)}, u32[]{:S(2)}) collective-permute-start(bf16[64,2048]{1,0:T(8,128)(2,1)S(1)} %merge.8.refs_3_), channel_id=1, source_target_pairs={{0,4},{1,5},{2,6},{3,7},{4,0},{5,1},{6,2},{7,3},{8,12},{9,13},{10,... | collective-permute-start | bytes 786440 | tf_op jit(solution)/shard_map/ppermute | solution.py:15
  75.2 8.8 %collective-permute-start.22 = (bf16[64,2048]{1,0:T(8,128)(2,1)S(1)}, bf16[64,2048]{1,0:T(8,128)(2,1)S(1)}, u32[]{:S(2)}, u32[]{:S(2)}) collective-permute-start(bf16[64,2048]{1,0:T(8,128)(2,1)S(1)} %get-tuple-element.106.refs_40_), channel_id=1, source_target_pairs={{0,1},{1,0},{2,3},{3,2},{4,5},{5,4},{6,7},{7,6},{8,9},{9,8},{10,11... | collective-permute-start | bytes 786440 | tf_op jit(solution)/shard_map/ppermute | solution.py:15
  84.2 4.3 %collective-permute-start.25 = (bf16[16,2048]{1,0:T(8,128)(2,1)S(1)}, bf16[16,2048]{1,0:T(8,128)(2,1)S(1)}, u32[]{:S(2)}, u32[]{:S(2)}) collective-permute-start(bf16[16,2048]{1,0:T(8,128)(2,1)S(1)} %get-tuple-element.149), channel_id=1, source_target_pairs={{0,2},{1,3},{2,0},{3,1},{4,6},{5,7},{6,4},{7,5},{8,10},{9,11},{10,... | collective-permute-start | bytes 196616 | tf_op jit(solution)/shard_map/ppermute | solution.py:15
  85.7 4.3 %collective-permute-start.26 = (bf16[16,2048]{1,0:T(8,128)(2,1)S(1)}, bf16[16,2048]{1,0:T(8,128)(2,1)S(1)}, u32[]{:S(2)}, u32[]{:S(2)}) collective-permute-start(bf16[16,2048]{1,0:T(8,128)(2,1)S(1)} %get-tuple-element.150), channel_id=1, source_target_pairs={{0,16},{1,17},{2,18},{3,19},{4,20},{5,21},{6,22},{7,23},{8,24},{9,... | collective-permute-start | bytes 196616 | tf_op jit(solution)/shard_map/ppermute | solution.py:21
  86.4 5.2 %collective-permute-start.27 = (bf16[16,2048]{1,0:T(8,128)(2,1)S(1)}, bf16[16,2048]{1,0:T(8,128)(2,1)S(1)}, u32[]{:S(2)}, u32[]{:S(2)}) collective-permute-start(bf16[16,2048]{1,0:T(8,128)(2,1)S(1)} %get-tuple-element.151), channel_id=1, source_target_pairs={{0,18},{1,19},{2,16},{3,17},{4,22},{5,23},{6,20},{7,21},{8,26},{9,... | collective-permute-start | bytes 196616 | tf_op jit(solution)/shard_map/ppermute | solution.py:21
